TPU v7x, 256 devices: a whole 4x4x8 slice. The times are simulated.
256 devices in a mesh: node: 4 (over y), wide: 64 (over x, z, core).
Axes of the slice: x: 4, y: 4, z: 8, core: 2. Of those that a mesh axis runs over, the one named last changes fastest.
Arguments:
- queries: bfloat16 [65536, 1024], P(('node', 'wide')), may hold values from -300 to 300
- keys: bfloat16 [65536, 128], P(('node', 'wide')), may hold values from -7 to 7
- values: bfloat16 [65536, 128], P(('node', 'wide')), may hold values from -6 to 6
- out_grad: bfloat16 [65536, 1024], P(('node', 'wide')), may hold values from -6 to 6
- doc_lengths: int32 [128], replicated, may hold values from 1 to 2048, 65536 in all
Outputs:
- attn_out: bfloat16 [65536, 1024], P(('node', 'wide'))
- grad_queries: bfloat16 [65536, 1024], P(('node', 'wide'))
- grad_keys: bfloat16 [65536, 128], P(('node', 'wide'))
- grad_values: bfloat16 [65536, 128], P(('node', 'wide'))
All inputs are finite; a program needn't handle non-finite values.
Results may differ from a plain program's by a relative error of at most 0.04.
Values may be sent and summed in bfloat16 or wider, within the bound.
No kernel may reach another device: no remote copies, remote signals or barrier semaphores. Data moves between devices by JAX's collectives and lax.ppermute only.
A program may use at most 128 MiB of HBM per device.

v0:
```python
import math

import jax
import jax.numpy as jnp
from jax import lax
from jax.sharding import PartitionSpec as P

WINDOW = 8


def shifted(shard, axis, by):
    peers = lax.axis_size(axis)
    pairs = [(i, i + by) for i in range(peers) if 0 <= i + by < peers]
    return lax.ppermute(shard, axis, pairs)


def doc_index(positions, doc_ends):
    return jnp.sum((positions[:, None] >= doc_ends[None, :]).astype(jnp.int32), axis=1)


def block_masks(device, tok_rows, blocks_count, doc_ends):
    local = jnp.arange(tok_rows, dtype=jnp.int32)
    query_pos = device * tok_rows + local
    query_doc = doc_index(query_pos, doc_ends)
    offsets = jnp.arange(blocks_count, dtype=jnp.int32)
    key_pos = (device - offsets)[:, None] * tok_rows + local[None, :]
    key_doc = doc_index(key_pos.reshape(-1), doc_ends).reshape(blocks_count, tok_rows)
    same_doc = key_doc[:, None, :] == query_doc[None, :, None]
    causal = key_pos[:, None, :] <= query_pos[None, :, None]
    return same_doc & causal & (key_pos[:, None, :] >= 0)


def attention_core(queries3, grads3, blocks, masks):
    heads = queries3.shape[1]
    head_dim = queries3.shape[2]
    tok_rows = queries3.shape[0]
    score_scale = 1.0 / math.sqrt(head_dim)

    def scores_of(block):
        return (
            jnp.einsum(
                "thd,ud->htu", queries3, block[:, :head_dim], preferred_element_type=jnp.float32
            )
            * score_scale
        )

    def stat_step(carry, pair):
        block, allowed = pair
        running_max, running_sum = carry
        scores = jnp.where(allowed[None], scores_of(block), -1e30)
        new_max = jnp.maximum(running_max, jnp.max(scores, axis=-1))
        terms = jnp.where(allowed[None], jnp.exp(scores - new_max[..., None]), 0.0)
        return (
            (new_max, running_sum * jnp.exp(running_max - new_max) + jnp.sum(terms, axis=-1)),
            None,
        )

    start = (
        jnp.full((heads, tok_rows), -1e30, jnp.float32),
        jnp.zeros((heads, tok_rows), jnp.float32),
    )
    (row_max, row_sum), _ = lax.scan(stat_step, start, (blocks, masks))
    log_total = row_max + jnp.log(row_sum)

    def out_step(total, pair):
        block, allowed = pair
        weights = jnp.where(
            allowed[None], jnp.exp(scores_of(block) - log_total[..., None]), 0.0
        ).astype(jnp.bfloat16)
        new_total = total + jnp.einsum(
            "htu,ud->thd", weights, block[:, head_dim:], preferred_element_type=jnp.float32
        )
        return (new_total, weights)

    out_sum, kept_probs = lax.scan(
        out_step, jnp.zeros((tok_rows, heads, head_dim), jnp.float32), (blocks, masks)
    )
    output = out_sum.astype(jnp.bfloat16)
    delta = jnp.sum(grads3.astype(jnp.float32) * output.astype(jnp.float32), axis=2).T

    def grad_step(dq_sum, triple):
        block, allowed, weights = triple
        dprob = jnp.einsum(
            "thd,ud->htu", grads3, block[:, head_dim:], preferred_element_type=jnp.float32
        )
        dscore = (weights.astype(jnp.float32) * (dprob - delta[..., None])).astype(jnp.bfloat16)
        new_dq = dq_sum + jnp.einsum(
            "htu,ud->thd", dscore, block[:, :head_dim], preferred_element_type=jnp.float32
        )
        key_grad = (
            jnp.einsum("htu,thd->ud", dscore, queries3, preferred_element_type=jnp.float32)
            * score_scale
        )
        value_grad = jnp.einsum("htu,thd->ud", weights, grads3, preferred_element_type=jnp.float32)
        return (new_dq, jnp.concatenate([key_grad, value_grad], axis=1))

    dq_sum, partials = lax.scan(
        grad_step, jnp.zeros((tok_rows, heads, head_dim), jnp.float32), (blocks, masks, kept_probs)
    )
    return (output, (dq_sum * score_scale).astype(jnp.bfloat16), partials)


def on_device(queries, keys, values, out_grad, doc_lengths):
    tok_rows = queries.shape[0]
    head_dim = keys.shape[1]
    heads = queries.shape[1] // head_dim
    device = lax.axis_index(("node", "wide"))
    doc_ends = jnp.cumsum(doc_lengths)
    own_block = jnp.concatenate([keys, values], axis=1)
    pieces = [own_block]
    for offset in range(1, WINDOW + 1):
        pieces.append(shifted(own_block, ("node", "wide"), offset))
    blocks = jnp.stack(pieces)
    masks = block_masks(device, tok_rows, WINDOW + 1, doc_ends)
    queries3 = queries.reshape(tok_rows, heads, head_dim)
    grads3 = out_grad.reshape(tok_rows, heads, head_dim)
    output, grad_q, partials = attention_core(queries3, grads3, blocks, masks)
    totals = partials[0]
    for offset in range(1, WINDOW + 1):
        totals = totals + shifted(partials[offset], ("node", "wide"), -offset)
    grad_keys = totals[:, :head_dim].astype(jnp.bfloat16)
    grad_values = totals[:, head_dim:].astype(jnp.bfloat16)
    return (
        output.reshape(tok_rows, heads * head_dim),
        grad_q.reshape(tok_rows, heads * head_dim),
        grad_keys,
        grad_values,
    )


def solution(mesh):
    in_specs = (
        P(("node", "wide"), None),
        P(("node", "wide"), None),
        P(("node", "wide"), None),
        P(("node", "wide"), None),
        P(),
    )
    out_specs = (
        P(("node", "wide"), None),
        P(("node", "wide"), None),
        P(("node", "wide"), None),
        P(("node", "wide"), None),
    )
    return jax.shard_map(
        on_device, mesh=mesh, in_specs=in_specs, out_specs=out_specs, check_vma=False
    )
```

profile of v0, /device:TPU:24, one launch (start us, length us, event | category | flops | bytes accessed | tf_op | source)
XLA Modules:
  0.0 305.6 jit_solution(15527255942939615807)
XLA Ops:
  2.4 1.9 collective-permute-start
  4.3 3.8 %collective-permute-start.1 = (bf16[256,256]{1,0:T(8,128)(2,1)S(1)}, bf16[256,256]{1,0:T(8,128)(2,1)S(1)}, u32[]{:S(2)}, u32[]{:S(2)}) collective-permute-start(bf16[256,256]{1,0:T(8,128)(2,1)S(1)} %constant_dynamic-update-slice_fusion.1), channel_id=1, source_target_pairs={{0,2},{1,3},{2,4},{3,5},{4,6},{5,7},{6,8},{7,9},{8,10},{9,11},{10,... | collective-permute-start | bytes 393224 | tf_op jit(solution)/shard_map/ppermute | solution.py:14
  8.2 5.2 %collective-permute-start.2 = (bf16[256,256]{1,0:T(8,128)(2,1)S(1)}, bf16[256,256]{1,0:T(8,128)(2,1)S(1)}, u32[]{:S(2)}, u32[]{:S(2)}) collective-permute-start(bf16[256,256]{1,0:T(8,128)(2,1)S(1)} %constant_dynamic-update-slice_fusion.1), channel_id=1, source_target_pairs={{0,3},{1,4},{2,5},{3,6},{4,7},{5,8},{6,9},{7,10},{8,11},{9,12},{10... | collective-permute-start | bytes 393224 | tf_op jit(solution)/shard_map/ppermute | solution.py:14
  13.4 5.5 %collective-permute-start.3 = (bf16[256,256]{1,0:T(8,128)(2,1)S(1)}, bf16[256,256]{1,0:T(8,128)(2,1)S(1)}, u32[]{:S(2)}, u32[]{:S(2)}) collective-permute-start(bf16[256,256]{1,0:T(8,128)(2,1)S(1)} %constant_dynamic-update-slice_fusion.1), channel_id=1, source_target_pairs={{0,4},{1,5},{2,6},{3,7},{4,8},{5,9},{6,10},{7,11},{8,12},{9,13},{1... | collective-permute-start | bytes 393224 | tf_op jit(solution)/shard_map/ppermute | solution.py:14
  18.9 2.8 collective-permute-start.4
  27.1 2.3 and_and_fusion
  30.0 2.9 collective-permute-start.5
  33.6 7.3 %collective-permute-start.6 = (bf16[256,256]{1,0:T(8,128)(2,1)S(1)}, bf16[256,256]{1,0:T(8,128)(2,1)S(1)}, u32[]{:S(2)}, u32[]{:S(2)}) collective-permute-start(bf16[256,256]{1,0:T(8,128)(2,1)S(1)} %constant_dynamic-update-slice_fusion.1), channel_id=1, source_target_pairs={{0,7},{1,8},{2,9},{3,10},{4,11},{5,12},{6,13},{7,14},{8,15},{9,16}... | collective-permute-start | bytes 393224 | tf_op jit(solution)/shard_map/ppermute | solution.py:14
  41.5 3.4 %collective-permute-start.7 = (bf16[256,256]{1,0:T(8,128)(2,1)S(1)}, bf16[256,256]{1,0:T(8,128)(2,1)S(1)}, u32[]{:S(2)}, u32[]{:S(2)}) collective-permute-start(bf16[256,256]{1,0:T(8,128)(2,1)S(1)} %constant_dynamic-update-slice_fusion.1), channel_id=1, source_target_pairs={{0,8},{1,9},{2,10},{3,11},{4,12},{5,13},{6,14},{7,15},{8,16},{9,17... | collective-permute-start | bytes 393224 | tf_op jit(solution)/shard_map/ppermute | solution.py:14
  46.9 2.0 collective-permute-done.5
  49.6 3.2 %collective-permute-done.6 = bf16[256,256]{1,0:T(8,128)(2,1)S(1)} collective-permute-done((bf16[256,256]{1,0:T(8,128)(2,1)S(1)}, bf16[256,256]{1,0:T(8,128)(2,1)S(1)}, u32[]{:S(2)}, u32[]{:S(2)}) %collective-permute-start.6) | collective-permute-done | bytes 131104 | tf_op jit(solution)/shard_map/ppermute | solution.py:14
  53.4 4.0 %collective-permute-done.7 = bf16[256,256]{1,0:T(8,128)(2,1)S(1)} collective-permute-done((bf16[256,256]{1,0:T(8,128)(2,1)S(1)}, bf16[256,256]{1,0:T(8,128)(2,1)S(1)}, u32[]{:S(2)}, u32[]{:S(2)}) %collective-permute-start.7) | collective-permute-done | bytes 131104 | tf_op jit(solution)/shard_map/ppermute | solution.py:14
  58.1 34.8 %while.39 = (s32[]{:T(128)}, f32[8,256]{1,0:T(8,128)S(1)}, f32[8,256]{1,0:T(8,128)S(1)}, pred[9,256,256]{1,2,0:T(8,128)(4,1)}, bf16[9,256,256]{2,1,0:T(8,128)(2,...) while((s32[]{:T(128)}, f32[8,256]{1,0:T(8,128)S(1)}, f32[8,256]{1,0:T(8,128)S(1)}, ...), condition=%wide.region_6.7_spmd.clone, body=%wide.region_3.6_spmd.clone.sunk | while | flops 138422272 | bytes 5415016 | solution.py:62
  92.9 53.8 %while.40 = (s32[]{:T(128)}, f32[256,8,128]{0,2,1:T(8,128)}, bf16[9,8,256,256]{2,3,1,0:T(8,128)(2,1)}, bf16[9,256,256]{2,1,0:T(8,128)(2,1)}, pred[9,256,256]{1,2...) while((s32[]{:T(128)}, f32[256,8,128]{0,2,1:T(8,128)}, ...), condition=%wide.region_8.9_spmd.clone, body=%wide.region_7.8_spmd.clone.sunk | while | flops 271056896 | bytes 14754471 | solution.py:75
  94.8 2.6 bitcast_dynamic-update-slice_fusion.11
  100.7 2.7 bitcast_dynamic-update-slice_fusion.11
  106.7 2.6 bitcast_dynamic-update-slice_fusion.11
  112.7 2.6 bitcast_dynamic-update-slice_fusion.11
  118.6 2.6 bitcast_dynamic-update-slice_fusion.11
  124.6 2.7 bitcast_dynamic-update-slice_fusion.11
  130.6 2.7 bitcast_dynamic-update-slice_fusion.11
  136.5 2.7 bitcast_dynamic-update-slice_fusion.11
  142.5 2.7 bitcast_dynamic-update-slice_fusion.11
  146.7 2.2 multiply_reduce_fusion
  148.9 61.5 %while.41 = (s32[]{:T(128)}, f32[256,8,128]{0,2,1:T(8,128)S(1)}, f32[9,256,256]{2,1,0:T(8,128)}, bf16[9,256,256]{2,1,0:T(8,128)(2,1)}, bf16[9,8,256,256]{2,3,1,0...) while((s32[]{:T(128)}, f32[256,8,128]{0,2,1:T(8,128)S(1)}, ...), condition=%wide.region_11.12_spmd.clone, body=%wide.region_10.11_spmd.clone.sunk | while | flops 539590656 | bytes 15344815 | solution.py:97
  152.1 1.7 convolution_bitcast_fusion.5
  159.0 1.7 convolution_bitcast_fusion.5
  165.8 1.7 convolution_bitcast_fusion.5
  172.6 1.7 convolution_bitcast_fusion.5
  179.5 1.7 convolution_bitcast_fusion.5
  186.3 1.7 convolution_bitcast_fusion.5
  193.1 1.7 convolution_bitcast_fusion.5
  200.0 1.7 convolution_bitcast_fusion.5
  206.8 1.7 convolution_bitcast_fusion.5
  210.4 2.5 slice_bitcast_fusion.17
  212.9 9.8 %collective-permute-start.10 = (f32[256,256]{1,0:T(8,128)S(1)}, f32[256,256]{1,0:T(8,128)S(1)}, u32[]{:S(2)}, u32[]{:S(2)}) collective-permute-start(f32[256,256]{1,0:T(8,128)S(1)} %get-tuple-element.288), channel_id=1, source_target_pairs={{3,0},{4,1},{5,2},{6,3},{7,4},{8,5},{9,6},{10,7},{11,8},{12,9},{13... | collective-permute-start | bytes 786440 | tf_op jit(solution)/shard_map/ppermute | solution.py:14
  222.7 1.9 collective-permute-start.11
  224.7 3.8 %collective-permute-start.12 = (f32[256,256]{1,0:T(8,128)S(1)}, f32[256,256]{1,0:T(8,128)S(1)}, u32[]{:S(2)}, u32[]{:S(2)}) collective-permute-start(f32[256,256]{1,0:T(8,128)S(1)} %get-tuple-element.286), channel_id=1, source_target_pairs={{5,0},{6,1},{7,2},{8,3},{9,4},{10,5},{11,6},{12,7},{13,8},{14,9},{... | collective-permute-start | bytes 786440 | tf_op jit(solution)/shard_map/ppermute | solution.py:14
  228.5 2.6 collective-permute-start.13
  231.1 5.8 %collective-permute-start.14 = (f32[256,256]{1,0:T(8,128)}, f32[256,256]{1,0:T(8,128)}, u32[]{:S(2)}, u32[]{:S(2)}) collective-permute-start(f32[256,256]{1,0:T(8,128)} %get-tuple-element.284), channel_id=1, source_target_pairs={{7,0},{8,1},{9,2},{10,3},{11,4},{12,5},{13,6},{14,7},{15,8},{16,9}... | collective-permute-start | bytes 786440 | tf_op jit(solution)/shard_map/ppermute | solution.py:14
  236.9 4.4 %collective-permute-start.15 = (f32[256,256]{1,0:T(8,128)}, f32[256,256]{1,0:T(8,128)}, u32[]{:S(2)}, u32[]{:S(2)}) collective-permute-start(f32[256,256]{1,0:T(8,128)} %get-tuple-element.290), channel_id=1, source_target_pairs={{8,0},{9,1},{10,2},{11,3},{12,4},{13,5},{14,6},{15,7},{16,8},{17,9... | collective-permute-start | bytes 786440 | tf_op jit(solution)/shard_map/ppermute | solution.py:14
  241.3 4.4 %collective-permute-done.11 = f32[256,256]{1,0:T(8,128)S(1)} collective-permute-done((f32[256,256]{1,0:T(8,128)S(1)}, f32[256,256]{1,0:T(8,128)S(1)}, u32[]{:S(2)}, u32[]{:S(2)}) %collective-permute-start.11) | collective-permute-done | bytes 262176 | tf_op jit(solution)/shard_map/ppermute | solution.py:14
  245.7 1.9 collective-permute-start.8
  247.6 14.5 %collective-permute-done.12 = f32[256,256]{1,0:T(8,128)S(1)} collective-permute-done((f32[256,256]{1,0:T(8,128)S(1)}, f32[256,256]{1,0:T(8,128)S(1)}, u32[]{:S(2)}, u32[]{:S(2)}) %collective-permute-start.12) | collective-permute-done | bytes 262176 | tf_op jit(solution)/shard_map/ppermute | solution.py:14
  262.1 1.9 collective-permute-start.9
  266.1 23.1 %collective-permute-done.13 = f32[256,256]{1,0:T(8,128)} collective-permute-done((f32[256,256]{1,0:T(8,128)}, f32[256,256]{1,0:T(8,128)}, u32[]{:S(2)}, u32[]{:S(2)}) %collective-permute-start.13) | collective-permute-done | bytes 262176 | tf_op jit(solution)/shard_map/ppermute | solution.py:14
  289.3 10.9 %collective-permute-done.8 = f32[256,256]{1,0:T(8,128)} collective-permute-done((f32[256,256]{1,0:T(8,128)S(1)}, f32[256,256]{1,0:T(8,128)}, u32[]{:S(2)}, u32[]{:S(2)}) %collective-permute-start.8) | collective-permute-done | bytes 262176 | tf_op jit(solution)/shard_map/ppermute | solution.py:14
  300.2 3.3 %collective-permute-done.9 = f32[256,256]{1,0:T(8,128)} collective-permute-done((f32[256,256]{1,0:T(8,128)S(1)}, f32[256,256]{1,0:T(8,128)}, u32[]{:S(2)}, u32[]{:S(2)}) %collective-permute-start.9) | collective-permute-done | bytes 262176 | tf_op jit(solution)/shard_map/ppermute | solution.py:14
  (276 shorter events, 126.9 us)
Async XLA Ops:
  0.6 26.2 %copy-start.6 = (bf16[256,1024]{1,0:T(8,128)(2,1)S(1)}, bf16[256,1024]{1,0:T(8,128)(2,1)}, u32[]{:S(2)}) copy-start(bf16[256,1024]{1,0:T(8,128)(2,1)} %param.14) | copy-start | bytes 1572868
  2.4 27.6 %collective-permute-start = (bf16[256,256]{1,0:T(8,128)(2,1)S(1)}, bf16[256,256]{1,0:T(8,128)(2,1)S(1)}, u32[]{:S(2)}, u32[]{:S(2)}) collective-permute-start(bf16[256,256]{1,0:T(8,128)(2,1)S(1)} %constant_dynamic-update-slice_fusion.1), channel_id=1, source_target_pairs={{0,1},{1,2},{2,3},{3,4},{4,5},{5,6},{6,7},{7,8},{8,9},{9,10},{10,1... | collective-permute-start | bytes 393224 | tf_op jit(solution)/shard_map/ppermute | solution.py:14
  4.3 29.2 %collective-permute-start.1 = (bf16[256,256]{1,0:T(8,128)(2,1)S(1)}, bf16[256,256]{1,0:T(8,128)(2,1)S(1)}, u32[]{:S(2)}, u32[]{:S(2)}) collective-permute-start(bf16[256,256]{1,0:T(8,128)(2,1)S(1)} %constant_dynamic-update-slice_fusion.1), channel_id=1, source_target_pairs={{0,2},{1,3},{2,4},{3,5},{4,6},{5,7},{6,8},{7,9},{8,10},{9,11},{10,... | collective-permute-start | bytes 393224 | tf_op jit(solution)/shard_map/ppermute | solution.py:14
  8.2 33.4 %collective-permute-start.2 = (bf16[256,256]{1,0:T(8,128)(2,1)S(1)}, bf16[256,256]{1,0:T(8,128)(2,1)S(1)}, u32[]{:S(2)}, u32[]{:S(2)}) collective-permute-start(bf16[256,256]{1,0:T(8,128)(2,1)S(1)} %constant_dynamic-update-slice_fusion.1), channel_id=1, source_target_pairs={{0,3},{1,4},{2,5},{3,6},{4,7},{5,8},{6,9},{7,10},{8,11},{9,12},{10... | collective-permute-start | bytes 393224 | tf_op jit(solution)/shard_map/ppermute | solution.py:14
  13.4 32.2 %collective-permute-start.3 = (bf16[256,256]{1,0:T(8,128)(2,1)S(1)}, bf16[256,256]{1,0:T(8,128)(2,1)S(1)}, u32[]{:S(2)}, u32[]{:S(2)}) collective-permute-start(bf16[256,256]{1,0:T(8,128)(2,1)S(1)} %constant_dynamic-update-slice_fusion.1), channel_id=1, source_target_pairs={{0,4},{1,5},{2,6},{3,7},{4,8},{5,9},{6,10},{7,11},{8,12},{9,13},{1... | collective-permute-start | bytes 393224 | tf_op jit(solution)/shard_map/ppermute | solution.py:14
  18.9 27.4 %collective-permute-start.4 = (bf16[256,256]{1,0:T(8,128)(2,1)S(1)}, bf16[256,256]{1,0:T(8,128)(2,1)S(1)}, u32[]{:S(2)}, u32[]{:S(2)}) collective-permute-start(bf16[256,256]{1,0:T(8,128)(2,1)S(1)} %constant_dynamic-update-slice_fusion.1), channel_id=1, source_target_pairs={{0,5},{1,6},{2,7},{3,8},{4,9},{5,10},{6,11},{7,12},{8,13},{9,14},{... | collective-permute-start | bytes 393224 | tf_op jit(solution)/shard_map/ppermute | solution.py:14
  30.0 18.9 %collective-permute-start.5 = (bf16[256,256]{1,0:T(8,128)(2,1)S(1)}, bf16[256,256]{1,0:T(8,128)(2,1)S(1)}, u32[]{:S(2)}, u32[]{:S(2)}) collective-permute-start(bf16[256,256]{1,0:T(8,128)(2,1)S(1)} %constant_dynamic-update-slice_fusion.1), channel_id=1, source_target_pairs={{0,6},{1,7},{2,8},{3,9},{4,10},{5,11},{6,12},{7,13},{8,14},{9,15},... | collective-permute-start | bytes 393224 | tf_op jit(solution)/shard_map/ppermute | solution.py:14
  33.6 19.2 %collective-permute-start.6 = (bf16[256,256]{1,0:T(8,128)(2,1)S(1)}, bf16[256,256]{1,0:T(8,128)(2,1)S(1)}, u32[]{:S(2)}, u32[]{:S(2)}) collective-permute-start(bf16[256,256]{1,0:T(8,128)(2,1)S(1)} %constant_dynamic-update-slice_fusion.1), channel_id=1, source_target_pairs={{0,7},{1,8},{2,9},{3,10},{4,11},{5,12},{6,13},{7,14},{8,15},{9,16}... | collective-permute-start | bytes 393224 | tf_op jit(solution)/shard_map/ppermute | solution.py:14
  41.5 15.8 %collective-permute-start.7 = (bf16[256,256]{1,0:T(8,128)(2,1)S(1)}, bf16[256,256]{1,0:T(8,128)(2,1)S(1)}, u32[]{:S(2)}, u32[]{:S(2)}) collective-permute-start(bf16[256,256]{1,0:T(8,128)(2,1)S(1)} %constant_dynamic-update-slice_fusion.1), channel_id=1, source_target_pairs={{0,8},{1,9},{2,10},{3,11},{4,12},{5,13},{6,14},{7,15},{8,16},{9,17... | collective-permute-start | bytes 393224 | tf_op jit(solution)/shard_map/ppermute | solution.py:14
  93.8 3.6 %copy-start.1 = (f32[256,8,128]{0,2,1:T(8,128)S(1)}, f32[256,8,128]{0,2,1:T(8,128)}, u32[]{:S(2)}) copy-start(f32[256,8,128]{0,2,1:T(8,128)} %get-tuple-element.464) | copy-start | bytes 3145732 | tf_op jit(solution)/shard_map/while
  97.9 1.0 copy-start.2
  99.8 3.6 %copy-start.1 = (f32[256,8,128]{0,2,1:T(8,128)S(1)}, f32[256,8,128]{0,2,1:T(8,128)}, u32[]{:S(2)}) copy-start(f32[256,8,128]{0,2,1:T(8,128)} %get-tuple-element.464) | copy-start | bytes 3145732 | tf_op jit(solution)/shard_map/while
  103.9 1.0 copy-start.2
  105.8 3.6 %copy-start.1 = (f32[256,8,128]{0,2,1:T(8,128)S(1)}, f32[256,8,128]{0,2,1:T(8,128)}, u32[]{:S(2)}) copy-start(f32[256,8,128]{0,2,1:T(8,128)} %get-tuple-element.464) | copy-start | bytes 3145732 | tf_op jit(solution)/shard_map/while
  111.7 3.6 %copy-start.1 = (f32[256,8,128]{0,2,1:T(8,128)S(1)}, f32[256,8,128]{0,2,1:T(8,128)}, u32[]{:S(2)}) copy-start(f32[256,8,128]{0,2,1:T(8,128)} %get-tuple-element.464) | copy-start | bytes 3145732 | tf_op jit(solution)/shard_map/while
  117.7 3.6 %copy-start.1 = (f32[256,8,128]{0,2,1:T(8,128)S(1)}, f32[256,8,128]{0,2,1:T(8,128)}, u32[]{:S(2)}) copy-start(f32[256,8,128]{0,2,1:T(8,128)} %get-tuple-element.464) | copy-start | bytes 3145732 | tf_op jit(solution)/shard_map/while
  123.6 3.6 %copy-start.1 = (f32[256,8,128]{0,2,1:T(8,128)S(1)}, f32[256,8,128]{0,2,1:T(8,128)}, u32[]{:S(2)}) copy-start(f32[256,8,128]{0,2,1:T(8,128)} %get-tuple-element.464) | copy-start | bytes 3145732 | tf_op jit(solution)/shard_map/while
  129.6 3.6 %copy-start.1 = (f32[256,8,128]{0,2,1:T(8,128)S(1)}, f32[256,8,128]{0,2,1:T(8,128)}, u32[]{:S(2)}) copy-start(f32[256,8,128]{0,2,1:T(8,128)} %get-tuple-element.464) | copy-start | bytes 3145732 | tf_op jit(solution)/shard_map/while
  135.6 3.6 %copy-start.1 = (f32[256,8,128]{0,2,1:T(8,128)S(1)}, f32[256,8,128]{0,2,1:T(8,128)}, u32[]{:S(2)}) copy-start(f32[256,8,128]{0,2,1:T(8,128)} %get-tuple-element.464) | copy-start | bytes 3145732 | tf_op jit(solution)/shard_map/while
  141.6 3.7 %copy-start.1 = (f32[256,8,128]{0,2,1:T(8,128)S(1)}, f32[256,8,128]{0,2,1:T(8,128)}, u32[]{:S(2)}) copy-start(f32[256,8,128]{0,2,1:T(8,128)} %get-tuple-element.464) | copy-start | bytes 3145732 | tf_op jit(solution)/shard_map/while
  146.7 2.2 copy-start
  148.9 3.2 %copy-start.3 = (bf16[256,8,128]{0,2,1:T(8,128)(2,1)}, bf16[256,8,128]{0,2,1:T(8,128)(2,1)S(1)}, u32[]{:S(2)}) copy-start(bf16[256,8,128]{0,2,1:T(8,128)(2,1)S(1)} %get-tuple-element.508) | copy-start | bytes 1572868 | tf_op jit(solution)/shard_map/while
  154.7 1.0 copy-start.4
  155.8 3.2 %copy-start.3 = (bf16[256,8,128]{0,2,1:T(8,128)(2,1)}, bf16[256,8,128]{0,2,1:T(8,128)(2,1)S(1)}, u32[]{:S(2)}) copy-start(bf16[256,8,128]{0,2,1:T(8,128)(2,1)S(1)} %get-tuple-element.508) | copy-start | bytes 1572868 | tf_op jit(solution)/shard_map/while
  161.6 1.0 copy-start.4
  162.6 3.2 %copy-start.3 = (bf16[256,8,128]{0,2,1:T(8,128)(2,1)}, bf16[256,8,128]{0,2,1:T(8,128)(2,1)S(1)}, u32[]{:S(2)}) copy-start(bf16[256,8,128]{0,2,1:T(8,128)(2,1)S(1)} %get-tuple-element.508) | copy-start | bytes 1572868 | tf_op jit(solution)/shard_map/while
  168.4 1.0 copy-start.4
  169.4 3.2 %copy-start.3 = (bf16[256,8,128]{0,2,1:T(8,128)(2,1)}, bf16[256,8,128]{0,2,1:T(8,128)(2,1)S(1)}, u32[]{:S(2)}) copy-start(bf16[256,8,128]{0,2,1:T(8,128)(2,1)S(1)} %get-tuple-element.508) | copy-start | bytes 1572868 | tf_op jit(solution)/shard_map/while
  175.2 1.0 copy-start.4
  176.3 3.2 %copy-start.3 = (bf16[256,8,128]{0,2,1:T(8,128)(2,1)}, bf16[256,8,128]{0,2,1:T(8,128)(2,1)S(1)}, u32[]{:S(2)}) copy-start(bf16[256,8,128]{0,2,1:T(8,128)(2,1)S(1)} %get-tuple-element.508) | copy-start | bytes 1572868 | tf_op jit(solution)/shard_map/while
  182.1 1.0 copy-start.4
  183.1 3.2 %copy-start.3 = (bf16[256,8,128]{0,2,1:T(8,128)(2,1)}, bf16[256,8,128]{0,2,1:T(8,128)(2,1)S(1)}, u32[]{:S(2)}) copy-start(bf16[256,8,128]{0,2,1:T(8,128)(2,1)S(1)} %get-tuple-element.508) | copy-start | bytes 1572868 | tf_op jit(solution)/shard_map/while
  188.9 1.0 copy-start.4
  189.9 3.2 %copy-start.3 = (bf16[256,8,128]{0,2,1:T(8,128)(2,1)}, bf16[256,8,128]{0,2,1:T(8,128)(2,1)S(1)}, u32[]{:S(2)}) copy-start(bf16[256,8,128]{0,2,1:T(8,128)(2,1)S(1)} %get-tuple-element.508) | copy-start | bytes 1572868 | tf_op jit(solution)/shard_map/while
  195.8 1.0 copy-start.4
  196.8 3.2 %copy-start.3 = (bf16[256,8,128]{0,2,1:T(8,128)(2,1)}, bf16[256,8,128]{0,2,1:T(8,128)(2,1)S(1)}, u32[]{:S(2)}) copy-start(bf16[256,8,128]{0,2,1:T(8,128)(2,1)S(1)} %get-tuple-element.508) | copy-start | bytes 1572868 | tf_op jit(solution)/shard_map/while
  202.6 1.0 copy-start.4
  203.6 3.2 %copy-start.3 = (bf16[256,8,128]{0,2,1:T(8,128)(2,1)}, bf16[256,8,128]{0,2,1:T(8,128)(2,1)S(1)}, u32[]{:S(2)}) copy-start(bf16[256,8,128]{0,2,1:T(8,128)(2,1)S(1)} %get-tuple-element.508) | copy-start | bytes 1572868 | tf_op jit(solution)/shard_map/while
  209.4 1.0 copy-start.4
  212.9 52.2 %copy-start.5 = (bf16[256,8,128]{0,2,1:T(8,128)(2,1)S(1)}, bf16[256,8,128]{0,2,1:T(8,128)(2,1)}, u32[]{:S(2)}) copy-start(bf16[256,8,128]{0,2,1:T(8,128)(2,1)} %get-tuple-element.278) | copy-start | bytes 1572868
  212.9 24.0 %collective-permute-start.10 = (f32[256,256]{1,0:T(8,128)S(1)}, f32[256,256]{1,0:T(8,128)S(1)}, u32[]{:S(2)}, u32[]{:S(2)}) collective-permute-start(f32[256,256]{1,0:T(8,128)S(1)} %get-tuple-element.288), channel_id=1, source_target_pairs={{3,0},{4,1},{5,2},{6,3},{7,4},{8,5},{9,6},{10,7},{11,8},{12,9},{13... | collective-permute-start | bytes 786440 | tf_op jit(solution)/shard_map/ppermute | solution.py:14
  222.7 23.0 %collective-permute-start.11 = (f32[256,256]{1,0:T(8,128)S(1)}, f32[256,256]{1,0:T(8,128)S(1)}, u32[]{:S(2)}, u32[]{:S(2)}) collective-permute-start(f32[256,256]{1,0:T(8,128)S(1)} %get-tuple-element.287), channel_id=1, source_target_pairs={{4,0},{5,1},{6,2},{7,3},{8,4},{9,5},{10,6},{11,7},{12,8},{13,9},{1... | collective-permute-start | bytes 786440 | tf_op jit(solution)/shard_map/ppermute | solution.py:14
  224.7 37.4 %collective-permute-start.12 = (f32[256,256]{1,0:T(8,128)S(1)}, f32[256,256]{1,0:T(8,128)S(1)}, u32[]{:S(2)}, u32[]{:S(2)}) collective-permute-start(f32[256,256]{1,0:T(8,128)S(1)} %get-tuple-element.286), channel_id=1, source_target_pairs={{5,0},{6,1},{7,2},{8,3},{9,4},{10,5},{11,6},{12,7},{13,8},{14,9},{... | collective-permute-start | bytes 786440 | tf_op jit(solution)/shard_map/ppermute | solution.py:14
  228.5 60.8 %collective-permute-start.13 = (f32[256,256]{1,0:T(8,128)}, f32[256,256]{1,0:T(8,128)}, u32[]{:S(2)}, u32[]{:S(2)}) collective-permute-start(f32[256,256]{1,0:T(8,128)} %get-tuple-element.285), channel_id=1, source_target_pairs={{6,0},{7,1},{8,2},{9,3},{10,4},{11,5},{12,6},{13,7},{14,8},{15,9},... | collective-permute-start | bytes 786440 | tf_op jit(solution)/shard_map/ppermute | solution.py:14
  231.1 58.2 %collective-permute-start.14 = (f32[256,256]{1,0:T(8,128)}, f32[256,256]{1,0:T(8,128)}, u32[]{:S(2)}, u32[]{:S(2)}) collective-permute-start(f32[256,256]{1,0:T(8,128)} %get-tuple-element.284), channel_id=1, source_target_pairs={{7,0},{8,1},{9,2},{10,3},{11,4},{12,5},{13,6},{14,7},{15,8},{16,9}... | collective-permute-start | bytes 786440 | tf_op jit(solution)/shard_map/ppermute | solution.py:14
  236.9 52.4 %collective-permute-start.15 = (f32[256,256]{1,0:T(8,128)}, f32[256,256]{1,0:T(8,128)}, u32[]{:S(2)}, u32[]{:S(2)}) collective-permute-start(f32[256,256]{1,0:T(8,128)} %get-tuple-element.290), channel_id=1, source_target_pairs={{8,0},{9,1},{10,2},{11,3},{12,4},{13,5},{14,6},{15,7},{16,8},{17,9... | collective-permute-start | bytes 786440 | tf_op jit(solution)/shard_map/ppermute | solution.py:14
  245.7 54.5 %collective-permute-start.8 = (f32[256,256]{1,0:T(8,128)S(1)}, f32[256,256]{1,0:T(8,128)}, u32[]{:S(2)}, u32[]{:S(2)}) collective-permute-start(f32[256,256]{1,0:T(8,128)S(1)} %get-tuple-element.283), channel_id=1, source_target_pairs={{1,0},{2,1},{3,2},{4,3},{5,4},{6,5},{7,6},{8,7},{9,8},{10,9},{11,1... | collective-permute-start | bytes 786440 | tf_op jit(solution)/shard_map/ppermute | solution.py:14
  262.1 41.4 %collective-permute-start.9 = (f32[256,256]{1,0:T(8,128)S(1)}, f32[256,256]{1,0:T(8,128)}, u32[]{:S(2)}, u32[]{:S(2)}) collective-permute-start(f32[256,256]{1,0:T(8,128)S(1)} %get-tuple-element.289), channel_id=1, source_target_pairs={{2,0},{3,1},{4,2},{5,3},{6,4},{7,5},{8,6},{9,7},{10,8},{11,9},{12,... | collective-permute-start | bytes 786440 | tf_op jit(solution)/shard_map/ppermute | solution.py:14
  (7 other events, 6.9 us)
where the time goes:
time: 310 us; the launch traced here: 306 us
  matrix products  80.4 us (26%)
  local copies, waits for them, and re-layouts  79.5 us (26%)
  waiting for transfers between devices  65.4 us (21%)
  starting transfers between devices  65 us (21%)
  other arithmetic  13.1 us (4%)
    ppermute x16, waiting for transfers between devices, shifted(): return lax.ppermute(shard, axis, pairs)  65.4 us
    ppermute x16, starting transfers between devices, shifted(): return lax.ppermute(shard, axis, pairs)  65 us
    dot_general x18, matrix products, scores_of(): jnp.einsum('thd,ud->htu', queries3, block[:, :head_dim], preferred_elemen...  37.5 us
    squeeze x27, local copies, waits for them, and re-layouts, attention_core(): (row_max, row_sum), _ = lax.scan(stat_step, start, (blocks, masks))  25.7 us
    dot_general x9, matrix products, grad_step(): jnp.einsum('htu,thd->ud', weights, grads3, preferred_element_type=jnp.flo...  15.3 us
    dot_general x9, matrix products, grad_step(): jnp.einsum('thd,ud->htu', grads3, block[:, head_dim:], preferred_element_...  14.8 us
    while x81, local copies, waits for them, and re-layouts  13.9 us
    unnamed x18, local copies, waits for them, and re-layouts  8.68 us
  transfers between devices with their start and end apart: 16, of which 8 were waited for; matrix products, arithmetic and copies ran while one was open for 5% of the time, Pallas kernels for 0%

commit v1 on v0

v1 whole, which is shorter than its diff:
```python
import functools
import math

import jax
import jax.numpy as jnp
from jax import lax
from jax.experimental import pallas as pl
from jax.experimental.pallas import tpu as pltpu
from jax.sharding import PartitionSpec as P

AXES = ("node", "wide")
REACH = 4
GROUP = 4
MASKED = -1e30
VMEM_LIMIT = 48 * 1024 * 1024


def shifted(shard, by):
    peers = lax.axis_size(AXES)
    pairs = [(i, i + by) for i in range(peers) if 0 <= i + by < peers]
    return lax.ppermute(shard, AXES, pairs)


def swapped(shard):
    peers = lax.axis_size(AXES)
    return lax.ppermute(shard, AXES, [(i, i ^ 1) for i in range(peers)])


def dot_nt(a, b):
    return lax.dot_general(a, b, (((1,), (1,)), ((), ())), preferred_element_type=jnp.float32)


def dot_nn(a, b):
    return lax.dot_general(a, b, (((1,), (0,)), ((), ())), preferred_element_type=jnp.float32)


def stack_heads(ref, dim):
    return jnp.concatenate([ref[:, h * dim : (h + 1) * dim] for h in range(GROUP)], axis=0)


def fwd_body(rows, dim, count, diag, first, final, *refs):
    refs = list(refs)
    info, start, q = refs[:3]
    blocks = refs[3 : 3 + count]
    rest = refs[3 + count :]
    if not first:
        m_in, l_in, acc_in = rest[:3]
        rest = rest[3:]
    if final:
        grad = rest[0]
        rest = rest[1:]
    probs, m_out, m_run, l_run, acc = rest[:5]
    rest = rest[5:]
    if final:
        out, delta = rest[:2]
        rest = rest[2:]
    value_t = rest[0]
    fold = math.log2(math.e) / math.sqrt(dim)

    @pl.when(pl.program_id(0) == 0)
    def _():
        for b in range(count):
            value_t[b] = blocks[b][:, dim:].astype(jnp.float32).T.astype(jnp.bfloat16)

    queries = stack_heads(q, dim)
    if not first:
        m_run[...] = m_in[...]
        l_run[...] = l_in[...]
        acc[...] = acc_in[...]

    def work(b):
        own = diag and b == 0
        fresh = first and b == 0
        scores = dot_nt(blocks[b][:, :dim], queries)
        key_pos = lax.broadcasted_iota(jnp.int32, (rows, rows), 0) + info[2 * b]
        allowed = key_pos >= start[...]
        if own:
            allowed = allowed & (key_pos <= lax.broadcasted_iota(jnp.int32, (rows, rows), 1))
        for h in range(GROUP):
            lanes = pl.ds(h * rows, rows)
            s = jnp.where(allowed, scores[:, h * rows : (h + 1) * rows], MASKED)
            top = jnp.max(s, axis=0, keepdims=True)
            if fresh:
                m = top
            else:
                old = m_run[:, lanes]
                m = jnp.maximum(old, top)
                alpha = jnp.exp2((old - m) * fold)
            p = jnp.exp2((s - m) * fold)
            total = jnp.sum(p, axis=0, keepdims=True)
            pb = p.astype(jnp.bfloat16)
            probs[b, :, lanes] = pb
            part = dot_nn(value_t[b], pb)
            if fresh:
                l_run[:, lanes] = total
                acc[:, lanes] = part
            else:
                l_run[:, lanes] = l_run[:, lanes] * alpha + total
                acc[:, lanes] = acc[:, lanes] * alpha + part
            m_run[:, lanes] = m
            m_out[b, :, lanes] = m

    for b in range(count):
        if diag and b == 0:
            work(b)
        else:
            pl.when(info[2 * b + 1] != 0)(functools.partial(work, b))

    if final:
        for h in range(GROUP):
            lanes = pl.ds(h * rows, rows)
            cols = pl.ds(h * dim, dim)
            inverse = 1.0 / l_run[:, lanes]
            o_t = (acc[:, lanes] * inverse).astype(jnp.bfloat16).astype(jnp.float32)
            out[:, cols] = o_t.T.astype(jnp.bfloat16)
            g_t = grad[:, cols].astype(jnp.float32).T
            delta[:, lanes] = jnp.sum(o_t * g_t, axis=0, keepdims=True)
            l_run[:, lanes] = inverse


def bwd_body(rows, dim, count, first, last, *refs):
    refs = list(refs)
    info, q, grad, probs, m_then, m_fin, inverse, delta = refs[:8]
    blocks = refs[8 : 8 + count]
    rest = refs[8 + count :]
    if not first:
        dq_in = rest[0]
        rest = rest[1:]
    dq = rest[0]
    outs = rest[1 : 1 + count]
    rest = rest[1 + count :]
    key_t, dkv = rest[:2]
    dq_acc = rest[2] if last else dq
    fold = math.log2(math.e) / math.sqrt(dim)
    scale = 1.0 / math.sqrt(dim)

    @pl.when(pl.program_id(0) == 0)
    def _():
        dkv[...] = jnp.zeros_like(dkv)
        for b in range(count):
            key_t[b] = blocks[b][:, :dim].astype(jnp.float32).T.astype(jnp.bfloat16)

    queries = stack_heads(q, dim)
    grads = stack_heads(grad, dim)
    dq_acc[...] = jnp.zeros_like(dq_acc) if first else dq_in[...]

    def work(b):
        dprob = dot_nt(blocks[b][:, dim:], grads)
        ps, ds = [], []
        for h in range(GROUP):
            lanes = pl.ds(h * rows, rows)
            c = jnp.exp2((m_then[b, :, lanes] - m_fin[:, lanes]) * fold) * inverse[:, lanes]
            p = probs[b, :, lanes].astype(jnp.float32) * c
            d = (p * (dprob[:, h * rows : (h + 1) * rows] - delta[:, lanes])).astype(jnp.bfloat16)
            ps.append(p.astype(jnp.bfloat16))
            ds.append(d)
            dq_acc[:, lanes] += dot_nn(key_t[b], d)
        dkv[b, :, :dim] += dot_nn(jnp.concatenate(ds, axis=1), queries)
        dkv[b, :, dim:] += dot_nn(jnp.concatenate(ps, axis=1), grads)

    for b in range(count):
        pl.when(info[2 * b + 1] != 0)(functools.partial(work, b))

    if last:
        for h in range(GROUP):
            lanes = pl.ds(h * rows, rows)
            dq[:, h * dim : (h + 1) * dim] = (dq_acc[:, lanes] * scale).T.astype(jnp.bfloat16)

    @pl.when(pl.program_id(0) == pl.num_programs(0) - 1)
    def _():
        for b in range(count):
            outs[b][:, :dim] = (dkv[b, :, :dim] * scale).astype(outs[b].dtype)
            outs[b][:, dim:] = dkv[b, :, dim:].astype(outs[b].dtype)


def specs_of(rows, dim):
    width = GROUP * rows
    whole = lambda *shape: pl.BlockSpec(shape, lambda g: (0,) * len(shape))
    return dict(
        info=pl.BlockSpec(memory_space=pltpu.SMEM),
        start=whole(1, rows),
        heads=pl.BlockSpec((rows, GROUP * dim), lambda g: (0, g)),
        block=whole(rows, 2 * dim),
        row=pl.BlockSpec((1, width), lambda g: (0, g)),
        tall=pl.BlockSpec((dim, width), lambda g: (0, g)),
        probs=lambda n: pl.BlockSpec((n, rows, width), lambda g: (0, 0, g)),
        rows=lambda n: pl.BlockSpec((n, 1, width), lambda g: (0, 0, g)),
    )


def forward(info, start, queries, blocks, state, grad, diag):
    rows, dim = blocks[0].shape[0], blocks[0].shape[1] // 2
    heads = queries.shape[1] // dim
    count, first, final = len(blocks), state is None, grad is not None
    s = specs_of(rows, dim)
    width = heads * rows
    args = [info, start, queries, *blocks]
    in_specs = [s["info"], s["start"], s["heads"]] + [s["block"]] * count
    if not first:
        args += list(state)
        in_specs += [s["row"], s["row"], s["tall"]]
    if final:
        args.append(grad)
        in_specs.append(s["heads"])
    f32 = jnp.float32
    out_shape = [
        jax.ShapeDtypeStruct((count, rows, width), jnp.bfloat16),
        jax.ShapeDtypeStruct((count, 1, width), f32),
        jax.ShapeDtypeStruct((1, width), f32),
        jax.ShapeDtypeStruct((1, width), f32),
        jax.ShapeDtypeStruct((dim, width), f32),
    ]
    out_specs = [s["probs"](count), s["rows"](count), s["row"], s["row"], s["tall"]]
    if final:
        out_shape += [
            jax.ShapeDtypeStruct((rows, heads * dim), jnp.bfloat16),
            jax.ShapeDtypeStruct((1, width), f32),
        ]
        out_specs += [s["heads"], s["row"]]
    return pl.pallas_call(
        functools.partial(fwd_body, rows, dim, count, diag, first, final),
        grid=(heads // GROUP,),
        in_specs=in_specs,
        out_specs=out_specs,
        out_shape=out_shape,
        scratch_shapes=[pltpu.VMEM((count, dim, rows), jnp.bfloat16)],
        compiler_params=pltpu.CompilerParams(vmem_limit_bytes=VMEM_LIMIT),
        cost_estimate=pl.CostEstimate(
            flops=4 * count * rows * width * dim,
            bytes_accessed=3 * count * rows * width,
            transcendentals=count * rows * width,
        ),
    )(*args)


def backward(info, queries, grad, probs, m_then, m_fin, inverse, delta, blocks, dq, out_types, last):
    rows, dim = blocks[0].shape[0], blocks[0].shape[1] // 2
    heads = queries.shape[1] // dim
    count, first = len(blocks), dq is None
    s = specs_of(rows, dim)
    width = heads * rows
    args = [info, queries, grad, probs, m_then, m_fin, inverse, delta, *blocks]
    in_specs = [s["info"], s["heads"], s["heads"], s["probs"](count), s["rows"](count)]
    in_specs += [s["row"]] * 3 + [s["block"]] * count
    if not first:
        args.append(dq)
        in_specs.append(s["tall"])
    if last:
        out_shape = [jax.ShapeDtypeStruct((rows, heads * dim), jnp.bfloat16)]
        out_specs = [s["heads"]]
    else:
        out_shape = [jax.ShapeDtypeStruct((dim, width), jnp.float32)]
        out_specs = [s["tall"]]
    out_shape += [jax.ShapeDtypeStruct((rows, 2 * dim), t) for t in out_types]
    out_specs += [s["block"]] * count
    scratch = [
        pltpu.VMEM((count, dim, rows), jnp.bfloat16),
        pltpu.VMEM((count, rows, 2 * dim), jnp.float32),
    ]
    if last:
        scratch.append(pltpu.VMEM((dim, GROUP * rows), jnp.float32))
    return pl.pallas_call(
        functools.partial(bwd_body, rows, dim, count, first, last),
        grid=(heads // GROUP,),
        in_specs=in_specs,
        out_specs=out_specs,
        out_shape=out_shape,
        scratch_shapes=scratch,
        compiler_params=pltpu.CompilerParams(vmem_limit_bytes=VMEM_LIMIT),
        cost_estimate=pl.CostEstimate(
            flops=8 * count * rows * width * dim,
            bytes_accessed=3 * count * rows * width,
            transcendentals=0,
        ),
    )(*args)


def on_device(queries, keys, values, out_grad, doc_lengths):
    rows, dim = keys.shape
    f32, bf16 = jnp.float32, jnp.bfloat16
    device = lax.axis_index(AXES)
    odd = device % 2
    doc_ends = jnp.cumsum(doc_lengths)
    here = device * rows
    pos = here + jnp.arange(rows, dtype=jnp.int32)
    start = jnp.max(jnp.where(doc_ends[:, None] <= pos[None, :], doc_ends[:, None], 0), axis=0)
    start = (start - here)[None, :]
    first_start = start[0, 0]

    def info_of(chips):
        base = []
        for chip in chips:
            base += [jnp.int32(-2 * chip * rows), (-2 * chip + 1 - 2 * odd) * rows]
        base = jnp.stack(base)
        active = (base + rows > first_start) & (base <= 0)
        return jnp.stack([base, active.astype(jnp.int32)], axis=1).reshape(-1)

    own = jnp.concatenate([keys, values], axis=1)
    mine = [own]
    mine.append(shifted(own, 2))
    mine.append(shifted(own, 4))
    other = list(swapped(jnp.stack(mine[:3])))
    mine.append(shifted(mine[2], 2))
    mine.append(shifted(mine[2], 4))
    other += list(swapped(jnp.stack(mine[3:])))
    pair = lambda chips: [x for c in chips for x in (mine[c], other[c])]

    near, far = (0, 1, 2), (3, 4)
    info_n, info_f = info_of(near), info_of(far)
    probs_n, m_n, m1, l1, acc1 = forward(info_n, start, queries, pair(near), None, None, True)
    probs_f, m_f, m_fin, inverse, _, out, delta = forward(
        info_f, start, queries, pair(far), (m1, l1, acc1), out_grad, False
    )
    dq, m3, o3, m4, o4 = backward(
        info_f, queries, out_grad, probs_f, m_f, m_fin, inverse, delta, pair(far), None,
        (f32, bf16) * 2, False,
    )
    grad_q, m0, o0, m1_, o1, m2, o2 = backward(
        info_n, queries, out_grad, probs_n, m_n, m_fin, inverse, delta, pair(near), dq,
        (f32, bf16) * 3, True,
    )
    got = swapped(jnp.stack([o3, o4]))
    t3 = (m3 + got[0].astype(f32)).astype(bf16)
    t4 = (m4 + got[1].astype(f32)).astype(bf16)
    r4 = shifted(t4, -4)
    r3 = shifted(t3, -2)
    got = swapped(jnp.stack([o0, o1, o2]))
    t2 = (m2 + got[2].astype(f32) + r4.astype(f32) + r3.astype(f32)).astype(bf16)
    t1 = (m1_ + got[1].astype(f32)).astype(bf16)
    r2 = shifted(t2, -4)
    r1 = shifted(t1, -2)
    total = m0 + got[0].astype(f32) + r1.astype(f32) + r2.astype(f32)
    return (out, grad_q, total[:, :dim].astype(bf16), total[:, dim:].astype(bf16))


def solution(mesh):
    rows = P(AXES, None)
    return jax.shard_map(
        on_device,
        mesh=mesh,
        in_specs=(rows, rows, rows, rows, P()),
        out_specs=(rows, rows, rows, rows),
        check_vma=False,
    )
```

time: 310 us -> 103 us (0.33); the launches traced: 306 us -> 104 us
  matrix products: 80.4 us -> 0 us
  local copies, waits for them, and re-layouts: 79.5 us -> 5.34 us
  starting transfers between devices: 65 us -> 27.6 us
  Pallas kernels: 0 us -> 34.8 us
  waiting for transfers between devices: 65.4 us -> 33.3 us
  other arithmetic: 13.1 us -> 2.28 us
    dot_general x63 -> x0, matrix products: 80.4 us -> none  [the longest x18 37.5 us: scores_of(): jnp.einsum('thd,ud->htu', queries3, block[:, :head_dim], preferred_elemen...]
    ppermute x16 -> x12, starting transfers between devices: 65 us -> 27.6 us  [the longest x8 26.6 us: shifted(): return lax.ppermute(shard, AXES, pairs)]
    pallas_call x0 -> x4, Pallas kernels: none -> 34.8 us  [the longest x2 18.1 us: backward(): pl.pallas_call(functools.partial(bwd_body, rows, dim, count, first, last)...]
    ppermute x16 -> x12, waiting for transfers between devices: 65.4 us -> 33.3 us  [the longest x8 32.3 us: shifted(): return lax.ppermute(shard, AXES, pairs)]
    squeeze x28 -> x0, local copies, waits for them, and re-layouts: 28.2 us -> none  [the longest x27 25.7 us: attention_core(): (row_max, row_sum), _ = lax.scan(stat_step, start, (blocks, masks))]
    broadcast_in_dim x18 -> x0, local copies, waits for them, and re-layouts: 16.1 us -> none  [the longest x9 8.44 us: out_step(): jnp.where(allowed[None], jnp.exp(scores_of(block) - log_total[..., None])...]
    while x81 -> x0, local copies, waits for them, and re-layouts: 13.9 us -> none
    reduce_sum x12 -> x0, other arithmetic: 8.51 us -> none  [the longest x9 4.64 us: stat_step(): jnp.sum(terms, axis=-1)]
  transfers between devices with their start and end apart: 16 -> 12, of which waited for: 8 -> 9; matrix products, arithmetic and copies ran while one was open for 5% -> 4% of each run, Pallas kernels for 0% -> 11%
where the time goes in v1:
time: 103 us; the launch traced here: 104 us
  Pallas kernels  34.8 us (34%)
  waiting for transfers between devices  33.3 us (32%)
  starting transfers between devices  27.6 us (27%)
  local copies, waits for them, and re-layouts  5.34 us (5%)
  other arithmetic  2.28 us (2%)
    ppermute x8, waiting for transfers between devices, shifted(): return lax.ppermute(shard, AXES, pairs)  32.3 us
    ppermute x8, starting transfers between devices, shifted(): return lax.ppermute(shard, AXES, pairs)  26.6 us
    pallas_call x2, Pallas kernels, backward(): pl.pallas_call(functools.partial(bwd_body, rows, dim, count, first, last)...  18.1 us
    pallas_call x2, Pallas kernels, forward(): pl.pallas_call(functools.partial(fwd_body, rows, dim, count, diag, first,...  16.7 us
  transfers between devices with their start and end apart: 12, of which 9 were waited for; matrix products, arithmetic and copies ran while one was open for 4% of the time, Pallas kernels for 11%

profile of v1, /device:TPU:24, one launch (start us, length us, event | category | flops | bytes accessed | tf_op | source)
XLA Modules:
  0.0 104.2 jit_solution(5209463241292531607)
XLA Ops:
  0.6 0.9 constant_dynamic-update-slice_fusion.1
  1.6 0.9 constant_dynamic-update-slice_fusion.refs_3_.refs_8_
  2.4 3.8 %collective-permute-start.4 = (bf16[256,256]{1,0:T(8,128)(2,1)S(1)}, bf16[256,256]{1,0:T(8,128)(2,1)S(1)}, u32[]{:S(2)}, u32[]{:S(2)}) collective-permute-start(bf16[256,256]{1,0:T(8,128)(2,1)S(1)} %constant_dynamic-update-slice_fusion.refs_3_.refs_8_), channel_id=1, source_target_pairs={{0,2},{1,3},{2,4},{3,5},{4,6},{5,7},{6,8},{7,9},{8,10},{9,11},{10,... | collective-permute-start | bytes 393224 | tf_op jit(solution)/shard_map/ppermute | solution.py:21
  6.2 5.2 %collective-permute-start = (bf16[256,256]{1,0:T(8,128)(2,1)S(1)}, bf16[256,256]{1,0:T(8,128)(2,1)S(1)}, u32[]{:S(2)}, u32[]{:S(2)}) collective-permute-start(bf16[256,256]{1,0:T(8,128)(2,1)S(1)} %constant_dynamic-update-slice_fusion.refs_3_.refs_8_), channel_id=1, source_target_pairs={{0,4},{1,5},{2,6},{3,7},{4,8},{5,9},{6,10},{7,11},{8,12},{9,13},{1... | collective-permute-start | bytes 393224 | tf_op jit(solution)/shard_map/ppermute | solution.py:21
  11.5 0.8 copy.15
  12.2 0.2 reduce-window.8
  12.4 0.1 reduce
  12.5 0.1 select_reduce_fusion
  12.6 0.5 slice.34
  13.2 0.1 stack.110
  13.3 0.6 and_convert_fusion
  13.9 7.6 %collective-permute-done.refs_7_.refs_12_ = bf16[256,256]{1,0:T(8,128)(2,1)S(1)} collective-permute-done((bf16[256,256]{1,0:T(8,128)(2,1)S(1)}, bf16[256,256]{1,0:T(8,128)(2,1)S(1)}, u32[]{:S(2)}, u32[]{:S(2)}) %collective-permute-start) | collective-permute-done | bytes 131104 | tf_op jit(solution)/shard_map/ppermute | solution.py:21
  21.5 1.9 %collective-permute-start.2 = (bf16[256,256]{1,0:T(8,128)(2,1)S(1)}, bf16[256,256]{1,0:T(8,128)(2,1)S(1)}, u32[]{:S(2)}, u32[]{:S(2)}) collective-permute-start(bf16[256,256]{1,0:T(8,128)(2,1)S(1)} %collective-permute-done.refs_7_.refs_12_), channel_id=1, source_target_pairs={{0,4},{1,5},{2,6},{3,7},{4,8},{5,9},{6,10},{7,11},{8,12},{9,13},{1... | collective-permute-start | bytes 393224 | tf_op jit(solution)/shard_map/ppermute | solution.py:21
  23.4 3.6 %collective-permute-start.1 = (bf16[256,256]{1,0:T(8,128)(2,1)S(1)}, bf16[256,256]{1,0:T(8,128)(2,1)S(1)}, u32[]{:S(2)}, u32[]{:S(2)}) collective-permute-start(bf16[256,256]{1,0:T(8,128)(2,1)S(1)} %collective-permute-done.refs_7_.refs_12_), channel_id=1, source_target_pairs={{0,2},{1,3},{2,4},{3,5},{4,6},{5,7},{6,8},{7,9},{8,10},{9,11},{10,... | collective-permute-start | bytes 393224 | tf_op jit(solution)/shard_map/ppermute | solution.py:21
  27.0 0.1 add_bitcast_fusion
  27.0 0.7 and_convert_fusion.1
  27.8 7.5 %collective-permute-done.2.refs_5_.refs_10_ = bf16[256,256]{1,0:T(8,128)(2,1)S(1)} collective-permute-done((bf16[256,256]{1,0:T(8,128)(2,1)S(1)}, bf16[256,256]{1,0:T(8,128)(2,1)S(1)}, u32[]{:S(2)}, u32[]{:S(2)}) %collective-permute-start.2) | collective-permute-done | bytes 131104 | tf_op jit(solution)/shard_map/ppermute | solution.py:21
  35.2 1.9 %collective-permute-done.1.refs_3_.refs_8_ = bf16[256,256]{1,0:T(8,128)(2,1)S(1)} collective-permute-done((bf16[256,256]{1,0:T(8,128)(2,1)S(1)}, bf16[256,256]{1,0:T(8,128)(2,1)S(1)}, u32[]{:S(2)}, u32[]{:S(2)}) %collective-permute-start.1) | collective-permute-done | bytes 131104 | tf_op jit(solution)/shard_map/ppermute | solution.py:21
  37.2 0.1 collective-permute-start.3
  37.3 0.0 collective-permute-done.4.refs_5_.refs_10_
  37.4 0.6 collective-permute-start.5
  38.0 0.1 copy.16
  38.1 0.1 reshape.317.refs_0_
  38.2 0.1 stack.105
  38.3 0.1 copy.17
  38.3 0.1 reshape.318.refs_0_
  38.4 0.4 collective-permute-done.3
  38.9 0.5 collective-permute-done.5
  39.4 0.0 copy-start
  39.5 1.0 copy-done
  40.5 9.7 %shard_map.84 = (bf16[6,256,2048]{2,1,0:T(8,128)(2,1)}, f32[6,1,2048]{2,1,0:T(1,128)S(1)}, f32[1,2048]{1,0:T(1,128)S(1)}, f32[1,2048]{1,0:T(1,128)S(1)}, f32[128,2048]{1,0:T(8,128)S(1)}) custom-call(s32[12]{0:T(128)S(1)} %reshape.318.refs_0_, s32[1,256]{1,0:T(1,128)S(1)} %bitcast.72, bf16[256,1024]{1,0:T(8,128)(2,1)S(1)} %copy-done, ...), custom_call_target="tpu_custom_call" | custom-call | flops 1610612736 | bytes 9437184 | tf_op jit(solution)/shard_map/pallas_call | solution.py:220
  50.2 7.0 %shard_map.85 = (bf16[4,256,2048]{2,1,0:T(8,128)(2,1)}, f32[4,1,2048]{2,1,0:T(1,128)S(1)}, f32[1,2048]{1,0:T(1,128)S(1)}, f32[1,2048]{1,0:T(1,128)S(1)}, f32[128...) custom-call(s32[8]{0:T(128)S(1)} %reshape.317.refs_0_, s32[1,256]{1,0:T(1,128)S(1)} %bitcast.73, ...), custom_call_target="tpu_custom_call" | custom-call | flops 1073741824 | bytes 6291456 | tf_op jit(solution)/shard_map/pallas_call | solution.py:220
  57.2 6.8 %shard_map.86 = (f32[128,2048]{1,0:T(8,128)S(1)}, f32[256,256]{1,0:T(8,128)S(1)}, bf16[256,256]{1,0:T(8,128)(2,1)S(1)}, f32[256,256]{1,0:T(8,128)S(1)}, bf16[256,256]{1,0:T(8,128)(2,1)S(1)}) custom-call(s32[8]{0:T(128)S(1)} %reshape.317.refs_0_, bf16[256,1024]{1,0:T(8,128)(2,1)S(1)} %copy-done.1, bf16[256,1024]{1,0:T(8,128)(2,1)S(1)} %copy-done.2, ...), custom_call_target="tpu_custom_call" | custom-call | flops 2147483648 | bytes 6291456 | tf_op jit(solution)/shard_map/pallas_call | solution.py:262
  64.1 0.3 collective-permute-start.8
  64.4 11.3 %shard_map.87 = (bf16[256,1024]{1,0:T(8,128)(2,1)}, f32[256,256]{1,0:T(8,128)S(1)}, bf16[256,256]{1,0:T(8,128)(2,1)S(1)}, f32[256,256]{1,0:T(8,128)S(1)}, bf16[2...) custom-call(s32[12]{0:T(128)S(1)} %reshape.318.refs_0_, ...), custom_call_target="tpu_custom_call" | custom-call | flops 3221225472 | bytes 9437184 | tf_op jit(solution)/shard_map/pallas_call | solution.py:262
  75.7 0.1 collective-permute-start.6
  75.8 0.1 fusion.1
  75.9 1.9 %collective-permute-start.9 = (bf16[256,256]{1,0:T(8,128)(2,1)S(1)}, bf16[256,256]{1,0:T(8,128)(2,1)S(1)}, u32[]{:S(2)}, u32[]{:S(2)}) collective-permute-start(bf16[256,256]{1,0:T(8,128)(2,1)S(1)} %get-tuple-element.55), channel_id=1, source_target_pairs={{4,0},{5,1},{6,2},{7,3},{8,4},{9,5},{10,6},{11,7},{12,8},{13,9},{1... | collective-permute-start | bytes 393224 | tf_op jit(solution)/shard_map/ppermute | solution.py:21
  77.8 1.9 %collective-permute-start.10 = (bf16[256,256]{1,0:T(8,128)(2,1)S(1)}, bf16[256,256]{1,0:T(8,128)(2,1)S(1)}, u32[]{:S(2)}, u32[]{:S(2)}) collective-permute-start(bf16[256,256]{1,0:T(8,128)(2,1)S(1)} %get-tuple-element.56), channel_id=1, source_target_pairs={{2,0},{3,1},{4,2},{5,3},{6,4},{7,5},{8,6},{9,7},{10,8},{11,9},{12,... | collective-permute-start | bytes 393224 | tf_op jit(solution)/shard_map/ppermute | solution.py:21
  79.8 5.2 %collective-permute-done.9 = bf16[256,256]{1,0:T(8,128)(2,1)S(1)} collective-permute-done((bf16[256,256]{1,0:T(8,128)(2,1)S(1)}, bf16[256,256]{1,0:T(8,128)(2,1)S(1)}, u32[]{:S(2)}, u32[]{:S(2)}) %collective-permute-start.9) | collective-permute-done | bytes 131104 | tf_op jit(solution)/shard_map/ppermute | solution.py:21
  85.0 2.4 %collective-permute-done.10 = bf16[256,256]{1,0:T(8,128)(2,1)S(1)} collective-permute-done((bf16[256,256]{1,0:T(8,128)(2,1)S(1)}, bf16[256,256]{1,0:T(8,128)(2,1)S(1)}, u32[]{:S(2)}, u32[]{:S(2)}) %collective-permute-start.10) | collective-permute-done | bytes 131104 | tf_op jit(solution)/shard_map/ppermute | solution.py:21
  87.4 0.1 fusion.5
  87.5 6.3 %collective-permute-start.7 = (bf16[256,256]{1,0:T(8,128)(2,1)S(1)}, bf16[256,256]{1,0:T(8,128)(2,1)S(1)}, u32[]{:S(2)}, u32[]{:S(2)}) collective-permute-start(bf16[256,256]{1,0:T(8,128)(2,1)S(1)} %get-tuple-element.50), channel_id=1, source_target_pairs={{2,0},{3,1},{4,2},{5,3},{6,4},{7,5},{8,6},{9,7},{10,8},{11,9},{12,... | collective-permute-start | bytes 393224 | tf_op jit(solution)/shard_map/ppermute | solution.py:21
  93.8 1.9 %collective-permute-start.11 = (bf16[256,256]{1,0:T(8,128)(2,1)S(1)}, bf16[256,256]{1,0:T(8,128)(2,1)S(1)}, u32[]{:S(2)}, u32[]{:S(2)}) collective-permute-start(bf16[256,256]{1,0:T(8,128)(2,1)S(1)} %get-tuple-element.51), channel_id=1, source_target_pairs={{4,0},{5,1},{6,2},{7,3},{8,4},{9,5},{10,6},{11,7},{12,8},{13,9},{1... | collective-permute-start | bytes 393224 | tf_op jit(solution)/shard_map/ppermute | solution.py:21
  95.8 4.5 %collective-permute-done.7 = bf16[256,256]{1,0:T(8,128)(2,1)S(1)} collective-permute-done((bf16[256,256]{1,0:T(8,128)(2,1)S(1)}, bf16[256,256]{1,0:T(8,128)(2,1)S(1)}, u32[]{:S(2)}, u32[]{:S(2)}) %collective-permute-start.7) | collective-permute-done | bytes 131104 | tf_op jit(solution)/shard_map/ppermute | solution.py:21
  100.3 3.2 %collective-permute-done.11 = bf16[256,256]{1,0:T(8,128)(2,1)S(1)} collective-permute-done((bf16[256,256]{1,0:T(8,128)(2,1)S(1)}, bf16[256,256]{1,0:T(8,128)(2,1)S(1)}, u32[]{:S(2)}, u32[]{:S(2)}) %collective-permute-start.11) | collective-permute-done | bytes 131104 | tf_op jit(solution)/shard_map/ppermute | solution.py:21
  103.5 0.1 fusion.8
  103.5 0.7 fusion.9
  (16 shorter events, 0.2 us)
Async XLA Ops:
  0.6 49.6 %copy-start.2 = (bf16[256,1024]{1,0:T(8,128)(2,1)S(1)}, bf16[256,1024]{1,0:T(8,128)(2,1)}, u32[]{:S(2)}) copy-start(bf16[256,1024]{1,0:T(8,128)(2,1)} %refs_2_.7) | copy-start | bytes 1572868
  2.4 34.9 %collective-permute-start.4 = (bf16[256,256]{1,0:T(8,128)(2,1)S(1)}, bf16[256,256]{1,0:T(8,128)(2,1)S(1)}, u32[]{:S(2)}, u32[]{:S(2)}) collective-permute-start(bf16[256,256]{1,0:T(8,128)(2,1)S(1)} %constant_dynamic-update-slice_fusion.refs_3_.refs_8_), channel_id=1, source_target_pairs={{0,2},{1,3},{2,4},{3,5},{4,6},{5,7},{6,8},{7,9},{8,10},{9,11},{10,... | collective-permute-start | bytes 393224 | tf_op jit(solution)/shard_map/ppermute | solution.py:21
  6.2 15.2 %collective-permute-start = (bf16[256,256]{1,0:T(8,128)(2,1)S(1)}, bf16[256,256]{1,0:T(8,128)(2,1)S(1)}, u32[]{:S(2)}, u32[]{:S(2)}) collective-permute-start(bf16[256,256]{1,0:T(8,128)(2,1)S(1)} %constant_dynamic-update-slice_fusion.refs_3_.refs_8_), channel_id=1, source_target_pairs={{0,4},{1,5},{2,6},{3,7},{4,8},{5,9},{6,10},{7,11},{8,12},{9,13},{1... | collective-permute-start | bytes 393224 | tf_op jit(solution)/shard_map/ppermute | solution.py:21
  21.5 13.8 %collective-permute-start.2 = (bf16[256,256]{1,0:T(8,128)(2,1)S(1)}, bf16[256,256]{1,0:T(8,128)(2,1)S(1)}, u32[]{:S(2)}, u32[]{:S(2)}) collective-permute-start(bf16[256,256]{1,0:T(8,128)(2,1)S(1)} %collective-permute-done.refs_7_.refs_12_), channel_id=1, source_target_pairs={{0,4},{1,5},{2,6},{3,7},{4,8},{5,9},{6,10},{7,11},{8,12},{9,13},{1... | collective-permute-start | bytes 393224 | tf_op jit(solution)/shard_map/ppermute | solution.py:21
  23.4 13.8 %collective-permute-start.1 = (bf16[256,256]{1,0:T(8,128)(2,1)S(1)}, bf16[256,256]{1,0:T(8,128)(2,1)S(1)}, u32[]{:S(2)}, u32[]{:S(2)}) collective-permute-start(bf16[256,256]{1,0:T(8,128)(2,1)S(1)} %collective-permute-done.refs_7_.refs_12_), channel_id=1, source_target_pairs={{0,2},{1,3},{2,4},{3,5},{4,6},{5,7},{6,8},{7,9},{8,10},{9,11},{10,... | collective-permute-start | bytes 393224 | tf_op jit(solution)/shard_map/ppermute | solution.py:21
  37.2 20.0 %copy-start.1 = (bf16[256,1024]{1,0:T(8,128)(2,1)S(1)}, bf16[256,1024]{1,0:T(8,128)(2,1)}, u32[]{:S(2)}) copy-start(bf16[256,1024]{1,0:T(8,128)(2,1)} %refs_1_.3) | copy-start | bytes 1572868
  37.2 1.6 %collective-permute-start.3 = (bf16[2,256,256]{2,1,0:T(8,128)(2,1)S(1)}, bf16[2,256,256]{2,1,0:T(8,128)(2,1)S(1)}, u32[]{:S(2)}, u32[]{:S(2)}) collective-permute-start(bf16[2,256,256]{2,1,0:T(8,128)(2,1)S(1)} %pad_maximum_fusion.2), channel_id=1, source_target_pairs={{0,1},{1,0},{2,3},{3,2},{4,5},{5,4},{6,7},{7,6},{8,9},{9,8},{10,11... | collective-permute-start | bytes 786440 | tf_op jit(solution)/shard_map/ppermute | solution.py:26
  37.4 2.0 %collective-permute-start.5 = (bf16[3,256,256]{2,1,0:T(8,128)(2,1)S(1)}, bf16[3,256,256]{2,1,0:T(8,128)(2,1)S(1)}, u32[]{:S(2)}, u32[]{:S(2)}) collective-permute-start(bf16[3,256,256]{2,1,0:T(8,128)(2,1)S(1)} %pad_maximum_fusion), channel_id=1, source_target_pairs={{0,1},{1,0},{2,3},{3,2},{4,5},{5,4},{6,7},{7,6},{8,9},{9,8},{10,11... | collective-permute-start | bytes 1179656 | tf_op jit(solution)/shard_map/ppermute | solution.py:26
  39.4 1.0 %copy-start = (bf16[256,1024]{1,0:T(8,128)(2,1)S(1)}, bf16[256,1024]{1,0:T(8,128)(2,1)}, u32[]{:S(2)}) copy-start(bf16[256,1024]{1,0:T(8,128)(2,1)} %refs_1_.3) | copy-start | bytes 1572868
  64.1 11.7 %collective-permute-start.8 = (bf16[2,256,256]{2,1,0:T(8,128)(2,1)S(1)}, bf16[2,256,256]{2,1,0:T(8,128)(2,1)S(1)}, u32[]{:S(2)}, u32[]{:S(2)}) collective-permute-start(bf16[2,256,256]{2,1,0:T(8,128)(2,1)S(1)} %pad_maximum_fusion.3), channel_id=1, source_target_pairs={{0,1},{1,0},{2,3},{3,2},{4,5},{5,4},{6,7},{7,6},{8,9},{9,8},{10,11... | collective-permute-start | bytes 786440 | tf_op jit(solution)/shard_map/ppermute | solution.py:26
  75.7 11.7 %collective-permute-start.6 = (bf16[3,256,256]{2,1,0:T(8,128)(2,1)S(1)}, bf16[3,256,256]{2,1,0:T(8,128)(2,1)S(1)}, u32[]{:S(2)}, u32[]{:S(2)}) collective-permute-start(bf16[3,256,256]{2,1,0:T(8,128)(2,1)S(1)} %pad_maximum_fusion.1), channel_id=1, source_target_pairs={{0,1},{1,0},{2,3},{3,2},{4,5},{5,4},{6,7},{7,6},{8,9},{9,8},{10,11... | collective-permute-start | bytes 1179656 | tf_op jit(solution)/shard_map/ppermute | solution.py:26
  75.9 9.1 %collective-permute-start.9 = (bf16[256,256]{1,0:T(8,128)(2,1)S(1)}, bf16[256,256]{1,0:T(8,128)(2,1)S(1)}, u32[]{:S(2)}, u32[]{:S(2)}) collective-permute-start(bf16[256,256]{1,0:T(8,128)(2,1)S(1)} %get-tuple-element.55), channel_id=1, source_target_pairs={{4,0},{5,1},{6,2},{7,3},{8,4},{9,5},{10,6},{11,7},{12,8},{13,9},{1... | collective-permute-start | bytes 393224 | tf_op jit(solution)/shard_map/ppermute | solution.py:21
  77.8 9.6 %collective-permute-start.10 = (bf16[256,256]{1,0:T(8,128)(2,1)S(1)}, bf16[256,256]{1,0:T(8,128)(2,1)S(1)}, u32[]{:S(2)}, u32[]{:S(2)}) collective-permute-start(bf16[256,256]{1,0:T(8,128)(2,1)S(1)} %get-tuple-element.56), channel_id=1, source_target_pairs={{2,0},{3,1},{4,2},{5,3},{6,4},{7,5},{8,6},{9,7},{10,8},{11,9},{12,... | collective-permute-start | bytes 393224 | tf_op jit(solution)/shard_map/ppermute | solution.py:21
  87.5 12.8 %collective-permute-start.7 = (bf16[256,256]{1,0:T(8,128)(2,1)S(1)}, bf16[256,256]{1,0:T(8,128)(2,1)S(1)}, u32[]{:S(2)}, u32[]{:S(2)}) collective-permute-start(bf16[256,256]{1,0:T(8,128)(2,1)S(1)} %get-tuple-element.50), channel_id=1, source_target_pairs={{2,0},{3,1},{4,2},{5,3},{6,4},{7,5},{8,6},{9,7},{10,8},{11,9},{12,... | collective-permute-start | bytes 393224 | tf_op jit(solution)/shard_map/ppermute | solution.py:21
  93.8 9.6 %collective-permute-start.11 = (bf16[256,256]{1,0:T(8,128)(2,1)S(1)}, bf16[256,256]{1,0:T(8,128)(2,1)S(1)}, u32[]{:S(2)}, u32[]{:S(2)}) collective-permute-start(bf16[256,256]{1,0:T(8,128)(2,1)S(1)} %get-tuple-element.51), channel_id=1, source_target_pairs={{4,0},{5,1},{6,2},{7,3},{8,4},{9,5},{10,6},{11,7},{12,8},{13,9},{1... | collective-permute-start | bytes 393224 | tf_op jit(solution)/shard_map/ppermute | solution.py:21

commit v2 on v0

v2 whole, which is shorter than its diff:
```python
import functools
import math

import jax
import jax.numpy as jnp
from jax import lax
from jax.experimental import pallas as pl
from jax.experimental.pallas import tpu as pltpu
from jax.sharding import PartitionSpec as P

AXES = ("node", "wide")
MASKED = -1e30
VMEM_LIMIT = 16 * 1024 * 1024
HERE = pl.BlockSpec(memory_space=pltpu.VMEM)


def shifted(shard, by):
    peers = lax.axis_size(AXES)
    pairs = [(i, i + by) for i in range(peers) if 0 <= i + by < peers]
    return lax.ppermute(shard, AXES, pairs)


def swapped(shard):
    peers = lax.axis_size(AXES)
    return lax.ppermute(shard, AXES, [(i, i ^ 1) for i in range(peers)])


def dot_nt(a, b):
    return lax.dot_general(a, b, (((1,), (1,)), ((), ())), preferred_element_type=jnp.float32)


def dot_nn(a, b):
    return lax.dot_general(a, b, (((1,), (0,)), ((), ())), preferred_element_type=jnp.float32)


def prep_body(keys, values, lengths, own, meta):
    rows, dim = keys.shape
    docs = lengths.shape[1]
    own[:, :dim] = keys[...]
    own[:, dim:] = values[...]
    device = lax.axis_index(AXES[0]) * lax.axis_size(AXES[1]) + lax.axis_index(AXES[1])
    here = device * rows
    later = lax.broadcasted_iota(jnp.int32, (docs, docs), 0)
    earlier = lax.broadcasted_iota(jnp.int32, (docs, docs), 1)
    counted = jnp.where(earlier <= later, lengths[...].astype(jnp.float32), 0.0)
    ends = jnp.sum(counted, axis=1, keepdims=True)
    pos = (lax.broadcasted_iota(jnp.int32, (docs, rows), 1) + here).astype(jnp.float32)
    start = jnp.max(jnp.where(ends <= pos, ends, 0.0), axis=0, keepdims=True)
    meta[0:1, :] = start.astype(jnp.int32) - here
    meta[1:2, :] = jnp.full((1, rows), device % 2, jnp.int32)


def prepare(keys, values, lengths):
    rows, dim = keys.shape
    return pl.pallas_call(
        prep_body,
        in_specs=[HERE] * 3,
        out_specs=[HERE] * 2,
        out_shape=[
            jax.ShapeDtypeStruct((rows, 2 * dim), keys.dtype),
            jax.ShapeDtypeStruct((2, rows), jnp.int32),
        ],
        compiler_params=pltpu.CompilerParams(vmem_limit_bytes=VMEM_LIMIT),
    )(keys, values, lengths)


def stage_body(plan, *refs):
    rows, dim, heads = plan["rows"], plan["dim"], plan["heads"]
    fwd, bwd = plan["fwd"], plan["bwd"]
    ref = dict(zip(plan["names"], refs))
    fold = math.log2(math.e) / math.sqrt(dim)
    scale = 1.0 / math.sqrt(dim)
    bf16, f32 = jnp.bfloat16, jnp.float32
    meta = ref["meta"]
    start = meta[0:1, :]
    earliest = jnp.min(start)
    odd = jnp.max(meta[1:2, :])
    blocks = sorted(set(fwd) | set(bwd))
    cols = [slice(h * dim, (h + 1) * dim) for h in range(heads)]
    lanes = [slice(h * rows, (h + 1) * rows) for h in range(heads)]

    def place(chip, side):
        return (side * (1 - 2 * odd) - 2 * chip) * rows

    def needed(chip, side):
        return (place(chip, side) + rows > earliest) & (place(chip, side) <= 0)

    if plan["first"]:
        for h in range(heads):
            g = ref["g"][:, cols[h]]
            ref["qs"][lanes[h], :] = ref["q"][:, cols[h]]
            ref["gs"][lanes[h], :] = g
            ref["gt"][:, lanes[h]] = g.T
        ref["m"][...] = jnp.full_like(ref["m"], MASKED)
        ref["l"][...] = jnp.zeros_like(ref["l"])
        ref["acc"][...] = jnp.zeros_like(ref["acc"])

    def load(chip, side):
        block, i = ref["kv", chip, side], blocks.index((chip, side))
        if (chip, side) in fwd:
            ref["vt"][i] = block[:, dim:].T
        if (chip, side) in bwd:
            ref["kt"][i] = block[:, :dim].T

    for block in blocks:
        pl.when(needed(*block))(functools.partial(load, *block))

    def fwd_block(chip, side):
        i = blocks.index((chip, side))
        key_pos = lax.broadcasted_iota(jnp.int32, (rows, rows), 0) + place(chip, side)
        allowed = (key_pos >= start) & (
            key_pos <= lax.broadcasted_iota(jnp.int32, (rows, rows), 1)
        )
        ref["bias"][...] = jnp.where(allowed, 0.0, MASKED)
        block_k, value_t = ref["kv", chip, side][:, :dim], ref["vt"][i]
        bias = jnp.concatenate([ref["bias"][...]] * 8, axis=1)
        for h in range(0, heads, 8):
            wide = slice(h * rows, (h + 8) * rows)
            s = dot_nt(block_k, ref["qs"][wide, :]) + bias
            old = ref["m"][:, wide]
            m = jnp.maximum(old, jnp.max(s, axis=0, keepdims=True))
            alpha = jnp.exp2((old - m) * fold)
            p = jnp.exp2((s - m) * fold)
            pb = p.astype(bf16)
            ref["probs", chip, side][:, wide] = pb
            total = jnp.sum(p, axis=0, keepdims=True)
            ref["l"][:, wide] = ref["l"][:, wide] * alpha + total
            ref["acc"][:, wide] = ref["acc"][:, wide] * alpha + dot_nn(value_t, pb)
            ref["m"][:, wide] = m
            ref["then", chip, side][:, wide] = m

    def finish():
        for h in range(heads):
            inverse = 1.0 / ref["l"][:, lanes[h]]
            o_t = (ref["acc"][:, lanes[h]] * inverse).astype(bf16)
            ref["out_t"][:, lanes[h]] = o_t
            terms = o_t.astype(f32) * ref["gt"][:, lanes[h]].astype(f32)
            ref["delta"][:, lanes[h]] = jnp.sum(terms, axis=0, keepdims=True)
            ref["l"][:, lanes[h]] = inverse
        ref["dq"][...] = jnp.zeros_like(ref["dq"])

    def bwd_block(chip, side):
        i = blocks.index((chip, side))
        block_v, key_t = ref["kv", chip, side][:, dim:], ref["kt"][i]
        dk = dv = None
        for h in range(0, heads, 8):
            wide = slice(h * rows, (h + 8) * rows)
            dprob = dot_nn(block_v, ref["gt"][:, wide])
            m_then = ref["then", chip, side][:, wide]
            c = jnp.exp2((m_then - ref["m"][:, wide]) * fold) * ref["l"][:, wide]
            p = ref["probs", chip, side][:, wide].astype(f32) * c
            d = (p * (dprob - ref["delta"][:, wide])).astype(bf16)
            p = p.astype(bf16)
            ref["dq"][:, wide] += dot_nn(key_t, d)
            dk_part = dot_nn(d, ref["qs"][wide, :])
            dv_part = dot_nn(p, ref["gs"][wide, :])
            dk = dk_part if dk is None else dk + dk_part
            dv = dv_part if dv is None else dv + dv_part
        part = ref["part", chip, side]
        part[:, :dim] = (dk * scale).astype(part.dtype)
        part[:, dim:] = dv.astype(part.dtype)

    for block in fwd:
        pl.when(needed(*block))(functools.partial(fwd_block, *block))
    if plan["final"]:
        finish()
    for block in bwd:
        part = ref["part", *block]
        pl.when(needed(*block))(functools.partial(bwd_block, *block))

        @pl.when(jnp.logical_not(needed(*block)))
        def _():
            part[...] = jnp.zeros_like(part)

    if plan["last"]:
        for h in range(heads):
            ref["out"][:, cols[h]] = ref["out_t"][:, lanes[h]].T
            ref["grad_q"][:, cols[h]] = (ref["dq"][:, lanes[h]] * scale).astype(bf16).T


def stage(state, fwd=(), bwd=(), final=False, last=False):
    rows, dim2 = state["kv", 0, 0].shape
    dim = dim2 // 2
    heads = state["q"].shape[1] // dim
    width = heads * rows
    bf16, f32 = jnp.bfloat16, jnp.float32
    shape = jax.ShapeDtypeStruct
    blocks = sorted(set(fwd) | set(bwd))
    first = (0, 0) in fwd
    row, tall = shape((1, width), f32), shape((dim, width), f32)
    ins, outs, both = ["meta"], {}, []
    if first:
        ins += ["q", "g"]
        outs.update(qs=shape((width, dim), bf16), gs=shape((width, dim), bf16), gt=shape((dim, width), bf16))
    else:
        ins.append("qs")
        if final or bwd:
            ins.append("gt")
        if bwd:
            ins.append("gs")
    ins += [("kv", *b) for b in blocks]
    if fwd:
        for b in fwd:
            outs["probs", *b] = shape((rows, width), bf16)
            outs["then", *b] = row
        outs.update(m=row, l=row, acc=tall)
        if not first:
            both += ["m", "l", "acc"]
    if final:
        outs.update(out_t=shape((dim, width), bf16), delta=row, dq=tall)
    if bwd:
        for b in bwd:
            if b not in fwd:
                ins += [("probs", *b), ("then", *b)]
            outs["part", *b] = shape((rows, dim2), bf16 if b[1] else f32)
        if not final:
            ins += ["m", "l", "delta"]
            outs["dq"] = tall
            both.append("dq")
    if last:
        ins.append("out_t")
        outs["out"] = outs["grad_q"] = shape((rows, heads * dim), bf16)
    out_names = list(outs)
    scratch = {}
    if fwd:
        scratch["vt"] = pltpu.VMEM((len(blocks), dim, rows), bf16)
        scratch["bias"] = pltpu.VMEM((rows, rows), f32)
    if bwd:
        scratch["kt"] = pltpu.VMEM((len(blocks), dim, rows), bf16)
    names = ins + [("in", b) for b in both] + out_names + list(scratch)
    plan = dict(
        rows=rows, dim=dim, heads=heads, fwd=fwd, bwd=bwd, first=first, final=final, last=last, names=names
    )
    products = 2 * len(fwd) + 4 * len(bwd)
    results = pl.pallas_call(
        functools.partial(stage_body, plan),
        in_specs=[HERE] * (len(ins) + len(both)),
        out_specs=[HERE] * len(out_names),
        out_shape=[outs[n] for n in out_names],
        scratch_shapes=list(scratch.values()),
        input_output_aliases={len(ins) + i: out_names.index(b) for i, b in enumerate(both)},
        compiler_params=pltpu.CompilerParams(vmem_limit_bytes=VMEM_LIMIT),
        cost_estimate=pl.CostEstimate(
            flops=2 * products * rows * width * dim, bytes_accessed=2**20, transcendentals=0
        ),
    )(*[state[n] for n in ins + both])
    state.update(zip(out_names, results))


def after(x, *others):
    return lax.optimization_barrier((x, *others))[0]


def pairs(*chips):
    return [(chip, side) for chip in chips for side in (0, 1)]


def on_device(queries, keys, values, out_grad, doc_lengths):
    rows, dim = keys.shape
    f32, bf16 = jnp.float32, jnp.bfloat16
    own, meta = prepare(keys, values, doc_lengths[None, :])
    state = {"meta": meta, "q": queries, "g": out_grad, ("kv", 0, 0): own}

    def arrive(chip, block):
        state["kv", chip, 0] = block
        state["kv", chip, 1] = swapped(block)

    back2 = shifted(own, 4)
    back1 = shifted(own, 2)
    arrive(0, own)
    stage(state, fwd=pairs(0))
    back2 = after(back2, state["l"])
    back4 = shifted(back2, 4)
    back3 = shifted(back2, 2)
    arrive(2, back2)
    arrive(1, after(back1, state["l"]))
    stage(state, fwd=pairs(1, 2))
    arrive(3, after(back3, state["l"]))
    arrive(4, after(back4, state["l"]))
    stage(state, fwd=pairs(3, 4), bwd=pairs(4), final=True)

    def summed(chip, *others):
        other = swapped(after(state["part", chip, 1], *others))
        return state["part", chip, 0] + other.astype(f32)

    t4 = summed(4).astype(bf16)
    r4 = shifted(t4, -4)
    state["dq"] = after(state["dq"], t4)
    stage(state, bwd=pairs(1, 3) + [(0, 1)])
    other = swapped(after(state["part", 0, 1], r4))
    t3 = summed(3, r4).astype(bf16)
    t1 = summed(1, r4).astype(bf16)
    r3 = shifted(t3, -2)
    r1 = shifted(t1, -2)
    state["dq"] = after(state["dq"], t1, t3)
    stage(state, bwd=pairs(2))
    t2 = (summed(2, r1, r3) + r4.astype(f32) + r3.astype(f32)).astype(bf16)
    r2 = shifted(t2, -4)
    state["dq"] = after(state["dq"], t2)
    stage(state, bwd=[(0, 0)], last=True)
    total = state["part", 0, 0] + other.astype(f32) + r1.astype(f32) + r2.astype(f32)
    return (state["out"], state["grad_q"], total[:, :dim].astype(bf16), total[:, dim:].astype(bf16))


def solution(mesh):
    rows = P(AXES, None)
    return jax.shard_map(
        on_device,
        mesh=mesh,
        in_specs=(rows, rows, rows, rows, P()),
        out_specs=(rows, rows, rows, rows),
        check_vma=False,
    )
```

time: 310 us -> 87.1 us (0.28)
  the two profiles are of different devices: /device:TPU:24 before, /device:TPU:238 now
where the time goes in v2:
time: 87.1 us; the launch traced here: 86.7 us
  starting transfers between devices  29.8 us (34%)
  waiting for transfers between devices  29.7 us (34%)
  Pallas kernels  21.1 us (24%)
  local copies, waits for them, and re-layouts  5.07 us (6%)
    ppermute x8, starting transfers between devices, shifted(): return lax.ppermute(shard, AXES, pairs)  27.3 us
    ppermute x8, waiting for transfers between devices, shifted(): return lax.ppermute(shard, AXES, pairs)  26 us
    pallas_call x6, Pallas kernels, stage(): pl.pallas_call(functools.partial(stage_body, plan), in_specs=[HERE] * (le...  21 us
    unnamed x10, local copies, waits for them, and re-layouts  4.4 us
    ppermute x10, waiting for transfers between devices, swapped(): return lax.ppermute(shard, AXES, [(i, i ^ 1) for i in range(peers)])  3.74 us
    ppermute x10, starting transfers between devices, swapped(): return lax.ppermute(shard, AXES, [(i, i ^ 1) for i in range(peers)])  2.45 us
  transfers between devices with their start and end apart: 18, of which 11 were waited for; matrix products, arithmetic and copies ran while one was open for 0% of the time, Pallas kernels for 20%

profile of v2, /device:TPU:238, one launch (start us, length us, event | category | flops | bytes accessed | tf_op | source)
XLA Modules:
  0.0 86.7 jit_solution(15546826673999837530)
XLA Ops:
  0.6 0.6 copy-done.2
  1.3 0.8 copy-done
  2.1 0.8 copy-done.1
  3.0 0.1 shard_map.84
  3.1 0.1 collective-permute-start
  3.2 1.9 %collective-permute-start.3 = (bf16[256,256]{1,0:T(8,128)(2,1)S(1)}, bf16[256,256]{1,0:T(8,128)(2,1)S(1)}, u32[]{:S(2)}, u32[]{:S(2)}) collective-permute-start(bf16[256,256]{1,0:T(8,128)(2,1)S(1)} %get-tuple-element.62.refs_3_.refs_4_), channel_id=1, source_target_pairs={{0,2},{1,3},{2,4},{3,5},{4,6},{5,7},{6,8},{7,9},{8,10},{9,11},{10,... | collective-permute-start | bytes 393224 | tf_op jit(solution)/shard_map/ppermute | solution.py:20
  5.1 3.5 %collective-permute-start.1 = (bf16[256,256]{1,0:T(8,128)(2,1)S(1)}, bf16[256,256]{1,0:T(8,128)(2,1)S(1)}, u32[]{:S(2)}, u32[]{:S(2)}) collective-permute-start(bf16[256,256]{1,0:T(8,128)(2,1)S(1)} %get-tuple-element.62.refs_3_.refs_4_), channel_id=1, source_target_pairs={{0,4},{1,5},{2,6},{3,7},{4,8},{5,9},{6,10},{7,11},{8,12},{9,13},{1... | collective-permute-start | bytes 393224 | tf_op jit(solution)/shard_map/ppermute | solution.py:20
  8.6 0.0 collective-permute-done.refs_4_
  8.6 0.0 copy-start.3
  8.6 1.0 %copy-done.3 = bf16[256,1024]{1,0:T(8,128)(2,1)S(1)} copy-done((bf16[256,1024]{1,0:T(8,128)(2,1)S(1)}, bf16[256,1024]{1,0:T(8,128)(2,1)}, u32[]{:S(2)}) %copy-start.3) | copy-done | bytes 524312
  9.6 1.0 %copy-done.4 = bf16[256,1024]{1,0:T(8,128)(2,1)S(1)} copy-done((bf16[256,1024]{1,0:T(8,128)(2,1)S(1)}, bf16[256,1024]{1,0:T(8,128)(2,1)}, u32[]{:S(2)}) %copy-start.4) | copy-done | bytes 524312
  10.7 1.7 %shard_map.85 = (bf16[2048,128]{1,0:T(8,128)(2,1)S(1)}, bf16[2048,128]{1,0:T(8,128)(2,1)S(1)}, bf16[128,2048]{1,0:T(8,128)(2,1)S(1)}, bf16[256,2048]{1,0:T(8,128...) custom-call(s32[2,256]{1,0:T(2,128)S(1)} %get-tuple-element.61.refs_, ...), custom_call_target="tpu_custom_call" | custom-call | flops 536870912 | bytes 1048576 | tf_op jit(solution)/shard_map/pallas_call | solution.py:235
  12.4 0.0 collective-permute-done.3.refs_2_.refs_5_
  12.4 4.3 %collective-permute-done.1.refs_4_ = bf16[256,256]{1,0:T(8,128)(2,1)S(1)} collective-permute-done((bf16[256,256]{1,0:T(8,128)(2,1)S(1)}, bf16[256,256]{1,0:T(8,128)(2,1)S(1)}, u32[]{:S(2)}, u32[]{:S(2)}) %collective-permute-start.1) | collective-permute-done | bytes 131104 | tf_op jit(solution)/shard_map/ppermute | solution.py:20
  16.8 0.0 collective-permute-start.5
  16.8 0.5 collective-permute-start.4
  17.3 7.2 %collective-permute-start.7 = (bf16[256,256]{1,0:T(8,128)(2,1)S(1)}, bf16[256,256]{1,0:T(8,128)(2,1)S(1)}, u32[]{:S(2)}, u32[]{:S(2)}) collective-permute-start(bf16[256,256]{1,0:T(8,128)(2,1)S(1)} %collective-permute-done.1.refs_4_), channel_id=1, source_target_pairs={{0,4},{1,5},{2,6},{3,7},{4,8},{5,9},{6,10},{7,11},{8,12},{9,13},{1... | collective-permute-start | bytes 393224 | tf_op jit(solution)/shard_map/ppermute | solution.py:20
  24.5 1.9 %collective-permute-start.2 = (bf16[256,256]{1,0:T(8,128)(2,1)S(1)}, bf16[256,256]{1,0:T(8,128)(2,1)S(1)}, u32[]{:S(2)}, u32[]{:S(2)}) collective-permute-start(bf16[256,256]{1,0:T(8,128)(2,1)S(1)} %collective-permute-done.1.refs_4_), channel_id=1, source_target_pairs={{0,2},{1,3},{2,4},{3,5},{4,6},{5,7},{6,8},{7,9},{8,10},{9,11},{10,... | collective-permute-start | bytes 393224 | tf_op jit(solution)/shard_map/ppermute | solution.py:20
  26.5 0.0 collective-permute-done.4.refs_3_.refs_6_
  26.5 5.6 %shard_map.86 = (bf16[256,2048]{1,0:T(8,128)(2,1)S(1)}, f32[1,2048]{1,0:T(1,128)S(1)}, bf16[256,2048]{1,0:T(8,128)(2,1)S(1)}, f32[1,2048]{1,0:T(1,128)S(1)}, bf1...) custom-call(s32[2,256]{1,0:T(2,128)S(1)} %get-tuple-element.61.refs_, ...), custom_call_target="tpu_custom_call", output_to_operand_aliasing={{8}: (6, {}), {9}: (7, {}), {10}: (8, {})} | custom-call | flops 1073741824 | bytes 1048576 | tf_op jit(solution)/shard_map/pallas_call | solution.py:235
  32.1 0.0 collective-permute-done.7.refs_6_
  32.1 0.6 collective-permute-done.2.refs_4_.refs_7_
  32.7 0.0 collective-permute-start.6
  32.7 0.5 collective-permute-start.8
  33.2 0.8 collective-permute-done.6.refs_5_.refs_8_
  34.1 0.2 collective-permute-done.8.refs_7_
  34.3 3.4 %shard_map.87 = (bf16[256,2048]{1,0:T(8,128)(2,1)S(1)}, f32[1,2048]{1,0:T(1,128)S(1)}, bf16[256,2048]{1,0:T(8,128)(2,1)S(1)}, f32[1,2048]{1,0:T(1,128)S(1)}, bf1...) custom-call(s32[2,256]{1,0:T(2,128)S(1)} %get-tuple-element.61.refs_, ...), custom_call_target="tpu_custom_call", output_to_operand_aliasing={{8}: (8, {}), {9}: (9, {}), {10}: (10, {})} | custom-call | flops 2147483648 | bytes 1048576 | tf_op jit(solution)/shard_map/pallas_call | solution.py:235
  37.7 0.3 collective-permute-start.9
  38.0 1.0 %collective-permute-done.9 = bf16[256,256]{1,0:T(8,128)(2,1)S(1)} collective-permute-done((bf16[256,256]{1,0:T(8,128)(2,1)S(1)}, bf16[256,256]{1,0:T(8,128)(2,1)S(1)}, u32[]{:S(2)}, u32[]{:S(2)}) %collective-permute-start.9) | collective-permute-done | bytes 131104 | tf_op jit(solution)/shard_map/ppermute | solution.py:25
  39.1 1.9 %collective-permute-start.10 = (bf16[256,256]{1,0:T(8,128)(2,1)S(1)}, bf16[256,256]{1,0:T(8,128)(2,1)S(1)}, u32[]{:S(2)}, u32[]{:S(2)}) collective-permute-start(bf16[256,256]{1,0:T(8,128)(2,1)S(1)} %add_convert_fusion.4), channel_id=1, source_target_pairs={{4,0},{5,1},{6,2},{7,3},{8,4},{9,5},{10,6},{11,7},{12,8},{13,9},{1... | collective-permute-start | bytes 393224 | tf_op jit(solution)/shard_map/ppermute | solution.py:20
  41.0 4.5 %shard_map.88 = (f32[256,256]{1,0:T(8,128)S(1)}, bf16[256,256]{1,0:T(8,128)(2,1)S(1)}, f32[256,256]{1,0:T(8,128)S(1)}, bf16[256,256]{1,0:T(8,128)(2,1)S(1)}, bf1...) custom-call(s32[2,256]{1,0:T(2,128)S(1)} %get-tuple-element.61.refs_0_, ...), custom_call_target="tpu_custom_call", output_to_operand_aliasing={{5}: (22, {})} | custom-call | flops 2684354560 | bytes 1048576 | tf_op jit(solution)/shard_map/pallas_call | solution.py:235
  45.5 6.3 %collective-permute-done.10 = bf16[256,256]{1,0:T(8,128)(2,1)S(1)} collective-permute-done((bf16[256,256]{1,0:T(8,128)(2,1)S(1)}, bf16[256,256]{1,0:T(8,128)(2,1)S(1)}, u32[]{:S(2)}, u32[]{:S(2)}) %collective-permute-start.10) | collective-permute-done | bytes 131104 | tf_op jit(solution)/shard_map/ppermute | solution.py:20
  51.8 0.5 collective-permute-start.12
  52.3 0.8 collective-permute-done.11
  53.2 7.0 %collective-permute-start.13 = (bf16[256,256]{1,0:T(8,128)(2,1)S(1)}, bf16[256,256]{1,0:T(8,128)(2,1)S(1)}, u32[]{:S(2)}, u32[]{:S(2)}) collective-permute-start(bf16[256,256]{1,0:T(8,128)(2,1)S(1)} %add_convert_fusion.3), channel_id=1, source_target_pairs={{2,0},{3,1},{4,2},{5,3},{6,4},{7,5},{8,6},{9,7},{10,8},{11,9},{12,... | collective-permute-start | bytes 393224 | tf_op jit(solution)/shard_map/ppermute | solution.py:20
  60.2 1.9 %collective-permute-start.14 = (bf16[256,256]{1,0:T(8,128)(2,1)S(1)}, bf16[256,256]{1,0:T(8,128)(2,1)S(1)}, u32[]{:S(2)}, u32[]{:S(2)}) collective-permute-start(bf16[256,256]{1,0:T(8,128)(2,1)S(1)} %add_convert_fusion.2), channel_id=1, source_target_pairs={{2,0},{3,1},{4,2},{5,3},{6,4},{7,5},{8,6},{9,7},{10,8},{11,9},{12,... | collective-permute-start | bytes 393224 | tf_op jit(solution)/shard_map/ppermute | solution.py:20
  62.2 2.9 %shard_map.89 = (f32[256,256]{1,0:T(8,128)S(1)}, bf16[256,256]{1,0:T(8,128)(2,1)S(1)}, f32[128,2048]{1,0:T(8,128)S(1)}) custom-call(s32[2,256]{1,0:T(2,128)S(1)} %get-tuple-element.61.refs_0_, bf16[2048,128]{1,0:T(8,128)(2,1)S(1)} %get-tuple-element.63.refs_1_, bf16[128,2048]{1,0:T(8,128)(2,1)S(1)} %get-tuple-element.64.refs_2_, ...), custom_call_target="tpu_custom_call", output_to_operand_aliasing={{2}: (13, {})} | custom-call | flops 1073741824 | bytes 1048576 | tf_op jit(solution)/shard_map/pallas_call | solution.py:235
  65.1 0.1 collective-permute-done.13
  65.2 6.5 %collective-permute-done.14 = bf16[256,256]{1,0:T(8,128)(2,1)S(1)} collective-permute-done((bf16[256,256]{1,0:T(8,128)(2,1)S(1)}, bf16[256,256]{1,0:T(8,128)(2,1)S(1)}, u32[]{:S(2)}, u32[]{:S(2)}) %collective-permute-start.14) | collective-permute-done | bytes 131104 | tf_op jit(solution)/shard_map/ppermute | solution.py:20
  71.6 0.0 collective-permute-start.15
  71.6 0.5 collective-permute-start.16
  72.1 0.8 collective-permute-done.15
  73.0 0.1 add_convert_fusion.1
  73.0 1.9 %collective-permute-start.17 = (bf16[256,256]{1,0:T(8,128)(2,1)S(1)}, bf16[256,256]{1,0:T(8,128)(2,1)S(1)}, u32[]{:S(2)}, u32[]{:S(2)}) collective-permute-start(bf16[256,256]{1,0:T(8,128)(2,1)S(1)} %add_convert_fusion.1), channel_id=1, source_target_pairs={{4,0},{5,1},{6,2},{7,3},{8,4},{9,5},{10,6},{11,7},{12,8},{13,9},{1... | collective-permute-start | bytes 393224 | tf_op jit(solution)/shard_map/ppermute | solution.py:20
  75.0 2.8 %shard_map.90 = (f32[256,256]{1,0:T(8,128)S(1)}, f32[128,2048]{1,0:T(8,128)S(1)}, bf16[256,1024]{1,0:T(8,128)(2,1)}, bf16[256,1024]{1,0:T(8,128)(2,1)}) custom-call(s32[2,256]{1,0:T(2,128)S(1)} %get-tuple-element.61.refs_0_, bf16[2048,128]{1,0:T(8,128)(2,1)S(1)} %get-tuple-element.63.refs_1_, ...), custom_call_target="tpu_custom_call", output_to_operand_aliasing={{1}: (11, {})} | custom-call | flops 536870912 | bytes 1048576 | tf_op jit(solution)/shard_map/pallas_call | solution.py:235
  77.8 8.2 %collective-permute-done.17 = bf16[256,256]{1,0:T(8,128)(2,1)S(1)} collective-permute-done((bf16[256,256]{1,0:T(8,128)(2,1)S(1)}, bf16[256,256]{1,0:T(8,128)(2,1)S(1)}, u32[]{:S(2)}, u32[]{:S(2)}) %collective-permute-start.17) | collective-permute-done | bytes 131104 | tf_op jit(solution)/shard_map/ppermute | solution.py:20
  85.9 0.1 add_convert_fusion
  86.0 0.7 fusion
  (11 shorter events, 0.1 us)
Async XLA Ops:
  0.6 0.7 copy-start.2
  1.3 0.8 copy-start
  2.1 0.8 copy-start.1
  3.1 5.5 %collective-permute-start = (bf16[256,256]{1,0:T(8,128)(2,1)S(1)}, bf16[256,256]{1,0:T(8,128)(2,1)S(1)}, u32[]{:S(2)}, u32[]{:S(2)}) collective-permute-start(bf16[256,256]{1,0:T(8,128)(2,1)S(1)} %get-tuple-element.62.refs_3_.refs_4_), channel_id=1, source_target_pairs={{0,1},{1,0},{2,3},{3,2},{4,5},{5,4},{6,7},{7,6},{8,9},{9,8},{10,11... | collective-permute-start | bytes 393224 | tf_op jit(solution)/shard_map/ppermute | solution.py:25
  3.2 9.2 %collective-permute-start.3 = (bf16[256,256]{1,0:T(8,128)(2,1)S(1)}, bf16[256,256]{1,0:T(8,128)(2,1)S(1)}, u32[]{:S(2)}, u32[]{:S(2)}) collective-permute-start(bf16[256,256]{1,0:T(8,128)(2,1)S(1)} %get-tuple-element.62.refs_3_.refs_4_), channel_id=1, source_target_pairs={{0,2},{1,3},{2,4},{3,5},{4,6},{5,7},{6,8},{7,9},{8,10},{9,11},{10,... | collective-permute-start | bytes 393224 | tf_op jit(solution)/shard_map/ppermute | solution.py:20
  5.1 11.6 %collective-permute-start.1 = (bf16[256,256]{1,0:T(8,128)(2,1)S(1)}, bf16[256,256]{1,0:T(8,128)(2,1)S(1)}, u32[]{:S(2)}, u32[]{:S(2)}) collective-permute-start(bf16[256,256]{1,0:T(8,128)(2,1)S(1)} %get-tuple-element.62.refs_3_.refs_4_), channel_id=1, source_target_pairs={{0,4},{1,5},{2,6},{3,7},{4,8},{5,9},{6,10},{7,11},{8,12},{9,13},{1... | collective-permute-start | bytes 393224 | tf_op jit(solution)/shard_map/ppermute | solution.py:20
  8.6 1.0 %copy-start.3 = (bf16[256,1024]{1,0:T(8,128)(2,1)S(1)}, bf16[256,1024]{1,0:T(8,128)(2,1)}, u32[]{:S(2)}) copy-start(bf16[256,1024]{1,0:T(8,128)(2,1)} %refs_1_.1) | copy-start | bytes 1572868
  9.6 1.0 %copy-start.4 = (bf16[256,1024]{1,0:T(8,128)(2,1)S(1)}, bf16[256,1024]{1,0:T(8,128)(2,1)}, u32[]{:S(2)}) copy-start(bf16[256,1024]{1,0:T(8,128)(2,1)} %refs_2_.1) | copy-start | bytes 1572868
  16.8 9.7 %collective-permute-start.5 = (bf16[256,256]{1,0:T(8,128)(2,1)S(1)}, bf16[256,256]{1,0:T(8,128)(2,1)S(1)}, u32[]{:S(2)}, u32[]{:S(2)}) collective-permute-start(bf16[256,256]{1,0:T(8,128)(2,1)S(1)} %collective-permute-done.1.refs_4_), channel_id=1, source_target_pairs={{0,1},{1,0},{2,3},{3,2},{4,5},{5,4},{6,7},{7,6},{8,9},{9,8},{10,11... | collective-permute-start | bytes 393224 | tf_op jit(solution)/shard_map/ppermute | solution.py:25
  16.8 9.7 %collective-permute-start.4 = (bf16[256,256]{1,0:T(8,128)(2,1)S(1)}, bf16[256,256]{1,0:T(8,128)(2,1)S(1)}, u32[]{:S(2)}, u32[]{:S(2)}) collective-permute-start(bf16[256,256]{1,0:T(8,128)(2,1)S(1)} %collective-permute-done.3.refs_2_.refs_5_), channel_id=1, source_target_pairs={{0,1},{1,0},{2,3},{3,2},{4,5},{5,4},{6,7},{7,6},{8,9},{9,8},{10,11... | collective-permute-start | bytes 393224 | tf_op jit(solution)/shard_map/ppermute | solution.py:25
  17.3 14.8 %collective-permute-start.7 = (bf16[256,256]{1,0:T(8,128)(2,1)S(1)}, bf16[256,256]{1,0:T(8,128)(2,1)S(1)}, u32[]{:S(2)}, u32[]{:S(2)}) collective-permute-start(bf16[256,256]{1,0:T(8,128)(2,1)S(1)} %collective-permute-done.1.refs_4_), channel_id=1, source_target_pairs={{0,4},{1,5},{2,6},{3,7},{4,8},{5,9},{6,10},{7,11},{8,12},{9,13},{1... | collective-permute-start | bytes 393224 | tf_op jit(solution)/shard_map/ppermute | solution.py:20
  24.5 8.2 %collective-permute-start.2 = (bf16[256,256]{1,0:T(8,128)(2,1)S(1)}, bf16[256,256]{1,0:T(8,128)(2,1)S(1)}, u32[]{:S(2)}, u32[]{:S(2)}) collective-permute-start(bf16[256,256]{1,0:T(8,128)(2,1)S(1)} %collective-permute-done.1.refs_4_), channel_id=1, source_target_pairs={{0,2},{1,3},{2,4},{3,5},{4,6},{5,7},{6,8},{7,9},{8,10},{9,11},{10,... | collective-permute-start | bytes 393224 | tf_op jit(solution)/shard_map/ppermute | solution.py:20
  32.7 1.3 %collective-permute-start.6 = (bf16[256,256]{1,0:T(8,128)(2,1)S(1)}, bf16[256,256]{1,0:T(8,128)(2,1)S(1)}, u32[]{:S(2)}, u32[]{:S(2)}) collective-permute-start(bf16[256,256]{1,0:T(8,128)(2,1)S(1)} %collective-permute-done.2.refs_4_.refs_7_), channel_id=1, source_target_pairs={{0,1},{1,0},{2,3},{3,2},{4,5},{5,4},{6,7},{7,6},{8,9},{9,8},{10,11... | collective-permute-start | bytes 393224 | tf_op jit(solution)/shard_map/ppermute | solution.py:25
  32.7 1.5 %collective-permute-start.8 = (bf16[256,256]{1,0:T(8,128)(2,1)S(1)}, bf16[256,256]{1,0:T(8,128)(2,1)S(1)}, u32[]{:S(2)}, u32[]{:S(2)}) collective-permute-start(bf16[256,256]{1,0:T(8,128)(2,1)S(1)} %collective-permute-done.7.refs_6_), channel_id=1, source_target_pairs={{0,1},{1,0},{2,3},{3,2},{4,5},{5,4},{6,7},{7,6},{8,9},{9,8},{10,11... | collective-permute-start | bytes 393224 | tf_op jit(solution)/shard_map/ppermute | solution.py:25
  37.7 1.3 %collective-permute-start.9 = (bf16[256,256]{1,0:T(8,128)(2,1)S(1)}, bf16[256,256]{1,0:T(8,128)(2,1)S(1)}, u32[]{:S(2)}, u32[]{:S(2)}) collective-permute-start(bf16[256,256]{1,0:T(8,128)(2,1)S(1)} %get-tuple-element.98), channel_id=1, source_target_pairs={{0,1},{1,0},{2,3},{3,2},{4,5},{5,4},{6,7},{7,6},{8,9},{9,8},{10,11... | collective-permute-start | bytes 393224 | tf_op jit(solution)/shard_map/ppermute | solution.py:25
  39.1 12.7 %collective-permute-start.10 = (bf16[256,256]{1,0:T(8,128)(2,1)S(1)}, bf16[256,256]{1,0:T(8,128)(2,1)S(1)}, u32[]{:S(2)}, u32[]{:S(2)}) collective-permute-start(bf16[256,256]{1,0:T(8,128)(2,1)S(1)} %add_convert_fusion.4), channel_id=1, source_target_pairs={{4,0},{5,1},{6,2},{7,3},{8,4},{9,5},{10,6},{11,7},{12,8},{13,9},{1... | collective-permute-start | bytes 393224 | tf_op jit(solution)/shard_map/ppermute | solution.py:20
  51.8 1.3 %collective-permute-start.11 = (bf16[256,256]{1,0:T(8,128)(2,1)S(1)}, bf16[256,256]{1,0:T(8,128)(2,1)S(1)}, u32[]{:S(2)}, u32[]{:S(2)}) collective-permute-start(bf16[256,256]{1,0:T(8,128)(2,1)S(1)} %get-tuple-element.103), channel_id=1, source_target_pairs={{0,1},{1,0},{2,3},{3,2},{4,5},{5,4},{6,7},{7,6},{8,9},{9,8},{10,11... | collective-permute-start | bytes 393224 | tf_op jit(solution)/shard_map/ppermute | solution.py:25
  51.8 8.4 %collective-permute-start.12 = (bf16[256,256]{1,0:T(8,128)(2,1)S(1)}, bf16[256,256]{1,0:T(8,128)(2,1)S(1)}, u32[]{:S(2)}, u32[]{:S(2)}) collective-permute-start(bf16[256,256]{1,0:T(8,128)(2,1)S(1)} %get-tuple-element.106), channel_id=1, source_target_pairs={{0,1},{1,0},{2,3},{3,2},{4,5},{5,4},{6,7},{7,6},{8,9},{9,8},{10,11... | collective-permute-start | bytes 393224 | tf_op jit(solution)/shard_map/ppermute | solution.py:25
  53.2 12.0 %collective-permute-start.13 = (bf16[256,256]{1,0:T(8,128)(2,1)S(1)}, bf16[256,256]{1,0:T(8,128)(2,1)S(1)}, u32[]{:S(2)}, u32[]{:S(2)}) collective-permute-start(bf16[256,256]{1,0:T(8,128)(2,1)S(1)} %add_convert_fusion.3), channel_id=1, source_target_pairs={{2,0},{3,1},{4,2},{5,3},{6,4},{7,5},{8,6},{9,7},{10,8},{11,9},{12,... | collective-permute-start | bytes 393224 | tf_op jit(solution)/shard_map/ppermute | solution.py:20
  60.2 11.4 %collective-permute-start.14 = (bf16[256,256]{1,0:T(8,128)(2,1)S(1)}, bf16[256,256]{1,0:T(8,128)(2,1)S(1)}, u32[]{:S(2)}, u32[]{:S(2)}) collective-permute-start(bf16[256,256]{1,0:T(8,128)(2,1)S(1)} %add_convert_fusion.2), channel_id=1, source_target_pairs={{2,0},{3,1},{4,2},{5,3},{6,4},{7,5},{8,6},{9,7},{10,8},{11,9},{12,... | collective-permute-start | bytes 393224 | tf_op jit(solution)/shard_map/ppermute | solution.py:20
  71.6 1.3 %collective-permute-start.15 = (bf16[256,256]{1,0:T(8,128)(2,1)S(1)}, bf16[256,256]{1,0:T(8,128)(2,1)S(1)}, u32[]{:S(2)}, u32[]{:S(2)}) collective-permute-start(bf16[256,256]{1,0:T(8,128)(2,1)S(1)} %get-tuple-element.111), channel_id=1, source_target_pairs={{0,1},{1,0},{2,3},{3,2},{4,5},{5,4},{6,7},{7,6},{8,9},{9,8},{10,11... | collective-permute-start | bytes 393224 | tf_op jit(solution)/shard_map/ppermute | solution.py:25
  71.6 6.1 %collective-permute-start.16 = (bf16[256,256]{1,0:T(8,128)(2,1)S(1)}, bf16[256,256]{1,0:T(8,128)(2,1)S(1)}, u32[]{:S(2)}, u32[]{:S(2)}) collective-permute-start(bf16[256,256]{1,0:T(8,128)(2,1)S(1)} %get-tuple-element.117), channel_id=1, source_target_pairs={{0,1},{1,0},{2,3},{3,2},{4,5},{5,4},{6,7},{7,6},{8,9},{9,8},{10,11... | collective-permute-start | bytes 393224 | tf_op jit(solution)/shard_map/ppermute | solution.py:25
  73.0 12.9 %collective-permute-start.17 = (bf16[256,256]{1,0:T(8,128)(2,1)S(1)}, bf16[256,256]{1,0:T(8,128)(2,1)S(1)}, u32[]{:S(2)}, u32[]{:S(2)}) collective-permute-start(bf16[256,256]{1,0:T(8,128)(2,1)S(1)} %add_convert_fusion.1), channel_id=1, source_target_pairs={{4,0},{5,1},{6,2},{7,3},{8,4},{9,5},{10,6},{11,7},{12,8},{13,9},{1... | collective-permute-start | bytes 393224 | tf_op jit(solution)/shard_map/ppermute | solution.py:20

commit v3 on v2

--- a/solution.py
+++ b/solution.py
@@ -33,35 +33,65 @@
     return lax.dot_general(a, b, (((1,), (0,)), ((), ())), preferred_element_type=jnp.float32)
 
 
-def prep_body(keys, values, lengths, own, meta):
+def prep_body(keys, values, lengths, own, meta, held, sems):
     rows, dim = keys.shape
     docs = lengths.shape[1]
-    own[:, :dim] = keys[...]
-    own[:, dim:] = values[...]
+    copies = [
+        pltpu.make_async_copy(keys, own.at[:, pl.ds(0, dim)], sems.at[0]),
+        pltpu.make_async_copy(values, own.at[:, pl.ds(dim, dim)], sems.at[1]),
+        pltpu.make_async_copy(lengths, held, sems.at[2]),
+    ]
+    for copy in copies:
+        copy.start()
+    copies[2].wait()
     device = lax.axis_index(AXES[0]) * lax.axis_size(AXES[1]) + lax.axis_index(AXES[1])
     here = device * rows
     later = lax.broadcasted_iota(jnp.int32, (docs, docs), 0)
     earlier = lax.broadcasted_iota(jnp.int32, (docs, docs), 1)
-    counted = jnp.where(earlier <= later, lengths[...].astype(jnp.float32), 0.0)
+    counted = jnp.where(earlier <= later, held[...].astype(jnp.float32), 0.0)
     ends = jnp.sum(counted, axis=1, keepdims=True)
     pos = (lax.broadcasted_iota(jnp.int32, (docs, rows), 1) + here).astype(jnp.float32)
     start = jnp.max(jnp.where(ends <= pos, ends, 0.0), axis=0, keepdims=True)
     meta[0:1, :] = start.astype(jnp.int32) - here
     meta[1:2, :] = jnp.full((1, rows), device % 2, jnp.int32)
+    copies[0].wait()
+    copies[1].wait()
 
 
 def prepare(keys, values, lengths):
     rows, dim = keys.shape
     return pl.pallas_call(
         prep_body,
-        in_specs=[HERE] * 3,
+        in_specs=[pl.BlockSpec(memory_space=pltpu.HBM)] * 3,
         out_specs=[HERE] * 2,
         out_shape=[
             jax.ShapeDtypeStruct((rows, 2 * dim), keys.dtype),
             jax.ShapeDtypeStruct((2, rows), jnp.int32),
         ],
+        scratch_shapes=[pltpu.VMEM(lengths.shape, lengths.dtype), pltpu.SemaphoreType.DMA((3,))],
         compiler_params=pltpu.CompilerParams(vmem_limit_bytes=VMEM_LIMIT),
     )(keys, values, lengths)
+
+
+def stack_body(q, g, qs, gs, gt):
+    rows, dim = q.shape[0], qs.shape[1]
+    for h in range(q.shape[1] // dim):
+        cols, lanes = slice(h * dim, (h + 1) * dim), slice(h * rows, (h + 1) * rows)
+        qs[lanes, :] = q[:, cols]
+        gs[lanes, :] = g[:, cols]
+        gt[:, lanes] = g[:, cols].T
+
+
+def stack(queries, grad, dim):
+    rows, wide = queries.shape
+    tall = jax.ShapeDtypeStruct((rows * wide // dim, dim), queries.dtype)
+    return pl.pallas_call(
+        stack_body,
+        in_specs=[HERE] * 2,
+        out_specs=[HERE] * 3,
+        out_shape=[tall, tall, jax.ShapeDtypeStruct(tall.shape[::-1], queries.dtype)],
+        compiler_params=pltpu.CompilerParams(vmem_limit_bytes=VMEM_LIMIT),
+    )(queries, grad)
 
 
 def stage_body(plan, *refs):
@@ -86,11 +116,6 @@
         return (place(chip, side) + rows > earliest) & (place(chip, side) <= 0)
 
     if plan["first"]:
-        for h in range(heads):
-            g = ref["g"][:, cols[h]]
-            ref["qs"][lanes[h], :] = ref["q"][:, cols[h]]
-            ref["gs"][lanes[h], :] = g
-            ref["gt"][:, lanes[h]] = g.T
         ref["m"][...] = jnp.full_like(ref["m"], MASKED)
         ref["l"][...] = jnp.zeros_like(ref["l"])
         ref["acc"][...] = jnp.zeros_like(ref["acc"])
@@ -181,23 +206,18 @@
 def stage(state, fwd=(), bwd=(), final=False, last=False):
     rows, dim2 = state["kv", 0, 0].shape
     dim = dim2 // 2
-    heads = state["q"].shape[1] // dim
-    width = heads * rows
+    width = state["qs"].shape[0]
+    heads = width // rows
     bf16, f32 = jnp.bfloat16, jnp.float32
     shape = jax.ShapeDtypeStruct
     blocks = sorted(set(fwd) | set(bwd))
     first = (0, 0) in fwd
     row, tall = shape((1, width), f32), shape((dim, width), f32)
-    ins, outs, both = ["meta"], {}, []
-    if first:
-        ins += ["q", "g"]
-        outs.update(qs=shape((width, dim), bf16), gs=shape((width, dim), bf16), gt=shape((dim, width), bf16))
-    else:
-        ins.append("qs")
-        if final or bwd:
-            ins.append("gt")
-        if bwd:
-            ins.append("gs")
+    ins, outs, both = ["meta", "qs"], {}, []
+    if final or bwd:
+        ins.append("gt")
+    if bwd:
+        ins.append("gs")
     ins += [("kv", *b) for b in blocks]
     if fwd:
         for b in fwd:
@@ -259,7 +279,8 @@
     rows, dim = keys.shape
     f32, bf16 = jnp.float32, jnp.bfloat16
     own, meta = prepare(keys, values, doc_lengths[None, :])
-    state = {"meta": meta, "q": queries, "g": out_grad, ("kv", 0, 0): own}
+    state = {"meta": meta, ("kv", 0, 0): own}
+    state.update(zip(("qs", "gs", "gt"), stack(queries, out_grad, dim)))
 
     def arrive(chip, block):
         state["kv", chip, 0] = block
@@ -267,14 +288,13 @@
 
     back2 = shifted(own, 4)
     back1 = shifted(own, 2)
-    arrive(0, own)
-    stage(state, fwd=pairs(0))
-    back2 = after(back2, state["l"])
+    back2 = after(back2, state["qs"])
     back4 = shifted(back2, 4)
     back3 = shifted(back2, 2)
+    arrive(0, own)
     arrive(2, back2)
-    arrive(1, after(back1, state["l"]))
-    stage(state, fwd=pairs(1, 2))
+    arrive(1, back1)
+    stage(state, fwd=pairs(0, 1, 2))
     arrive(3, after(back3, state["l"]))
     arrive(4, after(back4, state["l"]))
     stage(state, fwd=pairs(3, 4), bwd=pairs(4), final=True)
@@ -287,16 +307,16 @@
     r4 = shifted(t4, -4)
     state["dq"] = after(state["dq"], t4)
     stage(state, bwd=pairs(1, 3) + [(0, 1)])
-    other = swapped(after(state["part", 0, 1], r4))
     t3 = summed(3, r4).astype(bf16)
-    t1 = summed(1, r4).astype(bf16)
     r3 = shifted(t3, -2)
-    r1 = shifted(t1, -2)
-    state["dq"] = after(state["dq"], t1, t3)
+    state["dq"] = after(state["dq"], t3)
     stage(state, bwd=pairs(2))
-    t2 = (summed(2, r1, r3) + r4.astype(f32) + r3.astype(f32)).astype(bf16)
+    t2 = (summed(2, r3) + r4.astype(f32) + r3.astype(f32)).astype(bf16)
     r2 = shifted(t2, -4)
-    state["dq"] = after(state["dq"], t2)
+    t1 = summed(1, state["part", 2, 0]).astype(bf16)
+    r1 = shifted(after(t1, t2), -2)
+    other = swapped(after(state["part", 0, 1], state["part", 2, 0]))
+    state["dq"] = after(state["dq"], t1, t2)
     stage(state, bwd=[(0, 0)], last=True)
     total = state["part", 0, 0] + other.astype(f32) + r1.astype(f32) + r2.astype(f32)
     return (state["out"], state["grad_q"], total[:, :dim].astype(bf16), total[:, dim:].astype(bf16))

time: 87.1 us -> 87.3 us (level)
  the two profiles are of different devices: /device:TPU:238 before, /device:TPU:24 now
where the time goes in v3:
time: 87.3 us; the launch traced here: 86.4 us
  starting transfers between devices  41.8 us (48%)
  waiting for transfers between devices  25.5 us (29%)
  Pallas kernels  13 us (15%)
  local copies, waits for them, and re-layouts  5.07 us (6%)
    ppermute x8, starting transfers between devices, shifted(): return lax.ppermute(shard, AXES, pairs)  38.4 us
    ppermute x8, waiting for transfers between devices, shifted(): return lax.ppermute(shard, AXES, pairs)  21.1 us
    pallas_call x5, Pallas kernels, stage(): pl.pallas_call(functools.partial(stage_body, plan), in_specs=[HERE] * (le...  12.6 us
    unnamed x10, local copies, waits for them, and re-layouts  4.4 us
    ppermute x10, waiting for transfers between devices, swapped(): return lax.ppermute(shard, AXES, [(i, i ^ 1) for i in range(peers)])  4.35 us
    ppermute x10, starting transfers between devices, swapped(): return lax.ppermute(shard, AXES, [(i, i ^ 1) for i in range(peers)])  3.33 us
  transfers between devices with their start and end apart: 18, of which 11 were waited for; matrix products, arithmetic and copies ran while one was open for 0% of the time, Pallas kernels for 13%

profile of v3, /device:TPU:24, one launch (start us, length us, event | category | flops | bytes accessed | tf_op | source)
XLA Modules:
  0.0 86.4 jit_solution(5485488760271342274)
XLA Ops:
  0.6 0.6 copy-done.4
  1.3 0.8 copy-done.2
  2.1 0.8 copy-done.3
  3.0 0.2 shard_map.84
  3.1 5.2 %collective-permute-start.3 = (bf16[256,256]{1,0:T(8,128)(2,1)S(1)}, bf16[256,256]{1,0:T(8,128)(2,1)S(1)}, u32[]{:S(2)}, u32[]{:S(2)}) collective-permute-start(bf16[256,256]{1,0:T(8,128)(2,1)S(1)} %get-tuple-element.62.refs_2_.refs_4_), channel_id=1, source_target_pairs={{0,4},{1,5},{2,6},{3,7},{4,8},{5,9},{6,10},{7,11},{8,12},{9,13},{1... | collective-permute-start | bytes 393224 | tf_op jit(solution)/shard_map/ppermute | solution.py:20
  8.3 3.8 %collective-permute-start.1 = (bf16[256,256]{1,0:T(8,128)(2,1)S(1)}, bf16[256,256]{1,0:T(8,128)(2,1)S(1)}, u32[]{:S(2)}, u32[]{:S(2)}) collective-permute-start(bf16[256,256]{1,0:T(8,128)(2,1)S(1)} %get-tuple-element.62.refs_2_.refs_4_), channel_id=1, source_target_pairs={{0,2},{1,3},{2,4},{3,5},{4,6},{5,7},{6,8},{7,9},{8,10},{9,11},{10,... | collective-permute-start | bytes 393224 | tf_op jit(solution)/shard_map/ppermute | solution.py:20
  12.2 0.1 collective-permute-start
  12.3 0.0 copy-start
  12.3 1.0 %copy-done = bf16[256,1024]{1,0:T(8,128)(2,1)S(1)} copy-done((bf16[256,1024]{1,0:T(8,128)(2,1)S(1)}, bf16[256,1024]{1,0:T(8,128)(2,1)}, u32[]{:S(2)}) %copy-start) | copy-done | bytes 524312
  13.3 1.0 %copy-done.1 = bf16[256,1024]{1,0:T(8,128)(2,1)S(1)} copy-done((bf16[256,1024]{1,0:T(8,128)(2,1)S(1)}, bf16[256,1024]{1,0:T(8,128)(2,1)}, u32[]{:S(2)}) %copy-start.1) | copy-done | bytes 524312
  14.4 0.3 shard_map.85
  14.7 4.4 %collective-permute-done.3.refs_6_.refs_4_ = bf16[256,256]{1,0:T(8,128)(2,1)S(1)} collective-permute-done((bf16[256,256]{1,0:T(8,128)(2,1)S(1)}, bf16[256,256]{1,0:T(8,128)(2,1)S(1)}, u32[]{:S(2)}, u32[]{:S(2)}) %collective-permute-start.3) | collective-permute-done | bytes 131104 | tf_op jit(solution)/shard_map/ppermute | solution.py:20
  19.1 3.3 %collective-permute-done.1.refs_4_.refs_5_ = bf16[256,256]{1,0:T(8,128)(2,1)S(1)} collective-permute-done((bf16[256,256]{1,0:T(8,128)(2,1)S(1)}, bf16[256,256]{1,0:T(8,128)(2,1)S(1)}, u32[]{:S(2)}, u32[]{:S(2)}) %collective-permute-start.1) | collective-permute-done | bytes 131104 | tf_op jit(solution)/shard_map/ppermute | solution.py:20
  22.4 0.0 collective-permute-start.2
  22.4 0.5 collective-permute-start.4
  22.9 1.9 %collective-permute-start.7 = (bf16[256,256]{1,0:T(8,128)(2,1)S(1)}, bf16[256,256]{1,0:T(8,128)(2,1)S(1)}, u32[]{:S(2)}, u32[]{:S(2)}) collective-permute-start(bf16[256,256]{1,0:T(8,128)(2,1)S(1)} %collective-permute-done.3.refs_6_.refs_4_), channel_id=1, source_target_pairs={{0,4},{1,5},{2,6},{3,7},{4,8},{5,9},{6,10},{7,11},{8,12},{9,13},{1... | collective-permute-start | bytes 393224 | tf_op jit(solution)/shard_map/ppermute | solution.py:20
  24.8 3.1 %collective-permute-start.5 = (bf16[256,256]{1,0:T(8,128)(2,1)S(1)}, bf16[256,256]{1,0:T(8,128)(2,1)S(1)}, u32[]{:S(2)}, u32[]{:S(2)}) collective-permute-start(bf16[256,256]{1,0:T(8,128)(2,1)S(1)} %collective-permute-done.3.refs_6_.refs_4_), channel_id=1, source_target_pairs={{0,2},{1,3},{2,4},{3,5},{4,6},{5,7},{6,8},{7,9},{8,10},{9,11},{10,... | collective-permute-start | bytes 393224 | tf_op jit(solution)/shard_map/ppermute | solution.py:20
  27.9 0.0 collective-permute-done.refs_3_.refs_4_
  27.9 0.0 collective-permute-done.2.refs_5_.refs_6_
  27.9 0.0 collective-permute-done.4.refs_7_.refs_5_
  28.0 4.3 %shard_map.86 = (bf16[256,2048]{1,0:T(8,128)(2,1)S(1)}, f32[1,2048]{1,0:T(1,128)S(1)}, bf16[256,2048]{1,0:T(8,128)(2,1)S(1)}, f32[1,2048]{1,0:T(1,128)S(1)}, bf1...) custom-call(s32[2,256]{1,0:T(2,128)S(1)} %get-tuple-element.58.refs_, ...), custom_call_target="tpu_custom_call" | custom-call | flops 1610612736 | bytes 1048576 | tf_op jit(solution)/shard_map/pallas_call | solution.py:255
  32.2 4.1 %collective-permute-done.7.refs_6_ = bf16[256,256]{1,0:T(8,128)(2,1)S(1)} collective-permute-done((bf16[256,256]{1,0:T(8,128)(2,1)S(1)}, bf16[256,256]{1,0:T(8,128)(2,1)S(1)}, u32[]{:S(2)}, u32[]{:S(2)}) %collective-permute-start.7) | collective-permute-done | bytes 131104 | tf_op jit(solution)/shard_map/ppermute | solution.py:20
  36.3 2.6 %collective-permute-done.5.refs_4_.refs_7_ = bf16[256,256]{1,0:T(8,128)(2,1)S(1)} collective-permute-done((bf16[256,256]{1,0:T(8,128)(2,1)S(1)}, bf16[256,256]{1,0:T(8,128)(2,1)S(1)}, u32[]{:S(2)}, u32[]{:S(2)}) %collective-permute-start.5) | collective-permute-done | bytes 131104 | tf_op jit(solution)/shard_map/ppermute | solution.py:20
  38.9 0.0 collective-permute-start.6
  38.9 0.5 collective-permute-start.8
  39.4 0.8 collective-permute-done.6.refs_5_.refs_8_
  40.3 0.2 collective-permute-done.8.refs_7_
  40.5 2.1 %shard_map.87 = (bf16[256,2048]{1,0:T(8,128)(2,1)S(1)}, f32[1,2048]{1,0:T(1,128)S(1)}, bf16[256,2048]{1,0:T(8,128)(2,1)S(1)}, f32[1,2048]{1,0:T(1,128)S(1)}, bf1...) custom-call(s32[2,256]{1,0:T(2,128)S(1)} %get-tuple-element.58.refs_, ...), custom_call_target="tpu_custom_call", output_to_operand_aliasing={{8}: (8, {}), {9}: (9, {}), {10}: (10, {})} | custom-call | flops 2147483648 | bytes 1048576 | tf_op jit(solution)/shard_map/pallas_call | solution.py:255
  42.5 0.3 collective-permute-start.9
  42.9 1.0 %collective-permute-done.9 = bf16[256,256]{1,0:T(8,128)(2,1)S(1)} collective-permute-done((bf16[256,256]{1,0:T(8,128)(2,1)S(1)}, bf16[256,256]{1,0:T(8,128)(2,1)S(1)}, u32[]{:S(2)}, u32[]{:S(2)}) %collective-permute-start.9) | collective-permute-done | bytes 131104 | tf_op jit(solution)/shard_map/ppermute | solution.py:25
  43.9 10.2 %collective-permute-start.10 = (bf16[256,256]{1,0:T(8,128)(2,1)S(1)}, bf16[256,256]{1,0:T(8,128)(2,1)S(1)}, u32[]{:S(2)}, u32[]{:S(2)}) collective-permute-start(bf16[256,256]{1,0:T(8,128)(2,1)S(1)} %add_convert_fusion.4), channel_id=1, source_target_pairs={{4,0},{5,1},{6,2},{7,3},{8,4},{9,5},{10,6},{11,7},{12,8},{13,9},{1... | collective-permute-start | bytes 393224 | tf_op jit(solution)/shard_map/ppermute | solution.py:20
  54.1 3.2 %shard_map.88 = (f32[256,256]{1,0:T(8,128)S(1)}, bf16[256,256]{1,0:T(8,128)(2,1)S(1)}, f32[256,256]{1,0:T(8,128)S(1)}, bf16[256,256]{1,0:T(8,128)(2,1)S(1)}, bf1...) custom-call(s32[2,256]{1,0:T(2,128)S(1)} %get-tuple-element.58.refs_0_, ...), custom_call_target="tpu_custom_call", output_to_operand_aliasing={{5}: (22, {})} | custom-call | flops 2684354560 | bytes 1048576 | tf_op jit(solution)/shard_map/pallas_call | solution.py:255
  57.3 0.0 collective-permute-done.10
  57.3 1.3 %collective-permute-start.11 = (bf16[256,256]{1,0:T(8,128)(2,1)S(1)}, bf16[256,256]{1,0:T(8,128)(2,1)S(1)}, u32[]{:S(2)}, u32[]{:S(2)}) collective-permute-start(bf16[256,256]{1,0:T(8,128)(2,1)S(1)} %get-tuple-element.96), channel_id=1, source_target_pairs={{0,1},{1,0},{2,3},{3,2},{4,5},{5,4},{6,7},{7,6},{8,9},{9,8},{10,11... | collective-permute-start | bytes 393224 | tf_op jit(solution)/shard_map/ppermute | solution.py:25
  58.6 1.0 %collective-permute-done.11 = bf16[256,256]{1,0:T(8,128)(2,1)S(1)} collective-permute-done((bf16[256,256]{1,0:T(8,128)(2,1)S(1)}, bf16[256,256]{1,0:T(8,128)(2,1)S(1)}, u32[]{:S(2)}, u32[]{:S(2)}) %collective-permute-start.11) | collective-permute-done | bytes 131104 | tf_op jit(solution)/shard_map/ppermute | solution.py:25
  59.6 3.7 %collective-permute-start.13 = (bf16[256,256]{1,0:T(8,128)(2,1)S(1)}, bf16[256,256]{1,0:T(8,128)(2,1)S(1)}, u32[]{:S(2)}, u32[]{:S(2)}) collective-permute-start(bf16[256,256]{1,0:T(8,128)(2,1)S(1)} %add_convert_fusion.3), channel_id=1, source_target_pairs={{2,0},{3,1},{4,2},{5,3},{6,4},{7,5},{8,6},{9,7},{10,8},{11,9},{12,... | collective-permute-start | bytes 393224 | tf_op jit(solution)/shard_map/ppermute | solution.py:20
  63.4 0.2 shard_map.89
  63.6 0.1 collective-permute-start.12
  63.7 0.5 collective-permute-start.15
  64.2 3.1 %collective-permute-done.13 = bf16[256,256]{1,0:T(8,128)(2,1)S(1)} collective-permute-done((bf16[256,256]{1,0:T(8,128)(2,1)S(1)}, bf16[256,256]{1,0:T(8,128)(2,1)S(1)}, u32[]{:S(2)}, u32[]{:S(2)}) %collective-permute-start.13) | collective-permute-done | bytes 131104 | tf_op jit(solution)/shard_map/ppermute | solution.py:20
  67.3 1.3 %collective-permute-done.14 = bf16[256,256]{1,0:T(8,128)(2,1)S(1)} collective-permute-done((bf16[256,256]{1,0:T(8,128)(2,1)S(1)}, bf16[256,256]{1,0:T(8,128)(2,1)S(1)}, u32[]{:S(2)}, u32[]{:S(2)}) %collective-permute-start.14) | collective-permute-done | bytes 131104 | tf_op jit(solution)/shard_map/ppermute | solution.py:25
  68.6 0.1 add_convert_fusion.1
  68.7 7.7 %collective-permute-start.16 = (bf16[256,256]{1,0:T(8,128)(2,1)S(1)}, bf16[256,256]{1,0:T(8,128)(2,1)S(1)}, u32[]{:S(2)}, u32[]{:S(2)}) collective-permute-start(bf16[256,256]{1,0:T(8,128)(2,1)S(1)} %add_convert_fusion.2), channel_id=1, source_target_pairs={{2,0},{3,1},{4,2},{5,3},{6,4},{7,5},{8,6},{9,7},{10,8},{11,9},{12,... | collective-permute-start | bytes 393224 | tf_op jit(solution)/shard_map/ppermute | solution.py:20
  76.5 2.8 %collective-permute-start.17 = (bf16[256,256]{1,0:T(8,128)(2,1)S(1)}, bf16[256,256]{1,0:T(8,128)(2,1)S(1)}, u32[]{:S(2)}, u32[]{:S(2)}) collective-permute-start(bf16[256,256]{1,0:T(8,128)(2,1)S(1)} %add_convert_fusion.1), channel_id=1, source_target_pairs={{4,0},{5,1},{6,2},{7,3},{8,4},{9,5},{10,6},{11,7},{12,8},{13,9},{1... | collective-permute-start | bytes 393224 | tf_op jit(solution)/shard_map/ppermute | solution.py:20
  79.2 2.8 %shard_map.90 = (f32[256,256]{1,0:T(8,128)S(1)}, f32[128,2048]{1,0:T(8,128)S(1)}, bf16[256,1024]{1,0:T(8,128)(2,1)}, bf16[256,1024]{1,0:T(8,128)(2,1)}) custom-call(s32[2,256]{1,0:T(2,128)S(1)} %get-tuple-element.58.refs_0_, bf16[2048,128]{1,0:T(8,128)(2,1)S(1)} %get-tuple-element.59.refs_1_, ...), custom_call_target="tpu_custom_call", output_to_operand_aliasing={{1}: (11, {})} | custom-call | flops 536870912 | bytes 1048576 | tf_op jit(solution)/shard_map/pallas_call | solution.py:255
  82.0 3.6 %collective-permute-done.17 = bf16[256,256]{1,0:T(8,128)(2,1)S(1)} collective-permute-done((bf16[256,256]{1,0:T(8,128)(2,1)S(1)}, bf16[256,256]{1,0:T(8,128)(2,1)S(1)}, u32[]{:S(2)}, u32[]{:S(2)}) %collective-permute-start.17) | collective-permute-done | bytes 131104 | tf_op jit(solution)/shard_map/ppermute | solution.py:20
  85.7 0.1 add_convert_fusion
  85.8 0.7 fusion
  (11 shorter events, 0.1 us)
Async XLA Ops:
  0.6 0.7 copy-start.4
  1.3 0.8 copy-start.2
  2.1 0.8 copy-start.3
  3.1 15.9 %collective-permute-start.3 = (bf16[256,256]{1,0:T(8,128)(2,1)S(1)}, bf16[256,256]{1,0:T(8,128)(2,1)S(1)}, u32[]{:S(2)}, u32[]{:S(2)}) collective-permute-start(bf16[256,256]{1,0:T(8,128)(2,1)S(1)} %get-tuple-element.62.refs_2_.refs_4_), channel_id=1, source_target_pairs={{0,4},{1,5},{2,6},{3,7},{4,8},{5,9},{6,10},{7,11},{8,12},{9,13},{1... | collective-permute-start | bytes 393224 | tf_op jit(solution)/shard_map/ppermute | solution.py:20
  8.3 14.1 %collective-permute-start.1 = (bf16[256,256]{1,0:T(8,128)(2,1)S(1)}, bf16[256,256]{1,0:T(8,128)(2,1)S(1)}, u32[]{:S(2)}, u32[]{:S(2)}) collective-permute-start(bf16[256,256]{1,0:T(8,128)(2,1)S(1)} %get-tuple-element.62.refs_2_.refs_4_), channel_id=1, source_target_pairs={{0,2},{1,3},{2,4},{3,5},{4,6},{5,7},{6,8},{7,9},{8,10},{9,11},{10,... | collective-permute-start | bytes 393224 | tf_op jit(solution)/shard_map/ppermute | solution.py:20
  12.2 15.8 %collective-permute-start = (bf16[256,256]{1,0:T(8,128)(2,1)S(1)}, bf16[256,256]{1,0:T(8,128)(2,1)S(1)}, u32[]{:S(2)}, u32[]{:S(2)}) collective-permute-start(bf16[256,256]{1,0:T(8,128)(2,1)S(1)} %get-tuple-element.62.refs_2_.refs_4_), channel_id=1, source_target_pairs={{0,1},{1,0},{2,3},{3,2},{4,5},{5,4},{6,7},{7,6},{8,9},{9,8},{10,11... | collective-permute-start | bytes 393224 | tf_op jit(solution)/shard_map/ppermute | solution.py:25
  12.3 1.0 %copy-start = (bf16[256,1024]{1,0:T(8,128)(2,1)S(1)}, bf16[256,1024]{1,0:T(8,128)(2,1)}, u32[]{:S(2)}) copy-start(bf16[256,1024]{1,0:T(8,128)(2,1)} %q.1) | copy-start | bytes 1572868
  13.3 1.0 %copy-start.1 = (bf16[256,1024]{1,0:T(8,128)(2,1)S(1)}, bf16[256,1024]{1,0:T(8,128)(2,1)}, u32[]{:S(2)}) copy-start(bf16[256,1024]{1,0:T(8,128)(2,1)} %g.1) | copy-start | bytes 1572868
  22.4 5.5 %collective-permute-start.2 = (bf16[256,256]{1,0:T(8,128)(2,1)S(1)}, bf16[256,256]{1,0:T(8,128)(2,1)S(1)}, u32[]{:S(2)}, u32[]{:S(2)}) collective-permute-start(bf16[256,256]{1,0:T(8,128)(2,1)S(1)} %collective-permute-done.1.refs_4_.refs_5_), channel_id=1, source_target_pairs={{0,1},{1,0},{2,3},{3,2},{4,5},{5,4},{6,7},{7,6},{8,9},{9,8},{10,11... | collective-permute-start | bytes 393224 | tf_op jit(solution)/shard_map/ppermute | solution.py:25
  22.4 5.6 %collective-permute-start.4 = (bf16[256,256]{1,0:T(8,128)(2,1)S(1)}, bf16[256,256]{1,0:T(8,128)(2,1)S(1)}, u32[]{:S(2)}, u32[]{:S(2)}) collective-permute-start(bf16[256,256]{1,0:T(8,128)(2,1)S(1)} %collective-permute-done.3.refs_6_.refs_4_), channel_id=1, source_target_pairs={{0,1},{1,0},{2,3},{3,2},{4,5},{5,4},{6,7},{7,6},{8,9},{9,8},{10,11... | collective-permute-start | bytes 393224 | tf_op jit(solution)/shard_map/ppermute | solution.py:25
  22.9 13.4 %collective-permute-start.7 = (bf16[256,256]{1,0:T(8,128)(2,1)S(1)}, bf16[256,256]{1,0:T(8,128)(2,1)S(1)}, u32[]{:S(2)}, u32[]{:S(2)}) collective-permute-start(bf16[256,256]{1,0:T(8,128)(2,1)S(1)} %collective-permute-done.3.refs_6_.refs_4_), channel_id=1, source_target_pairs={{0,4},{1,5},{2,6},{3,7},{4,8},{5,9},{6,10},{7,11},{8,12},{9,13},{1... | collective-permute-start | bytes 393224 | tf_op jit(solution)/shard_map/ppermute | solution.py:20
  24.8 14.1 %collective-permute-start.5 = (bf16[256,256]{1,0:T(8,128)(2,1)S(1)}, bf16[256,256]{1,0:T(8,128)(2,1)S(1)}, u32[]{:S(2)}, u32[]{:S(2)}) collective-permute-start(bf16[256,256]{1,0:T(8,128)(2,1)S(1)} %collective-permute-done.3.refs_6_.refs_4_), channel_id=1, source_target_pairs={{0,2},{1,3},{2,4},{3,5},{4,6},{5,7},{6,8},{7,9},{8,10},{9,11},{10,... | collective-permute-start | bytes 393224 | tf_op jit(solution)/shard_map/ppermute | solution.py:20
  38.9 1.3 %collective-permute-start.6 = (bf16[256,256]{1,0:T(8,128)(2,1)S(1)}, bf16[256,256]{1,0:T(8,128)(2,1)S(1)}, u32[]{:S(2)}, u32[]{:S(2)}) collective-permute-start(bf16[256,256]{1,0:T(8,128)(2,1)S(1)} %collective-permute-done.5.refs_4_.refs_7_), channel_id=1, source_target_pairs={{0,1},{1,0},{2,3},{3,2},{4,5},{5,4},{6,7},{7,6},{8,9},{9,8},{10,11... | collective-permute-start | bytes 393224 | tf_op jit(solution)/shard_map/ppermute | solution.py:25
  38.9 1.5 %collective-permute-start.8 = (bf16[256,256]{1,0:T(8,128)(2,1)S(1)}, bf16[256,256]{1,0:T(8,128)(2,1)S(1)}, u32[]{:S(2)}, u32[]{:S(2)}) collective-permute-start(bf16[256,256]{1,0:T(8,128)(2,1)S(1)} %collective-permute-done.7.refs_6_), channel_id=1, source_target_pairs={{0,1},{1,0},{2,3},{3,2},{4,5},{5,4},{6,7},{7,6},{8,9},{9,8},{10,11... | collective-permute-start | bytes 393224 | tf_op jit(solution)/shard_map/ppermute | solution.py:25
  42.5 1.3 %collective-permute-start.9 = (bf16[256,256]{1,0:T(8,128)(2,1)S(1)}, bf16[256,256]{1,0:T(8,128)(2,1)S(1)}, u32[]{:S(2)}, u32[]{:S(2)}) collective-permute-start(bf16[256,256]{1,0:T(8,128)(2,1)S(1)} %get-tuple-element.91), channel_id=1, source_target_pairs={{0,1},{1,0},{2,3},{3,2},{4,5},{5,4},{6,7},{7,6},{8,9},{9,8},{10,11... | collective-permute-start | bytes 393224 | tf_op jit(solution)/shard_map/ppermute | solution.py:25
  43.9 13.4 %collective-permute-start.10 = (bf16[256,256]{1,0:T(8,128)(2,1)S(1)}, bf16[256,256]{1,0:T(8,128)(2,1)S(1)}, u32[]{:S(2)}, u32[]{:S(2)}) collective-permute-start(bf16[256,256]{1,0:T(8,128)(2,1)S(1)} %add_convert_fusion.4), channel_id=1, source_target_pairs={{4,0},{5,1},{6,2},{7,3},{8,4},{9,5},{10,6},{11,7},{12,8},{13,9},{1... | collective-permute-start | bytes 393224 | tf_op jit(solution)/shard_map/ppermute | solution.py:20
  57.3 2.3 %collective-permute-start.11 = (bf16[256,256]{1,0:T(8,128)(2,1)S(1)}, bf16[256,256]{1,0:T(8,128)(2,1)S(1)}, u32[]{:S(2)}, u32[]{:S(2)}) collective-permute-start(bf16[256,256]{1,0:T(8,128)(2,1)S(1)} %get-tuple-element.96), channel_id=1, source_target_pairs={{0,1},{1,0},{2,3},{3,2},{4,5},{5,4},{6,7},{7,6},{8,9},{9,8},{10,11... | collective-permute-start | bytes 393224 | tf_op jit(solution)/shard_map/ppermute | solution.py:25
  59.6 7.7 %collective-permute-start.13 = (bf16[256,256]{1,0:T(8,128)(2,1)S(1)}, bf16[256,256]{1,0:T(8,128)(2,1)S(1)}, u32[]{:S(2)}, u32[]{:S(2)}) collective-permute-start(bf16[256,256]{1,0:T(8,128)(2,1)S(1)} %add_convert_fusion.3), channel_id=1, source_target_pairs={{2,0},{3,1},{4,2},{5,3},{6,4},{7,5},{8,6},{9,7},{10,8},{11,9},{12,... | collective-permute-start | bytes 393224 | tf_op jit(solution)/shard_map/ppermute | solution.py:20
  63.6 3.7 %collective-permute-start.12 = (bf16[256,256]{1,0:T(8,128)(2,1)S(1)}, bf16[256,256]{1,0:T(8,128)(2,1)S(1)}, u32[]{:S(2)}, u32[]{:S(2)}) collective-permute-start(bf16[256,256]{1,0:T(8,128)(2,1)S(1)} %get-tuple-element.102), channel_id=1, source_target_pairs={{0,1},{1,0},{2,3},{3,2},{4,5},{5,4},{6,7},{7,6},{8,9},{9,8},{10,11... | collective-permute-start | bytes 393224 | tf_op jit(solution)/shard_map/ppermute | solution.py:25
  63.7 18.3 %collective-permute-start.15 = (bf16[256,256]{1,0:T(8,128)(2,1)S(1)}, bf16[256,256]{1,0:T(8,128)(2,1)S(1)}, u32[]{:S(2)}, u32[]{:S(2)}) collective-permute-start(bf16[256,256]{1,0:T(8,128)(2,1)S(1)} %get-tuple-element.110), channel_id=1, source_target_pairs={{0,1},{1,0},{2,3},{3,2},{4,5},{5,4},{6,7},{7,6},{8,9},{9,8},{10,11... | collective-permute-start | bytes 393224 | tf_op jit(solution)/shard_map/ppermute | solution.py:25
  67.3 1.3 %collective-permute-start.14 = (bf16[256,256]{1,0:T(8,128)(2,1)S(1)}, bf16[256,256]{1,0:T(8,128)(2,1)S(1)}, u32[]{:S(2)}, u32[]{:S(2)}) collective-permute-start(bf16[256,256]{1,0:T(8,128)(2,1)S(1)} %get-tuple-element.104), channel_id=1, source_target_pairs={{0,1},{1,0},{2,3},{3,2},{4,5},{5,4},{6,7},{7,6},{8,9},{9,8},{10,11... | collective-permute-start | bytes 393224 | tf_op jit(solution)/shard_map/ppermute | solution.py:25
  68.7 13.3 %collective-permute-start.16 = (bf16[256,256]{1,0:T(8,128)(2,1)S(1)}, bf16[256,256]{1,0:T(8,128)(2,1)S(1)}, u32[]{:S(2)}, u32[]{:S(2)}) collective-permute-start(bf16[256,256]{1,0:T(8,128)(2,1)S(1)} %add_convert_fusion.2), channel_id=1, source_target_pairs={{2,0},{3,1},{4,2},{5,3},{6,4},{7,5},{8,6},{9,7},{10,8},{11,9},{12,... | collective-permute-start | bytes 393224 | tf_op jit(solution)/shard_map/ppermute | solution.py:20
  76.5 9.2 %collective-permute-start.17 = (bf16[256,256]{1,0:T(8,128)(2,1)S(1)}, bf16[256,256]{1,0:T(8,128)(2,1)S(1)}, u32[]{:S(2)}, u32[]{:S(2)}) collective-permute-start(bf16[256,256]{1,0:T(8,128)(2,1)S(1)} %add_convert_fusion.1), channel_id=1, source_target_pairs={{4,0},{5,1},{6,2},{7,3},{8,4},{9,5},{10,6},{11,7},{12,8},{13,9},{1... | collective-permute-start | bytes 393224 | tf_op jit(solution)/shard_map/ppermute | solution.py:20

commit v4 on v3

--- a/solution.py
+++ b/solution.py
@@ -9,8 +9,10 @@
 from jax.sharding import PartitionSpec as P
 
 AXES = ("node", "wide")
+REACH = 4
 MASKED = -1e30
 VMEM_LIMIT = 16 * 1024 * 1024
+QUICK = pl.CostEstimate(flops=1, bytes_accessed=1, transcendentals=0)
 HERE = pl.BlockSpec(memory_space=pltpu.VMEM)
 
 
@@ -251,7 +253,6 @@
     plan = dict(
         rows=rows, dim=dim, heads=heads, fwd=fwd, bwd=bwd, first=first, final=final, last=last, names=names
     )
-    products = 2 * len(fwd) + 4 * len(bwd)
     results = pl.pallas_call(
         functools.partial(stage_body, plan),
         in_specs=[HERE] * (len(ins) + len(both)),
@@ -260,9 +261,7 @@
         scratch_shapes=list(scratch.values()),
         input_output_aliases={len(ins) + i: out_names.index(b) for i, b in enumerate(both)},
         compiler_params=pltpu.CompilerParams(vmem_limit_bytes=VMEM_LIMIT),
-        cost_estimate=pl.CostEstimate(
-            flops=2 * products * rows * width * dim, bytes_accessed=2**20, transcendentals=0
-        ),
+        cost_estimate=QUICK,
     )(*[state[n] for n in ins + both])
     state.update(zip(out_names, results))
 
@@ -282,43 +281,26 @@
     state = {"meta": meta, ("kv", 0, 0): own}
     state.update(zip(("qs", "gs", "gt"), stack(queries, out_grad, dim)))
 
-    def arrive(chip, block):
-        state["kv", chip, 0] = block
-        state["kv", chip, 1] = swapped(block)
-
-    back2 = shifted(own, 4)
-    back1 = shifted(own, 2)
-    back2 = after(back2, state["qs"])
-    back4 = shifted(back2, 4)
-    back3 = shifted(back2, 2)
-    arrive(0, own)
-    arrive(2, back2)
-    arrive(1, back1)
-    stage(state, fwd=pairs(0, 1, 2))
-    arrive(3, after(back3, state["l"]))
-    arrive(4, after(back4, state["l"]))
-    stage(state, fwd=pairs(3, 4), bwd=pairs(4), final=True)
-
-    def summed(chip, *others):
-        other = swapped(after(state["part", chip, 1], *others))
-        return state["part", chip, 0] + other.astype(f32)
-
-    t4 = summed(4).astype(bf16)
-    r4 = shifted(t4, -4)
-    state["dq"] = after(state["dq"], t4)
-    stage(state, bwd=pairs(1, 3) + [(0, 1)])
-    t3 = summed(3, r4).astype(bf16)
-    r3 = shifted(t3, -2)
-    state["dq"] = after(state["dq"], t3)
-    stage(state, bwd=pairs(2))
-    t2 = (summed(2, r3) + r4.astype(f32) + r3.astype(f32)).astype(bf16)
-    r2 = shifted(t2, -4)
-    t1 = summed(1, state["part", 2, 0]).astype(bf16)
-    r1 = shifted(after(t1, t2), -2)
-    other = swapped(after(state["part", 0, 1], state["part", 2, 0]))
-    state["dq"] = after(state["dq"], t1, t2)
-    stage(state, bwd=[(0, 0)], last=True)
-    total = state["part", 0, 0] + other.astype(f32) + r1.astype(f32) + r2.astype(f32)
+    block = own
+    for chip in range(REACH):
+        coming = shifted(block, 2)
+        state["kv", chip, 0], state["kv", chip, 1] = block, swapped(block)
+        stage(state, fwd=pairs(chip))
+        block = after(coming, state["l"])
+    state["kv", REACH, 0], state["kv", REACH, 1] = block, swapped(block)
+    stage(state, fwd=pairs(REACH), bwd=[(REACH, 0), (REACH, 1), (REACH - 1, 1)], final=True)
+
+    passed = None
+    for chip in range(REACH, -1, -1):
+        total = state["part", chip, 0] + swapped(state["part", chip, 1]).astype(f32)
+        if passed is not None:
+            total = total + passed.astype(f32)
+        if chip:
+            total = total.astype(bf16)
+            passed = shifted(total, -2)
+            state["dq"] = after(state["dq"], total)
+            todo = [(chip - 1, 0)] + [(chip - 2, 1)] * (chip > 1)
+            stage(state, bwd=todo, last=chip == 1)
     return (state["out"], state["grad_q"], total[:, :dim].astype(bf16), total[:, dim:].astype(bf16))
 
 

time: 87.3 us -> 98.7 us (1.13)
  waiting for transfers between devices: 25.5 us -> 38.7 us
  starting transfers between devices: 41.8 us -> 36.8 us
  Pallas kernels: 13 us -> 16.2 us
    ppermute x8, waiting for transfers between devices: 21.1 us -> 36.5 us  [shifted(): return lax.ppermute(shard, AXES, pairs)]
    ppermute x8, starting transfers between devices: 38.4 us -> 35.1 us  [shifted(): return lax.ppermute(shard, AXES, pairs)]
    pallas_call x5 -> x9, Pallas kernels: 12.6 us -> 15.7 us  [stage(): pl.pallas_call(functools.partial(stage_body, plan), in_specs=[HERE] * (le...]
    ppermute x10, waiting for transfers between devices: 4.35 us -> 2.2 us  [swapped(): return lax.ppermute(shard, AXES, [(i, i ^ 1) for i in range(peers)])]
    ppermute x10, starting transfers between devices: 3.33 us -> 1.76 us  [swapped(): return lax.ppermute(shard, AXES, [(i, i ^ 1) for i in range(peers)])]
  transfers between devices with their start and end apart: 18 -> 18, of which waited for: 11 -> 9; matrix products, arithmetic and copies ran while one was open for 0% -> 0% of each run, Pallas kernels for 13% -> 14%
where the time goes in v4:
time: 98.7 us; the launch traced here: 98 us
  waiting for transfers between devices  38.7 us (39%)
  starting transfers between devices  36.8 us (37%)
  Pallas kernels  16.2 us (16%)
  local copies, waits for them, and re-layouts  5.07 us (5%)
    ppermute x8, waiting for transfers between devices, shifted(): return lax.ppermute(shard, AXES, pairs)  36.5 us
    ppermute x8, starting transfers between devices, shifted(): return lax.ppermute(shard, AXES, pairs)  35.1 us
    pallas_call x9, Pallas kernels, stage(): pl.pallas_call(functools.partial(stage_body, plan), in_specs=[HERE] * (le...  15.7 us
    unnamed x10, local copies, waits for them, and re-layouts  4.4 us
    ppermute x10, waiting for transfers between devices, swapped(): return lax.ppermute(shard, AXES, [(i, i ^ 1) for i in range(peers)])  2.2 us
  transfers between devices with their start and end apart: 18, of which 9 were waited for; matrix products, arithmetic and copies ran while one was open for 0% of the time, Pallas kernels for 14%

profile of v4, /device:TPU:24, one launch (start us, length us, event | category | flops | bytes accessed | tf_op | source)
XLA Modules:
  0.0 98.0 jit_solution(17700085306759716053)
XLA Ops:
  0.6 0.6 copy-done.4
  1.3 0.8 copy-done.2
  2.1 0.8 copy-done.3
  3.0 0.2 shard_map.84
  3.1 0.1 collective-permute-start
  3.2 3.8 %collective-permute-start.1 = (bf16[256,256]{1,0:T(8,128)(2,1)S(1)}, bf16[256,256]{1,0:T(8,128)(2,1)S(1)}, u32[]{:S(2)}, u32[]{:S(2)}) collective-permute-start(bf16[256,256]{1,0:T(8,128)(2,1)S(1)} %get-tuple-element.69.refs_2_.refs_4_), channel_id=1, source_target_pairs={{0,2},{1,3},{2,4},{3,5},{4,6},{5,7},{6,8},{7,9},{8,10},{9,11},{10,... | collective-permute-start | bytes 393224 | tf_op jit(solution)/shard_map/ppermute | solution.py:22
  7.1 0.0 copy-start
  7.1 1.0 %copy-done = bf16[256,1024]{1,0:T(8,128)(2,1)S(1)} copy-done((bf16[256,1024]{1,0:T(8,128)(2,1)S(1)}, bf16[256,1024]{1,0:T(8,128)(2,1)}, u32[]{:S(2)}) %copy-start) | copy-done | bytes 524312
  8.1 1.0 %copy-done.1 = bf16[256,1024]{1,0:T(8,128)(2,1)S(1)} copy-done((bf16[256,1024]{1,0:T(8,128)(2,1)S(1)}, bf16[256,1024]{1,0:T(8,128)(2,1)}, u32[]{:S(2)}) %copy-start.1) | copy-done | bytes 524312
  9.2 0.3 shard_map.85
  9.5 1.5 %shard_map.86 = (bf16[256,2048]{1,0:T(8,128)(2,1)S(1)}, f32[1,2048]{1,0:T(1,128)S(1)}, bf16[256,2048]{1,0:T(8,128)(2,1)S(1)}, f32[1,2048]{1,0:T(1,128)S(1)}, f32...) custom-call(s32[2,256]{1,0:T(2,128)S(1)} %get-tuple-element.65.refs_0_, ...), custom_call_target="tpu_custom_call" | custom-call | flops 1 | bytes 1 | tf_op jit(solution)/shard_map/pallas_call | solution.py:256
  11.0 6.5 %collective-permute-done.1.refs_2_.refs_5_ = bf16[256,256]{1,0:T(8,128)(2,1)S(1)} collective-permute-done((bf16[256,256]{1,0:T(8,128)(2,1)S(1)}, bf16[256,256]{1,0:T(8,128)(2,1)S(1)}, u32[]{:S(2)}, u32[]{:S(2)}) %collective-permute-start.1) | collective-permute-done | bytes 131104 | tf_op jit(solution)/shard_map/ppermute | solution.py:22
  17.5 1.9 %collective-permute-start.2 = (bf16[256,256]{1,0:T(8,128)(2,1)S(1)}, bf16[256,256]{1,0:T(8,128)(2,1)S(1)}, u32[]{:S(2)}, u32[]{:S(2)}) collective-permute-start(bf16[256,256]{1,0:T(8,128)(2,1)S(1)} %collective-permute-done.1.refs_2_.refs_5_), channel_id=1, source_target_pairs={{0,2},{1,3},{2,4},{3,5},{4,6},{5,7},{6,8},{7,9},{8,10},{9,11},{10,... | collective-permute-start | bytes 393224 | tf_op jit(solution)/shard_map/ppermute | solution.py:22
  19.4 0.0 collective-permute-done.3.refs_3_.refs_4_
  19.5 2.9 %shard_map.87 = (bf16[256,2048]{1,0:T(8,128)(2,1)S(1)}, f32[1,2048]{1,0:T(1,128)S(1)}, bf16[256,2048]{1,0:T(8,128)(2,1)S(1)}, f32[1,2048]{1,0:T(1,128)S(1)}, f32...) custom-call(s32[2,256]{1,0:T(2,128)S(1)} %get-tuple-element.65.refs_, ...), custom_call_target="tpu_custom_call", output_to_operand_aliasing={{4}: (4, {}), {5}: (5, {}), {6}: (6, {})} | custom-call | flops 1 | bytes 1 | tf_op jit(solution)/shard_map/pallas_call | solution.py:256
  22.4 7.2 %collective-permute-done.2.refs_2_.refs_5_ = bf16[256,256]{1,0:T(8,128)(2,1)S(1)} collective-permute-done((bf16[256,256]{1,0:T(8,128)(2,1)S(1)}, bf16[256,256]{1,0:T(8,128)(2,1)S(1)}, u32[]{:S(2)}, u32[]{:S(2)}) %collective-permute-start.2) | collective-permute-done | bytes 131104 | tf_op jit(solution)/shard_map/ppermute | solution.py:22
  29.5 0.0 collective-permute-start.5
  29.5 1.9 %collective-permute-start.4 = (bf16[256,256]{1,0:T(8,128)(2,1)S(1)}, bf16[256,256]{1,0:T(8,128)(2,1)S(1)}, u32[]{:S(2)}, u32[]{:S(2)}) collective-permute-start(bf16[256,256]{1,0:T(8,128)(2,1)S(1)} %collective-permute-done.2.refs_2_.refs_5_), channel_id=1, source_target_pairs={{0,2},{1,3},{2,4},{3,5},{4,6},{5,7},{6,8},{7,9},{8,10},{9,11},{10,... | collective-permute-start | bytes 393224 | tf_op jit(solution)/shard_map/ppermute | solution.py:22
  31.5 0.0 collective-permute-done.5.refs_3_.refs_4_
  31.5 1.6 %shard_map.88 = (bf16[256,2048]{1,0:T(8,128)(2,1)S(1)}, f32[1,2048]{1,0:T(1,128)S(1)}, bf16[256,2048]{1,0:T(8,128)(2,1)S(1)}, f32[1,2048]{1,0:T(1,128)S(1)}, f32...) custom-call(s32[2,256]{1,0:T(2,128)S(1)} %get-tuple-element.65.refs_, ...), custom_call_target="tpu_custom_call", output_to_operand_aliasing={{4}: (4, {}), {5}: (5, {}), {6}: (6, {})} | custom-call | flops 1 | bytes 1 | tf_op jit(solution)/shard_map/pallas_call | solution.py:256
  33.0 8.5 %collective-permute-done.4.refs_2_.refs_5_ = bf16[256,256]{1,0:T(8,128)(2,1)S(1)} collective-permute-done((bf16[256,256]{1,0:T(8,128)(2,1)S(1)}, bf16[256,256]{1,0:T(8,128)(2,1)S(1)}, u32[]{:S(2)}, u32[]{:S(2)}) %collective-permute-start.4) | collective-permute-done | bytes 131104 | tf_op jit(solution)/shard_map/ppermute | solution.py:22
  41.6 0.0 collective-permute-start.6
  41.6 1.9 %collective-permute-start.7 = (bf16[256,256]{1,0:T(8,128)(2,1)S(1)}, bf16[256,256]{1,0:T(8,128)(2,1)S(1)}, u32[]{:S(2)}, u32[]{:S(2)}) collective-permute-start(bf16[256,256]{1,0:T(8,128)(2,1)S(1)} %collective-permute-done.4.refs_2_.refs_5_), channel_id=1, source_target_pairs={{0,2},{1,3},{2,4},{3,5},{4,6},{5,7},{6,8},{7,9},{8,10},{9,11},{10,... | collective-permute-start | bytes 393224 | tf_op jit(solution)/shard_map/ppermute | solution.py:22
  43.5 0.4 shard_map.89
  43.9 9.7 %collective-permute-done.7.refs_5_ = bf16[256,256]{1,0:T(8,128)(2,1)S(1)} collective-permute-done((bf16[256,256]{1,0:T(8,128)(2,1)S(1)}, bf16[256,256]{1,0:T(8,128)(2,1)S(1)}, u32[]{:S(2)}, u32[]{:S(2)}) %collective-permute-start.7) | collective-permute-done | bytes 131104 | tf_op jit(solution)/shard_map/ppermute | solution.py:22
  53.6 1.3 %collective-permute-done.8.refs_6_ = bf16[256,256]{1,0:T(8,128)(2,1)S(1)} collective-permute-done((bf16[256,256]{1,0:T(8,128)(2,1)S(1)}, bf16[256,256]{1,0:T(8,128)(2,1)S(1)}, u32[]{:S(2)}, u32[]{:S(2)}) %collective-permute-start.8) | collective-permute-done | bytes 131104 | tf_op jit(solution)/shard_map/ppermute | solution.py:27
  54.9 1.9 %shard_map.90 = (bf16[256,2048]{1,0:T(8,128)(2,1)}, f32[1,2048]{1,0:T(1,128)}, bf16[256,2048]{1,0:T(8,128)(2,1)}, f32[1,2048]{1,0:T(1,128)}, f32[1,2048]{1,0:T(1...) custom-call(s32[2,256]{1,0:T(2,128)S(1)} %get-tuple-element.65.refs_, ...), custom_call_target="tpu_custom_call", output_to_operand_aliasing={{4}: (9, {}), {5}: (10, {}), {6}: (11, {})} | custom-call | flops 1 | bytes 1 | tf_op jit(solution)/shard_map/pallas_call | solution.py:256
  56.8 0.1 collective-permute-start.9
  57.0 0.4 collective-permute-start.10
  57.3 0.8 collective-permute-done.9
  58.2 1.9 %collective-permute-start.11 = (bf16[256,256]{1,0:T(8,128)(2,1)S(1)}, bf16[256,256]{1,0:T(8,128)(2,1)S(1)}, u32[]{:S(2)}, u32[]{:S(2)}) collective-permute-start(bf16[256,256]{1,0:T(8,128)(2,1)S(1)} %add_convert_fusion.4), channel_id=1, source_target_pairs={{2,0},{3,1},{4,2},{5,3},{6,4},{7,5},{8,6},{9,7},{10,8},{11,9},{12,... | collective-permute-start | bytes 393224 | tf_op jit(solution)/shard_map/ppermute | solution.py:22
  60.1 1.6 %shard_map.91 = (f32[256,256]{1,0:T(8,128)S(1)}, bf16[256,256]{1,0:T(8,128)(2,1)S(1)}, f32[128,2048]{1,0:T(8,128)S(1)}) custom-call(s32[2,256]{1,0:T(2,128)S(1)} %get-tuple-element.65.refs_0_, bf16[2048,128]{1,0:T(8,128)(2,1)S(1)} %get-tuple-element.66.refs_1_, bf16[128,2048]{1,0:T(8,128)(2,1)S(1)} %get-tuple-element.67.refs_2_, ...), custom_call_target="tpu_custom_call", output_to_operand_aliasing={{2}: (13, {})} | custom-call | flops 1 | bytes 1 | tf_op jit(solution)/shard_map/pallas_call | solution.py:256
  61.7 0.3 collective-permute-start.12
  62.0 3.6 %collective-permute-done.11 = bf16[256,256]{1,0:T(8,128)(2,1)S(1)} collective-permute-done((bf16[256,256]{1,0:T(8,128)(2,1)S(1)}, bf16[256,256]{1,0:T(8,128)(2,1)S(1)}, u32[]{:S(2)}, u32[]{:S(2)}) %collective-permute-start.11) | collective-permute-done | bytes 131104 | tf_op jit(solution)/shard_map/ppermute | solution.py:22
  65.6 0.1 add_convert_fusion.3
  65.7 6.4 %collective-permute-start.13 = (bf16[256,256]{1,0:T(8,128)(2,1)S(1)}, bf16[256,256]{1,0:T(8,128)(2,1)S(1)}, u32[]{:S(2)}, u32[]{:S(2)}) collective-permute-start(bf16[256,256]{1,0:T(8,128)(2,1)S(1)} %add_convert_fusion.3), channel_id=1, source_target_pairs={{2,0},{3,1},{4,2},{5,3},{6,4},{7,5},{8,6},{9,7},{10,8},{11,9},{12,... | collective-permute-start | bytes 393224 | tf_op jit(solution)/shard_map/ppermute | solution.py:22
  72.1 1.6 %shard_map.92 = (f32[256,256]{1,0:T(8,128)S(1)}, bf16[256,256]{1,0:T(8,128)(2,1)S(1)}, f32[128,2048]{1,0:T(8,128)S(1)}) custom-call(s32[2,256]{1,0:T(2,128)S(1)} %get-tuple-element.65.refs_0_, bf16[2048,128]{1,0:T(8,128)(2,1)S(1)} %get-tuple-element.66.refs_1_, bf16[128,2048]{1,0:T(8,128)(2,1)S(1)} %get-tuple-element.67.refs_2_, ...), custom_call_target="tpu_custom_call", output_to_operand_aliasing={{2}: (13, {})} | custom-call | flops 1 | bytes 1 | tf_op jit(solution)/shard_map/pallas_call | solution.py:256
  73.7 0.7 collective-permute-start.14
  74.4 0.2 collective-permute-done.13
  74.7 8.6 %collective-permute-start.15 = (bf16[256,256]{1,0:T(8,128)(2,1)S(1)}, bf16[256,256]{1,0:T(8,128)(2,1)S(1)}, u32[]{:S(2)}, u32[]{:S(2)}) collective-permute-start(bf16[256,256]{1,0:T(8,128)(2,1)S(1)} %add_convert_fusion.2), channel_id=1, source_target_pairs={{2,0},{3,1},{4,2},{5,3},{6,4},{7,5},{8,6},{9,7},{10,8},{11,9},{12,... | collective-permute-start | bytes 393224 | tf_op jit(solution)/shard_map/ppermute | solution.py:22
  83.3 1.5 %shard_map.93 = (f32[256,256]{1,0:T(8,128)S(1)}, bf16[256,256]{1,0:T(8,128)(2,1)S(1)}, f32[128,2048]{1,0:T(8,128)S(1)}) custom-call(s32[2,256]{1,0:T(2,128)S(1)} %get-tuple-element.65.refs_0_, bf16[2048,128]{1,0:T(8,128)(2,1)S(1)} %get-tuple-element.66.refs_1_, bf16[128,2048]{1,0:T(8,128)(2,1)S(1)} %get-tuple-element.67.refs_2_, ...), custom_call_target="tpu_custom_call", output_to_operand_aliasing={{2}: (13, {})} | custom-call | flops 1 | bytes 1 | tf_op jit(solution)/shard_map/pallas_call | solution.py:256
  84.8 0.1 collective-permute-start.16
  84.9 0.0 collective-permute-done.14
  85.0 0.9 collective-permute-done.15
  85.8 0.1 add_convert_fusion.1
  85.9 8.6 %collective-permute-start.17 = (bf16[256,256]{1,0:T(8,128)(2,1)S(1)}, bf16[256,256]{1,0:T(8,128)(2,1)S(1)}, u32[]{:S(2)}, u32[]{:S(2)}) collective-permute-start(bf16[256,256]{1,0:T(8,128)(2,1)S(1)} %add_convert_fusion.1), channel_id=1, source_target_pairs={{2,0},{3,1},{4,2},{5,3},{6,4},{7,5},{8,6},{9,7},{10,8},{11,9},{12,... | collective-permute-start | bytes 393224 | tf_op jit(solution)/shard_map/ppermute | solution.py:22
  94.4 2.8 %shard_map.94 = (f32[256,256]{1,0:T(8,128)S(1)}, f32[128,2048]{1,0:T(8,128)S(1)}, bf16[256,1024]{1,0:T(8,128)(2,1)}, bf16[256,1024]{1,0:T(8,128)(2,1)}) custom-call(s32[2,256]{1,0:T(2,128)S(1)} %get-tuple-element.65.refs_0_, bf16[2048,128]{1,0:T(8,128)(2,1)S(1)} %get-tuple-element.66.refs_1_, ...), custom_call_target="tpu_custom_call", output_to_operand_aliasing={{1}: (11, {})} | custom-call | flops 1 | bytes 1 | tf_op jit(solution)/shard_map/pallas_call | solution.py:256
  97.3 0.7 fusion
  (15 shorter events, 0.1 us)
Async XLA Ops:
  0.6 0.7 copy-start.4
  1.3 0.8 copy-start.2
  2.1 0.8 copy-start.3
  3.1 6.3 %collective-permute-start = (bf16[256,256]{1,0:T(8,128)(2,1)S(1)}, bf16[256,256]{1,0:T(8,128)(2,1)S(1)}, u32[]{:S(2)}, u32[]{:S(2)}) collective-permute-start(bf16[256,256]{1,0:T(8,128)(2,1)S(1)} %get-tuple-element.69.refs_2_.refs_4_), channel_id=1, source_target_pairs={{0,1},{1,0},{2,3},{3,2},{4,5},{5,4},{6,7},{7,6},{8,9},{9,8},{10,11... | collective-permute-start | bytes 393224 | tf_op jit(solution)/shard_map/ppermute | solution.py:27
  3.2 14.3 %collective-permute-start.1 = (bf16[256,256]{1,0:T(8,128)(2,1)S(1)}, bf16[256,256]{1,0:T(8,128)(2,1)S(1)}, u32[]{:S(2)}, u32[]{:S(2)}) collective-permute-start(bf16[256,256]{1,0:T(8,128)(2,1)S(1)} %get-tuple-element.69.refs_2_.refs_4_), channel_id=1, source_target_pairs={{0,2},{1,3},{2,4},{3,5},{4,6},{5,7},{6,8},{7,9},{8,10},{9,11},{10,... | collective-permute-start | bytes 393224 | tf_op jit(solution)/shard_map/ppermute | solution.py:22
  7.1 1.0 %copy-start = (bf16[256,1024]{1,0:T(8,128)(2,1)S(1)}, bf16[256,1024]{1,0:T(8,128)(2,1)}, u32[]{:S(2)}) copy-start(bf16[256,1024]{1,0:T(8,128)(2,1)} %q.1) | copy-start | bytes 1572868
  8.1 1.0 %copy-start.1 = (bf16[256,1024]{1,0:T(8,128)(2,1)S(1)}, bf16[256,1024]{1,0:T(8,128)(2,1)}, u32[]{:S(2)}) copy-start(bf16[256,1024]{1,0:T(8,128)(2,1)} %g.1) | copy-start | bytes 1572868
  17.5 1.9 %collective-permute-start.3 = (bf16[256,256]{1,0:T(8,128)(2,1)S(1)}, bf16[256,256]{1,0:T(8,128)(2,1)S(1)}, u32[]{:S(2)}, u32[]{:S(2)}) collective-permute-start(bf16[256,256]{1,0:T(8,128)(2,1)S(1)} %collective-permute-done.1.refs_2_.refs_5_), channel_id=1, source_target_pairs={{0,1},{1,0},{2,3},{3,2},{4,5},{5,4},{6,7},{7,6},{8,9},{9,8},{10,11... | collective-permute-start | bytes 393224 | tf_op jit(solution)/shard_map/ppermute | solution.py:27
  17.5 12.0 %collective-permute-start.2 = (bf16[256,256]{1,0:T(8,128)(2,1)S(1)}, bf16[256,256]{1,0:T(8,128)(2,1)S(1)}, u32[]{:S(2)}, u32[]{:S(2)}) collective-permute-start(bf16[256,256]{1,0:T(8,128)(2,1)S(1)} %collective-permute-done.1.refs_2_.refs_5_), channel_id=1, source_target_pairs={{0,2},{1,3},{2,4},{3,5},{4,6},{5,7},{6,8},{7,9},{8,10},{9,11},{10,... | collective-permute-start | bytes 393224 | tf_op jit(solution)/shard_map/ppermute | solution.py:22
  29.5 1.9 %collective-permute-start.5 = (bf16[256,256]{1,0:T(8,128)(2,1)S(1)}, bf16[256,256]{1,0:T(8,128)(2,1)S(1)}, u32[]{:S(2)}, u32[]{:S(2)}) collective-permute-start(bf16[256,256]{1,0:T(8,128)(2,1)S(1)} %collective-permute-done.2.refs_2_.refs_5_), channel_id=1, source_target_pairs={{0,1},{1,0},{2,3},{3,2},{4,5},{5,4},{6,7},{7,6},{8,9},{9,8},{10,11... | collective-permute-start | bytes 393224 | tf_op jit(solution)/shard_map/ppermute | solution.py:27
  29.5 12.0 %collective-permute-start.4 = (bf16[256,256]{1,0:T(8,128)(2,1)S(1)}, bf16[256,256]{1,0:T(8,128)(2,1)S(1)}, u32[]{:S(2)}, u32[]{:S(2)}) collective-permute-start(bf16[256,256]{1,0:T(8,128)(2,1)S(1)} %collective-permute-done.2.refs_2_.refs_5_), channel_id=1, source_target_pairs={{0,2},{1,3},{2,4},{3,5},{4,6},{5,7},{6,8},{7,9},{8,10},{9,11},{10,... | collective-permute-start | bytes 393224 | tf_op jit(solution)/shard_map/ppermute | solution.py:22
  41.6 1.9 %collective-permute-start.6 = (bf16[256,256]{1,0:T(8,128)(2,1)S(1)}, bf16[256,256]{1,0:T(8,128)(2,1)S(1)}, u32[]{:S(2)}, u32[]{:S(2)}) collective-permute-start(bf16[256,256]{1,0:T(8,128)(2,1)S(1)} %collective-permute-done.4.refs_2_.refs_5_), channel_id=1, source_target_pairs={{0,1},{1,0},{2,3},{3,2},{4,5},{5,4},{6,7},{7,6},{8,9},{9,8},{10,11... | collective-permute-start | bytes 393224 | tf_op jit(solution)/shard_map/ppermute | solution.py:27
  41.6 12.0 %collective-permute-start.7 = (bf16[256,256]{1,0:T(8,128)(2,1)S(1)}, bf16[256,256]{1,0:T(8,128)(2,1)S(1)}, u32[]{:S(2)}, u32[]{:S(2)}) collective-permute-start(bf16[256,256]{1,0:T(8,128)(2,1)S(1)} %collective-permute-done.4.refs_2_.refs_5_), channel_id=1, source_target_pairs={{0,2},{1,3},{2,4},{3,5},{4,6},{5,7},{6,8},{7,9},{8,10},{9,11},{10,... | collective-permute-start | bytes 393224 | tf_op jit(solution)/shard_map/ppermute | solution.py:22
  53.6 1.3 %collective-permute-start.8 = (bf16[256,256]{1,0:T(8,128)(2,1)S(1)}, bf16[256,256]{1,0:T(8,128)(2,1)S(1)}, u32[]{:S(2)}, u32[]{:S(2)}) collective-permute-start(bf16[256,256]{1,0:T(8,128)(2,1)S(1)} %collective-permute-done.7.refs_5_), channel_id=1, source_target_pairs={{0,1},{1,0},{2,3},{3,2},{4,5},{5,4},{6,7},{7,6},{8,9},{9,8},{10,11... | collective-permute-start | bytes 393224 | tf_op jit(solution)/shard_map/ppermute | solution.py:27
  56.8 1.3 %collective-permute-start.9 = (bf16[256,256]{1,0:T(8,128)(2,1)S(1)}, bf16[256,256]{1,0:T(8,128)(2,1)S(1)}, u32[]{:S(2)}, u32[]{:S(2)}) collective-permute-start(bf16[256,256]{1,0:T(8,128)(2,1)S(1)} %get-tuple-element.108), channel_id=1, source_target_pairs={{0,1},{1,0},{2,3},{3,2},{4,5},{5,4},{6,7},{7,6},{8,9},{9,8},{10,11... | collective-permute-start | bytes 393224 | tf_op jit(solution)/shard_map/ppermute | solution.py:27
  57.0 5.1 %collective-permute-start.10 = (bf16[256,256]{1,0:T(8,128)(2,1)S(1)}, bf16[256,256]{1,0:T(8,128)(2,1)S(1)}, u32[]{:S(2)}, u32[]{:S(2)}) collective-permute-start(bf16[256,256]{1,0:T(8,128)(2,1)S(1)} %get-tuple-element.112), channel_id=1, source_target_pairs={{0,1},{1,0},{2,3},{3,2},{4,5},{5,4},{6,7},{7,6},{8,9},{9,8},{10,11... | collective-permute-start | bytes 393224 | tf_op jit(solution)/shard_map/ppermute | solution.py:27
  58.2 7.4 %collective-permute-start.11 = (bf16[256,256]{1,0:T(8,128)(2,1)S(1)}, bf16[256,256]{1,0:T(8,128)(2,1)S(1)}, u32[]{:S(2)}, u32[]{:S(2)}) collective-permute-start(bf16[256,256]{1,0:T(8,128)(2,1)S(1)} %add_convert_fusion.4), channel_id=1, source_target_pairs={{2,0},{3,1},{4,2},{5,3},{6,4},{7,5},{8,6},{9,7},{10,8},{11,9},{12,... | collective-permute-start | bytes 393224 | tf_op jit(solution)/shard_map/ppermute | solution.py:22
  61.7 12.7 %collective-permute-start.12 = (bf16[256,256]{1,0:T(8,128)(2,1)S(1)}, bf16[256,256]{1,0:T(8,128)(2,1)S(1)}, u32[]{:S(2)}, u32[]{:S(2)}) collective-permute-start(bf16[256,256]{1,0:T(8,128)(2,1)S(1)} %get-tuple-element.116), channel_id=1, source_target_pairs={{0,1},{1,0},{2,3},{3,2},{4,5},{5,4},{6,7},{7,6},{8,9},{9,8},{10,11... | collective-permute-start | bytes 393224 | tf_op jit(solution)/shard_map/ppermute | solution.py:27
  65.7 9.0 %collective-permute-start.13 = (bf16[256,256]{1,0:T(8,128)(2,1)S(1)}, bf16[256,256]{1,0:T(8,128)(2,1)S(1)}, u32[]{:S(2)}, u32[]{:S(2)}) collective-permute-start(bf16[256,256]{1,0:T(8,128)(2,1)S(1)} %add_convert_fusion.3), channel_id=1, source_target_pairs={{2,0},{3,1},{4,2},{5,3},{6,4},{7,5},{8,6},{9,7},{10,8},{11,9},{12,... | collective-permute-start | bytes 393224 | tf_op jit(solution)/shard_map/ppermute | solution.py:22
  73.7 11.3 %collective-permute-start.14 = (bf16[256,256]{1,0:T(8,128)(2,1)S(1)}, bf16[256,256]{1,0:T(8,128)(2,1)S(1)}, u32[]{:S(2)}, u32[]{:S(2)}) collective-permute-start(bf16[256,256]{1,0:T(8,128)(2,1)S(1)} %get-tuple-element.120), channel_id=1, source_target_pairs={{0,1},{1,0},{2,3},{3,2},{4,5},{5,4},{6,7},{7,6},{8,9},{9,8},{10,11... | collective-permute-start | bytes 393224 | tf_op jit(solution)/shard_map/ppermute | solution.py:27
  74.7 11.1 %collective-permute-start.15 = (bf16[256,256]{1,0:T(8,128)(2,1)S(1)}, bf16[256,256]{1,0:T(8,128)(2,1)S(1)}, u32[]{:S(2)}, u32[]{:S(2)}) collective-permute-start(bf16[256,256]{1,0:T(8,128)(2,1)S(1)} %add_convert_fusion.2), channel_id=1, source_target_pairs={{2,0},{3,1},{4,2},{5,3},{6,4},{7,5},{8,6},{9,7},{10,8},{11,9},{12,... | collective-permute-start | bytes 393224 | tf_op jit(solution)/shard_map/ppermute | solution.py:22
  84.8 12.4 %collective-permute-start.16 = (bf16[256,256]{1,0:T(8,128)(2,1)S(1)}, bf16[256,256]{1,0:T(8,128)(2,1)S(1)}, u32[]{:S(2)}, u32[]{:S(2)}) collective-permute-start(bf16[256,256]{1,0:T(8,128)(2,1)S(1)} %get-tuple-element.125), channel_id=1, source_target_pairs={{0,1},{1,0},{2,3},{3,2},{4,5},{5,4},{6,7},{7,6},{8,9},{9,8},{10,11... | collective-permute-start | bytes 393224 | tf_op jit(solution)/shard_map/ppermute | solution.py:27
  85.9 11.4 %collective-permute-start.17 = (bf16[256,256]{1,0:T(8,128)(2,1)S(1)}, bf16[256,256]{1,0:T(8,128)(2,1)S(1)}, u32[]{:S(2)}, u32[]{:S(2)}) collective-permute-start(bf16[256,256]{1,0:T(8,128)(2,1)S(1)} %add_convert_fusion.1), channel_id=1, source_target_pairs={{2,0},{3,1},{4,2},{5,3},{6,4},{7,5},{8,6},{9,7},{10,8},{11,9},{12,... | collective-permute-start | bytes 393224 | tf_op jit(solution)/shard_map/ppermute | solution.py:22

commit v5 on v4

--- a/solution.py
+++ b/solution.py
@@ -9,7 +9,6 @@
 from jax.sharding import PartitionSpec as P
 
 AXES = ("node", "wide")
-REACH = 4
 MASKED = -1e30
 VMEM_LIMIT = 16 * 1024 * 1024
 QUICK = pl.CostEstimate(flops=1, bytes_accessed=1, transcendentals=0)
@@ -281,26 +280,36 @@
     state = {"meta": meta, ("kv", 0, 0): own}
     state.update(zip(("qs", "gs", "gt"), stack(queries, out_grad, dim)))
 
-    block = own
-    for chip in range(REACH):
-        coming = shifted(block, 2)
+    back2 = shifted(own, 4)
+    back1 = shifted(own, 2)
+    back2 = after(back2, state["qs"])
+    back4 = shifted(back2, 4)
+    back3 = shifted(back2, 2)
+    state["kv", 0, 0], state["kv", 0, 1] = own, swapped(own)
+    state["kv", 1, 0] = back1
+    state["kv", 2, 0], state["kv", 2, 1] = back2, swapped(back2)
+    stage(state, fwd=pairs(0, 2) + [(1, 0)])
+    state["kv", 1, 1] = swapped(after(back1, state["l"]))
+    for chip, block in ((3, back3), (4, back4)):
+        block = after(block, state["l"])
         state["kv", chip, 0], state["kv", chip, 1] = block, swapped(block)
-        stage(state, fwd=pairs(chip))
-        block = after(coming, state["l"])
-    state["kv", REACH, 0], state["kv", REACH, 1] = block, swapped(block)
-    stage(state, fwd=pairs(REACH), bwd=[(REACH, 0), (REACH, 1), (REACH - 1, 1)], final=True)
-
-    passed = None
-    for chip in range(REACH, -1, -1):
-        total = state["part", chip, 0] + swapped(state["part", chip, 1]).astype(f32)
-        if passed is not None:
-            total = total + passed.astype(f32)
-        if chip:
-            total = total.astype(bf16)
-            passed = shifted(total, -2)
-            state["dq"] = after(state["dq"], total)
-            todo = [(chip - 1, 0)] + [(chip - 2, 1)] * (chip > 1)
-            stage(state, bwd=todo, last=chip == 1)
+    stage(state, fwd=[(1, 1)] + pairs(3, 4), bwd=pairs(3, 4), final=True)
+
+    def summed(chip, *others):
+        other = swapped(after(state["part", chip, 1], *others))
+        return state["part", chip, 0] + other.astype(f32)
+
+    t4, t3 = summed(4).astype(bf16), summed(3).astype(bf16)
+    r4, r3 = shifted(t4, -4), shifted(t3, -2)
+    state["dq"] = after(state["dq"], t3, t4)
+    stage(state, bwd=pairs(1, 2) + [(0, 1)])
+    t2 = (summed(2, r3, r4) + r4.astype(f32) + r3.astype(f32)).astype(bf16)
+    t1 = summed(1, r3, r4).astype(bf16)
+    r2, r1 = shifted(t2, -4), shifted(t1, -2)
+    other = swapped(after(state["part", 0, 1], r3, r4))
+    state["dq"] = after(state["dq"], t1, t2)
+    stage(state, bwd=[(0, 0)], last=True)
+    total = state["part", 0, 0] + other.astype(f32) + r1.astype(f32) + r2.astype(f32)
     return (state["out"], state["grad_q"], total[:, :dim].astype(bf16), total[:, dim:].astype(bf16))
 
 

time: 98.7 us -> 84.2 us (0.85)
  the two profiles are of different devices: /device:TPU:24 before, /device:TPU:16 now
where the time goes in v5:
time: 84.2 us; the launch traced here: 85.1 us
  starting transfers between devices  43.4 us (52%)
  waiting for transfers between devices  19.4 us (23%)
  Pallas kernels  16.2 us (19%)
  local copies, waits for them, and re-layouts  5.07 us (6%)
    ppermute x8, starting transfers between devices, shifted(): return lax.ppermute(shard, AXES, pairs)  41.7 us
    ppermute x8, waiting for transfers between devices, shifted(): return lax.ppermute(shard, AXES, pairs)  16.4 us
    pallas_call x4, Pallas kernels, stage(): pl.pallas_call(functools.partial(stage_body, plan), in_specs=[HERE] * (le...  15.7 us
    unnamed x10, local copies, waits for them, and re-layouts  4.4 us
    ppermute x10, waiting for transfers between devices, swapped(): return lax.ppermute(shard, AXES, [(i, i ^ 1) for i in range(peers)])  2.96 us
    ppermute x10, starting transfers between devices, swapped(): return lax.ppermute(shard, AXES, [(i, i ^ 1) for i in range(peers)])  1.7 us
  transfers between devices with their start and end apart: 18, of which 10 were waited for; matrix products, arithmetic and copies ran while one was open for 0% of the time, Pallas kernels for 14%

profile of v5, /device:TPU:16, one launch (start us, length us, event | category | flops | bytes accessed | tf_op | source)
XLA Modules:
  0.0 85.1 jit_solution(14308562746366725620)
XLA Ops:
  0.6 0.6 copy-done.4
  1.3 0.8 copy-done.2
  2.1 0.8 copy-done.3
  3.0 0.2 shard_map.84
  3.1 5.2 %collective-permute-start.2 = (bf16[256,256]{1,0:T(8,128)(2,1)S(1)}, bf16[256,256]{1,0:T(8,128)(2,1)S(1)}, u32[]{:S(2)}, u32[]{:S(2)}) collective-permute-start(bf16[256,256]{1,0:T(8,128)(2,1)S(1)} %get-tuple-element.55.refs_2_.refs_4_), channel_id=1, source_target_pairs={{0,4},{1,5},{2,6},{3,7},{4,8},{5,9},{6,10},{7,11},{8,12},{9,13},{1... | collective-permute-start | bytes 393224 | tf_op jit(solution)/shard_map/ppermute | solution.py:21
  8.3 3.8 %collective-permute-start.1 = (bf16[256,256]{1,0:T(8,128)(2,1)S(1)}, bf16[256,256]{1,0:T(8,128)(2,1)S(1)}, u32[]{:S(2)}, u32[]{:S(2)}) collective-permute-start(bf16[256,256]{1,0:T(8,128)(2,1)S(1)} %get-tuple-element.55.refs_2_.refs_4_), channel_id=1, source_target_pairs={{0,2},{1,3},{2,4},{3,5},{4,6},{5,7},{6,8},{7,9},{8,10},{9,11},{10,... | collective-permute-start | bytes 393224 | tf_op jit(solution)/shard_map/ppermute | solution.py:21
  12.2 0.1 collective-permute-start
  12.3 0.0 copy-start
  12.3 1.0 %copy-done = bf16[256,1024]{1,0:T(8,128)(2,1)S(1)} copy-done((bf16[256,1024]{1,0:T(8,128)(2,1)S(1)}, bf16[256,1024]{1,0:T(8,128)(2,1)}, u32[]{:S(2)}) %copy-start) | copy-done | bytes 524312
  13.3 1.0 %copy-done.1 = bf16[256,1024]{1,0:T(8,128)(2,1)S(1)} copy-done((bf16[256,1024]{1,0:T(8,128)(2,1)S(1)}, bf16[256,1024]{1,0:T(8,128)(2,1)}, u32[]{:S(2)}) %copy-start.1) | copy-done | bytes 524312
  14.4 0.3 shard_map.85
  14.7 4.1 %collective-permute-done.2.refs_5_.refs_7_ = bf16[256,256]{1,0:T(8,128)(2,1)S(1)} collective-permute-done((bf16[256,256]{1,0:T(8,128)(2,1)S(1)}, bf16[256,256]{1,0:T(8,128)(2,1)S(1)}, u32[]{:S(2)}, u32[]{:S(2)}) %collective-permute-start.2) | collective-permute-done | bytes 131104 | tf_op jit(solution)/shard_map/ppermute | solution.py:21
  18.8 0.0 collective-permute-start.3
  18.8 2.0 %collective-permute-start.7 = (bf16[256,256]{1,0:T(8,128)(2,1)S(1)}, bf16[256,256]{1,0:T(8,128)(2,1)S(1)}, u32[]{:S(2)}, u32[]{:S(2)}) collective-permute-start(bf16[256,256]{1,0:T(8,128)(2,1)S(1)} %collective-permute-done.2.refs_5_.refs_7_), channel_id=1, source_target_pairs={{0,4},{1,5},{2,6},{3,7},{4,8},{5,9},{6,10},{7,11},{8,12},{9,13},{1... | collective-permute-start | bytes 393224 | tf_op jit(solution)/shard_map/ppermute | solution.py:21
  20.8 4.3 %collective-permute-start.5 = (bf16[256,256]{1,0:T(8,128)(2,1)S(1)}, bf16[256,256]{1,0:T(8,128)(2,1)S(1)}, u32[]{:S(2)}, u32[]{:S(2)}) collective-permute-start(bf16[256,256]{1,0:T(8,128)(2,1)S(1)} %collective-permute-done.2.refs_5_.refs_7_), channel_id=1, source_target_pairs={{0,2},{1,3},{2,4},{3,5},{4,6},{5,7},{6,8},{7,9},{8,10},{9,11},{10,... | collective-permute-start | bytes 393224 | tf_op jit(solution)/shard_map/ppermute | solution.py:21
  25.1 0.0 collective-permute-done.1.refs_4_.refs_5_
  25.1 0.0 collective-permute-done.refs_3_.refs_4_
  25.1 4.3 %shard_map.86 = (bf16[256,2048]{1,0:T(8,128)(2,1)S(1)}, f32[1,2048]{1,0:T(1,128)S(1)}, bf16[256,2048]{1,0:T(8,128)(2,1)S(1)}, f32[1,2048]{1,0:T(1,128)S(1)}, bf1...) custom-call(s32[2,256]{1,0:T(2,128)S(1)} %get-tuple-element.51.refs_, ...), custom_call_target="tpu_custom_call" | custom-call | flops 1 | bytes 1 | tf_op jit(solution)/shard_map/pallas_call | solution.py:255
  29.4 4.8 %collective-permute-done.7.refs_7_ = bf16[256,256]{1,0:T(8,128)(2,1)S(1)} collective-permute-done((bf16[256,256]{1,0:T(8,128)(2,1)S(1)}, bf16[256,256]{1,0:T(8,128)(2,1)S(1)}, u32[]{:S(2)}, u32[]{:S(2)}) %collective-permute-start.7) | collective-permute-done | bytes 131104 | tf_op jit(solution)/shard_map/ppermute | solution.py:21
  34.2 3.1 %collective-permute-done.5.refs_5_ = bf16[256,256]{1,0:T(8,128)(2,1)S(1)} collective-permute-done((bf16[256,256]{1,0:T(8,128)(2,1)S(1)}, bf16[256,256]{1,0:T(8,128)(2,1)S(1)}, u32[]{:S(2)}, u32[]{:S(2)}) %collective-permute-start.5) | collective-permute-done | bytes 131104 | tf_op jit(solution)/shard_map/ppermute | solution.py:21
  37.3 0.1 collective-permute-start.4
  37.4 0.4 collective-permute-start.6
  37.8 0.1 collective-permute-start.8
  37.9 0.8 collective-permute-done.4.refs_4_.refs_6_
  38.6 0.2 collective-permute-done.6.refs_6_
  38.8 0.3 collective-permute-done.8.refs_8_
  39.2 4.1 %shard_map.87 = (bf16[256,2048]{1,0:T(8,128)(2,1)S(1)}, f32[1,2048]{1,0:T(1,128)S(1)}, bf16[256,2048]{1,0:T(8,128)(2,1)}, f32[1,2048]{1,0:T(1,128)}, bf16[256,20...) custom-call(s32[2,256]{1,0:T(2,128)S(1)} %get-tuple-element.51.refs_, ...), custom_call_target="tpu_custom_call", output_to_operand_aliasing={{10}: (9, {}), {11}: (10, {}), {12}: (11, {})} | custom-call | flops 1 | bytes 1 | tf_op jit(solution)/shard_map/pallas_call | solution.py:255
  43.3 0.5 collective-permute-start.10
  43.8 0.8 collective-permute-done.9
  44.7 1.9 %collective-permute-start.11 = (bf16[256,256]{1,0:T(8,128)(2,1)S(1)}, bf16[256,256]{1,0:T(8,128)(2,1)S(1)}, u32[]{:S(2)}, u32[]{:S(2)}) collective-permute-start(bf16[256,256]{1,0:T(8,128)(2,1)S(1)} %add_convert_fusion.4), channel_id=1, source_target_pairs={{2,0},{3,1},{4,2},{5,3},{6,4},{7,5},{8,6},{9,7},{10,8},{11,9},{12,... | collective-permute-start | bytes 393224 | tf_op jit(solution)/shard_map/ppermute | solution.py:21
  46.6 0.0 collective-permute-done.10
  46.6 13.0 %collective-permute-start.12 = (bf16[256,256]{1,0:T(8,128)(2,1)S(1)}, bf16[256,256]{1,0:T(8,128)(2,1)S(1)}, u32[]{:S(2)}, u32[]{:S(2)}) collective-permute-start(bf16[256,256]{1,0:T(8,128)(2,1)S(1)} %add_convert_fusion.3), channel_id=1, source_target_pairs={{4,0},{5,1},{6,2},{7,3},{8,4},{9,5},{10,6},{11,7},{12,8},{13,9},{1... | collective-permute-start | bytes 393224 | tf_op jit(solution)/shard_map/ppermute | solution.py:21
  59.7 4.5 %shard_map.88 = (f32[256,256]{1,0:T(8,128)S(1)}, bf16[256,256]{1,0:T(8,128)(2,1)S(1)}, f32[256,256]{1,0:T(8,128)S(1)}, bf16[256,256]{1,0:T(8,128)(2,1)S(1)}, bf1...) custom-call(s32[2,256]{1,0:T(2,128)S(1)} %get-tuple-element.51.refs_0_, ...), custom_call_target="tpu_custom_call", output_to_operand_aliasing={{5}: (22, {})} | custom-call | flops 1 | bytes 1 | tf_op jit(solution)/shard_map/pallas_call | solution.py:255
  64.2 0.0 collective-permute-done.11
  64.2 1.3 %collective-permute-done.12 = bf16[256,256]{1,0:T(8,128)(2,1)S(1)} collective-permute-done((bf16[256,256]{1,0:T(8,128)(2,1)S(1)}, bf16[256,256]{1,0:T(8,128)(2,1)S(1)}, u32[]{:S(2)}, u32[]{:S(2)}) %collective-permute-start.12) | collective-permute-done | bytes 131104 | tf_op jit(solution)/shard_map/ppermute | solution.py:21
  65.5 0.0 collective-permute-start.13
  65.5 0.5 collective-permute-start.14
  66.0 0.0 collective-permute-start.15
  66.0 0.8 collective-permute-done.13
  66.9 7.1 %collective-permute-start.16 = (bf16[256,256]{1,0:T(8,128)(2,1)S(1)}, bf16[256,256]{1,0:T(8,128)(2,1)S(1)}, u32[]{:S(2)}, u32[]{:S(2)}) collective-permute-start(bf16[256,256]{1,0:T(8,128)(2,1)S(1)} %add_convert_fusion.2), channel_id=1, source_target_pairs={{2,0},{3,1},{4,2},{5,3},{6,4},{7,5},{8,6},{9,7},{10,8},{11,9},{12,... | collective-permute-start | bytes 393224 | tf_op jit(solution)/shard_map/ppermute | solution.py:21
  74.0 0.0 collective-permute-done.14
  74.0 0.1 add_convert_fusion.1
  74.1 4.4 %collective-permute-start.17 = (bf16[256,256]{1,0:T(8,128)(2,1)S(1)}, bf16[256,256]{1,0:T(8,128)(2,1)S(1)}, u32[]{:S(2)}, u32[]{:S(2)}) collective-permute-start(bf16[256,256]{1,0:T(8,128)(2,1)S(1)} %add_convert_fusion.1), channel_id=1, source_target_pairs={{4,0},{5,1},{6,2},{7,3},{8,4},{9,5},{10,6},{11,7},{12,8},{13,9},{1... | collective-permute-start | bytes 393224 | tf_op jit(solution)/shard_map/ppermute | solution.py:21
  78.5 2.8 %shard_map.89 = (f32[256,256]{1,0:T(8,128)S(1)}, f32[128,2048]{1,0:T(8,128)S(1)}, bf16[256,1024]{1,0:T(8,128)(2,1)}, bf16[256,1024]{1,0:T(8,128)(2,1)}) custom-call(s32[2,256]{1,0:T(2,128)S(1)} %get-tuple-element.51.refs_0_, bf16[2048,128]{1,0:T(8,128)(2,1)S(1)} %get-tuple-element.52.refs_1_, ...), custom_call_target="tpu_custom_call", output_to_operand_aliasing={{1}: (11, {})} | custom-call | flops 1 | bytes 1 | tf_op jit(solution)/shard_map/pallas_call | solution.py:255
  81.3 0.0 collective-permute-done.15
  81.3 3.1 %collective-permute-done.17 = bf16[256,256]{1,0:T(8,128)(2,1)S(1)} collective-permute-done((bf16[256,256]{1,0:T(8,128)(2,1)S(1)}, bf16[256,256]{1,0:T(8,128)(2,1)S(1)}, u32[]{:S(2)}, u32[]{:S(2)}) %collective-permute-start.17) | collective-permute-done | bytes 131104 | tf_op jit(solution)/shard_map/ppermute | solution.py:21
  84.4 0.1 add_convert_fusion
  84.5 0.7 fusion
  (10 shorter events, 0.1 us)
Async XLA Ops:
  0.6 0.7 copy-start.4
  1.3 0.8 copy-start.2
  2.1 0.8 copy-start.3
  3.1 15.6 %collective-permute-start.2 = (bf16[256,256]{1,0:T(8,128)(2,1)S(1)}, bf16[256,256]{1,0:T(8,128)(2,1)S(1)}, u32[]{:S(2)}, u32[]{:S(2)}) collective-permute-start(bf16[256,256]{1,0:T(8,128)(2,1)S(1)} %get-tuple-element.55.refs_2_.refs_4_), channel_id=1, source_target_pairs={{0,4},{1,5},{2,6},{3,7},{4,8},{5,9},{6,10},{7,11},{8,12},{9,13},{1... | collective-permute-start | bytes 393224 | tf_op jit(solution)/shard_map/ppermute | solution.py:21
  8.3 16.8 %collective-permute-start.1 = (bf16[256,256]{1,0:T(8,128)(2,1)S(1)}, bf16[256,256]{1,0:T(8,128)(2,1)S(1)}, u32[]{:S(2)}, u32[]{:S(2)}) collective-permute-start(bf16[256,256]{1,0:T(8,128)(2,1)S(1)} %get-tuple-element.55.refs_2_.refs_4_), channel_id=1, source_target_pairs={{0,2},{1,3},{2,4},{3,5},{4,6},{5,7},{6,8},{7,9},{8,10},{9,11},{10,... | collective-permute-start | bytes 393224 | tf_op jit(solution)/shard_map/ppermute | solution.py:21
  12.2 13.0 %collective-permute-start = (bf16[256,256]{1,0:T(8,128)(2,1)S(1)}, bf16[256,256]{1,0:T(8,128)(2,1)S(1)}, u32[]{:S(2)}, u32[]{:S(2)}) collective-permute-start(bf16[256,256]{1,0:T(8,128)(2,1)S(1)} %get-tuple-element.55.refs_2_.refs_4_), channel_id=1, source_target_pairs={{0,1},{1,0},{2,3},{3,2},{4,5},{5,4},{6,7},{7,6},{8,9},{9,8},{10,11... | collective-permute-start | bytes 393224 | tf_op jit(solution)/shard_map/ppermute | solution.py:26
  12.3 1.0 %copy-start = (bf16[256,1024]{1,0:T(8,128)(2,1)S(1)}, bf16[256,1024]{1,0:T(8,128)(2,1)}, u32[]{:S(2)}) copy-start(bf16[256,1024]{1,0:T(8,128)(2,1)} %q.1) | copy-start | bytes 1572868
  13.3 1.0 %copy-start.1 = (bf16[256,1024]{1,0:T(8,128)(2,1)S(1)}, bf16[256,1024]{1,0:T(8,128)(2,1)}, u32[]{:S(2)}) copy-start(bf16[256,1024]{1,0:T(8,128)(2,1)} %g.1) | copy-start | bytes 1572868
  18.8 6.4 %collective-permute-start.3 = (bf16[256,256]{1,0:T(8,128)(2,1)S(1)}, bf16[256,256]{1,0:T(8,128)(2,1)S(1)}, u32[]{:S(2)}, u32[]{:S(2)}) collective-permute-start(bf16[256,256]{1,0:T(8,128)(2,1)S(1)} %collective-permute-done.2.refs_5_.refs_7_), channel_id=1, source_target_pairs={{0,1},{1,0},{2,3},{3,2},{4,5},{5,4},{6,7},{7,6},{8,9},{9,8},{10,11... | collective-permute-start | bytes 393224 | tf_op jit(solution)/shard_map/ppermute | solution.py:26
  18.8 15.4 %collective-permute-start.7 = (bf16[256,256]{1,0:T(8,128)(2,1)S(1)}, bf16[256,256]{1,0:T(8,128)(2,1)S(1)}, u32[]{:S(2)}, u32[]{:S(2)}) collective-permute-start(bf16[256,256]{1,0:T(8,128)(2,1)S(1)} %collective-permute-done.2.refs_5_.refs_7_), channel_id=1, source_target_pairs={{0,4},{1,5},{2,6},{3,7},{4,8},{5,9},{6,10},{7,11},{8,12},{9,13},{1... | collective-permute-start | bytes 393224 | tf_op jit(solution)/shard_map/ppermute | solution.py:21
  20.8 16.5 %collective-permute-start.5 = (bf16[256,256]{1,0:T(8,128)(2,1)S(1)}, bf16[256,256]{1,0:T(8,128)(2,1)S(1)}, u32[]{:S(2)}, u32[]{:S(2)}) collective-permute-start(bf16[256,256]{1,0:T(8,128)(2,1)S(1)} %collective-permute-done.2.refs_5_.refs_7_), channel_id=1, source_target_pairs={{0,2},{1,3},{2,4},{3,5},{4,6},{5,7},{6,8},{7,9},{8,10},{9,11},{10,... | collective-permute-start | bytes 393224 | tf_op jit(solution)/shard_map/ppermute | solution.py:21
  37.3 1.3 %collective-permute-start.4 = (bf16[256,256]{1,0:T(8,128)(2,1)S(1)}, bf16[256,256]{1,0:T(8,128)(2,1)S(1)}, u32[]{:S(2)}, u32[]{:S(2)}) collective-permute-start(bf16[256,256]{1,0:T(8,128)(2,1)S(1)} %collective-permute-done.1.refs_4_.refs_5_), channel_id=1, source_target_pairs={{0,1},{1,0},{2,3},{3,2},{4,5},{5,4},{6,7},{7,6},{8,9},{9,8},{10,11... | collective-permute-start | bytes 393224 | tf_op jit(solution)/shard_map/ppermute | solution.py:26
  37.4 1.5 %collective-permute-start.6 = (bf16[256,256]{1,0:T(8,128)(2,1)S(1)}, bf16[256,256]{1,0:T(8,128)(2,1)S(1)}, u32[]{:S(2)}, u32[]{:S(2)}) collective-permute-start(bf16[256,256]{1,0:T(8,128)(2,1)S(1)} %collective-permute-done.5.refs_5_), channel_id=1, source_target_pairs={{0,1},{1,0},{2,3},{3,2},{4,5},{5,4},{6,7},{7,6},{8,9},{9,8},{10,11... | collective-permute-start | bytes 393224 | tf_op jit(solution)/shard_map/ppermute | solution.py:26
  37.8 1.3 %collective-permute-start.8 = (bf16[256,256]{1,0:T(8,128)(2,1)S(1)}, bf16[256,256]{1,0:T(8,128)(2,1)S(1)}, u32[]{:S(2)}, u32[]{:S(2)}) collective-permute-start(bf16[256,256]{1,0:T(8,128)(2,1)S(1)} %collective-permute-done.7.refs_7_), channel_id=1, source_target_pairs={{0,1},{1,0},{2,3},{3,2},{4,5},{5,4},{6,7},{7,6},{8,9},{9,8},{10,11... | collective-permute-start | bytes 393224 | tf_op jit(solution)/shard_map/ppermute | solution.py:26
  43.3 1.3 %collective-permute-start.9 = (bf16[256,256]{1,0:T(8,128)(2,1)S(1)}, bf16[256,256]{1,0:T(8,128)(2,1)S(1)}, u32[]{:S(2)}, u32[]{:S(2)}) collective-permute-start(bf16[256,256]{1,0:T(8,128)(2,1)S(1)} %get-tuple-element.81), channel_id=1, source_target_pairs={{0,1},{1,0},{2,3},{3,2},{4,5},{5,4},{6,7},{7,6},{8,9},{9,8},{10,11... | collective-permute-start | bytes 393224 | tf_op jit(solution)/shard_map/ppermute | solution.py:26
  43.3 3.3 %collective-permute-start.10 = (bf16[256,256]{1,0:T(8,128)(2,1)S(1)}, bf16[256,256]{1,0:T(8,128)(2,1)S(1)}, u32[]{:S(2)}, u32[]{:S(2)}) collective-permute-start(bf16[256,256]{1,0:T(8,128)(2,1)S(1)} %get-tuple-element.83), channel_id=1, source_target_pairs={{0,1},{1,0},{2,3},{3,2},{4,5},{5,4},{6,7},{7,6},{8,9},{9,8},{10,11... | collective-permute-start | bytes 393224 | tf_op jit(solution)/shard_map/ppermute | solution.py:26
  44.7 19.5 %collective-permute-start.11 = (bf16[256,256]{1,0:T(8,128)(2,1)S(1)}, bf16[256,256]{1,0:T(8,128)(2,1)S(1)}, u32[]{:S(2)}, u32[]{:S(2)}) collective-permute-start(bf16[256,256]{1,0:T(8,128)(2,1)S(1)} %add_convert_fusion.4), channel_id=1, source_target_pairs={{2,0},{3,1},{4,2},{5,3},{6,4},{7,5},{8,6},{9,7},{10,8},{11,9},{12,... | collective-permute-start | bytes 393224 | tf_op jit(solution)/shard_map/ppermute | solution.py:21
  46.6 18.9 %collective-permute-start.12 = (bf16[256,256]{1,0:T(8,128)(2,1)S(1)}, bf16[256,256]{1,0:T(8,128)(2,1)S(1)}, u32[]{:S(2)}, u32[]{:S(2)}) collective-permute-start(bf16[256,256]{1,0:T(8,128)(2,1)S(1)} %add_convert_fusion.3), channel_id=1, source_target_pairs={{4,0},{5,1},{6,2},{7,3},{8,4},{9,5},{10,6},{11,7},{12,8},{13,9},{1... | collective-permute-start | bytes 393224 | tf_op jit(solution)/shard_map/ppermute | solution.py:21
  65.5 1.3 %collective-permute-start.13 = (bf16[256,256]{1,0:T(8,128)(2,1)S(1)}, bf16[256,256]{1,0:T(8,128)(2,1)S(1)}, u32[]{:S(2)}, u32[]{:S(2)}) collective-permute-start(bf16[256,256]{1,0:T(8,128)(2,1)S(1)} %get-tuple-element.88), channel_id=1, source_target_pairs={{0,1},{1,0},{2,3},{3,2},{4,5},{5,4},{6,7},{7,6},{8,9},{9,8},{10,11... | collective-permute-start | bytes 393224 | tf_op jit(solution)/shard_map/ppermute | solution.py:26
  65.5 8.5 %collective-permute-start.14 = (bf16[256,256]{1,0:T(8,128)(2,1)S(1)}, bf16[256,256]{1,0:T(8,128)(2,1)S(1)}, u32[]{:S(2)}, u32[]{:S(2)}) collective-permute-start(bf16[256,256]{1,0:T(8,128)(2,1)S(1)} %get-tuple-element.91), channel_id=1, source_target_pairs={{0,1},{1,0},{2,3},{3,2},{4,5},{5,4},{6,7},{7,6},{8,9},{9,8},{10,11... | collective-permute-start | bytes 393224 | tf_op jit(solution)/shard_map/ppermute | solution.py:26
  66.0 15.3 %collective-permute-start.15 = (bf16[256,256]{1,0:T(8,128)(2,1)S(1)}, bf16[256,256]{1,0:T(8,128)(2,1)S(1)}, u32[]{:S(2)}, u32[]{:S(2)}) collective-permute-start(bf16[256,256]{1,0:T(8,128)(2,1)S(1)} %get-tuple-element.97), channel_id=1, source_target_pairs={{0,1},{1,0},{2,3},{3,2},{4,5},{5,4},{6,7},{7,6},{8,9},{9,8},{10,11... | collective-permute-start | bytes 393224 | tf_op jit(solution)/shard_map/ppermute | solution.py:26
  66.9 14.4 %collective-permute-start.16 = (bf16[256,256]{1,0:T(8,128)(2,1)S(1)}, bf16[256,256]{1,0:T(8,128)(2,1)S(1)}, u32[]{:S(2)}, u32[]{:S(2)}) collective-permute-start(bf16[256,256]{1,0:T(8,128)(2,1)S(1)} %add_convert_fusion.2), channel_id=1, source_target_pairs={{2,0},{3,1},{4,2},{5,3},{6,4},{7,5},{8,6},{9,7},{10,8},{11,9},{12,... | collective-permute-start | bytes 393224 | tf_op jit(solution)/shard_map/ppermute | solution.py:21
  74.1 10.3 %collective-permute-start.17 = (bf16[256,256]{1,0:T(8,128)(2,1)S(1)}, bf16[256,256]{1,0:T(8,128)(2,1)S(1)}, u32[]{:S(2)}, u32[]{:S(2)}) collective-permute-start(bf16[256,256]{1,0:T(8,128)(2,1)S(1)} %add_convert_fusion.1), channel_id=1, source_target_pairs={{4,0},{5,1},{6,2},{7,3},{8,4},{9,5},{10,6},{11,7},{12,8},{13,9},{1... | collective-permute-start | bytes 393224 | tf_op jit(solution)/shard_map/ppermute | solution.py:21
